TPU v7x, 32 devices: a whole 2x2x4 slice. The times are simulated.
32 devices in a mesh: dp: 8 (over z, y), tensor: 4 (over x, core).
Axes of the slice: x: 2, y: 2, z: 4, core: 2. Of those that a mesh axis runs over, the one named last changes fastest.
Arguments:
- gradient: bfloat16 [8, 4608, 1024], P('dp', None, 'tensor'), may hold values from -6 to 6
- error_buffer: float32 [8, 4608, 1024], P('dp', None, 'tensor'), may hold values from -4 to 4
- q_given: float32 [1024, 32], P('tensor'), may hold values from -6 to 6
Outputs:
- new_error: float32 [8, 4608, 1024], P('dp', None, 'tensor')
- p_hat: float32 [4608, 32], replicated
- q_new: float32 [1024, 32], P('tensor')
All inputs are finite; a program needn't handle non-finite values.
Results may differ from a plain program's by a relative error of at most 0.0003.
Values sent between devices are 32-bit elements; how exact they have to be, the bound alone decides.
No kernel may reach another device: no remote copies, remote signals or barrier semaphores. Data moves between devices by JAX's collectives and lax.ppermute only.
A program may use at most 64 MiB of HBM per device.

v0:
```python
import jax
import jax.numpy as jnp
from jax import lax
from jax.sharding import PartitionSpec as P


def shards(gradient, error_buffer, q_given):
    highest = lax.Precision.HIGHEST
    merged = gradient[0].astype(jnp.float32) + error_buffer[0]
    p_block = lax.psum_scatter(
        jnp.dot(merged, q_given, precision=highest, preferred_element_type=jnp.float32),
        "tensor",
        scatter_dimension=0,
        tiled=True,
    )
    p_block = lax.psum(p_block, "dp")
    p_sum = lax.all_gather(p_block, "tensor", axis=0, tiled=True)
    gram = jnp.dot(p_sum.T, p_sum, precision=highest, preferred_element_type=jnp.float32)
    chol = jnp.linalg.cholesky(gram)
    p_hat = lax.linalg.triangular_solve(chol, p_sum, left_side=False, lower=True, transpose_a=True)
    q_local = lax.dot_general(
        merged,
        p_hat,
        (((0,), (0,)), ((), ())),
        precision=highest,
        preferred_element_type=jnp.float32,
    )
    q_new = lax.psum(q_local, "dp") / lax.axis_size("dp")
    approx = jnp.dot(p_hat, q_new.T, precision=highest, preferred_element_type=jnp.float32)
    new_error = (merged - approx)[None]
    return (new_error, p_hat, q_new)


def solution(mesh):
    placed = (P("dp", None, "tensor"), P("dp", None, "tensor"), P("tensor", None))
    return jax.shard_map(
        shards,
        mesh=mesh,
        in_specs=placed,
        out_specs=(P("dp", None, "tensor"), P(), P("tensor", None)),
        check_vma=False,
    )
```

profile of v0, /device:TPU:0, one launch (start us, length us, event | category | flops | bytes accessed | tf_op | source)
XLA Modules:
  0.0 187.3 jit_solution(1784425741552653066)
XLA Ops:
  7.2 0.0 copy-start
  7.2 0.0 copy-start.1
  7.2 0.0 reduce-scatter.2.cloned.1.call-start
  7.2 0.7 copy-done
  7.9 8.4 %fusion.3 = f32[4608,32]{0,1:T(8,128)} fusion(f32[256,32]{0,1:T(8,128)S(1)} %copy-done, f32[1,4608,256]{2,1,0:T(8,128)} %param.4, bf16[1,4608,256]{2,1,0:T(8,128)(2,1)} %param.3), kind=kOutput, calls=%fused_computation.4 | convolution fusion | flops 455344128 | bytes 7700480 | tf_op jit(solution)/shard_map/dot_general | solution.py:11
  16.4 0.0 reduce-scatter.2.cloned.1.call-update
  16.4 0.0 all-reduce.2.cloned.1.call-start
  16.4 24.9 %reduce-scatter.2.cloned.1.call-done = f32[1152,32]{0,1:T(8,128)} async-done(((f32[4608,32]{0,1:T(8,128)}), f32[1152,32]{0,1:T(8,128)}) %reduce-scatter.2.cloned.1.call-update) | async-done | bytes 147472 | tf_op jit(solution)/shard_map/reduce_scatter | solution.py:10
  41.3 0.0 all-reduce.2.cloned.1.call-update
  41.3 73.2 %all-reduce.2.cloned.1.call-done = f32[1152,32]{0,1:T(8,128)} async-done(((f32[1152,32]{0,1:T(8,128)}), f32[1152,32]{0,1:T(8,128)}) %all-reduce.2.cloned.1.call-update) | async-done | bytes 147472 | tf_op jit(solution)/shard_map/psum | solution.py:16
  114.6 7.7 %all_gather.3 = f32[4608,32]{0,1:T(8,128)S(1)} all-gather(f32[1152,32]{0,1:T(8,128)} %all-reduce.2.cloned.1.call-done), channel_id=1, replica_groups=mesh['dp'=8,'tensor'=4] {'tensor'}, dimensions={0}, use_global_device_ids=true | all-gather | bytes 737280 | tf_op jit(solution)/shard_map/all_gather | solution.py:17
  122.3 0.6 fusion.9
  122.9 0.1 copy.6
  123.0 2.9 %cholesky.16 = f32[32,32]{1,0:T(8,128)S(1)} custom-call(f32[32,32]{1,0:T(8,128)S(1)} %fusion.8), custom_call_target="Cholesky" | custom-call | tf_op jit(solution)/shard_map/jit(cholesky)/cholesky | solution.py:19
  125.9 0.6 compare_reduce_fusion
  126.6 0.7 fusion.5
  127.2 2.4 %custom-call.6 = f32[1,32,32]{1,2,0:T(8,128)S(1)} custom-call(f32[1,32,32]{2,1,0:T(8,128)S(1)} %fusion.5), custom_call_target="InvertDiagBlocksLowerTriangular" | custom-call | tf_op jit(solution)/shard_map/triangular_solve | solution.py:20
  129.7 0.7 fusion.6
  130.3 0.0 copy-start.2
  130.4 0.8 copy-done.2
  131.2 0.0 copy-done.1
  131.2 5.2 %fusion.1 = f32[256,32]{0,1:T(8,128)S(1)} fusion(f32[4608,32]{0,1:T(8,128)S(1)} %fusion.6, f32[1,4608,256]{2,1,0:T(8,128)} %param.4, bf16[1,4608,256]{2,1,0:T(8,128)(2,1)S(1)} %copy-done.1), kind=kOutput, calls=%fused_computation.2 | convolution fusion | flops 455344128 | bytes 7700480 | tf_op jit(solution)/shard_map/dot_general | solution.py:21
  136.3 35.3 %psum.15 = f32[256,32]{0,1:T(8,128)S(1)} all-reduce(f32[256,32]{0,1:T(8,128)S(1)} %fusion.1), channel_id=1, replica_groups=mesh['dp'=8,'tensor'=4] {'dp'}, use_global_device_ids=true, to_apply=%region_4.5 | all-reduce | flops 8192 | bytes 65536 | tf_op jit(solution)/shard_map/psum | solution.py:28
  171.6 0.0 copy-start.3
  171.6 8.8 %fusion = f32[1,4608,256]{2,1,0:T(8,128)} fusion(f32[4608,32]{0,1:T(8,128)} %copy-done.2, f32[256,32]{0,1:T(8,128)S(1)} %broadcast_multiply_fusion, f32[1,4608,256]{2,1,0:T(8,128)} %param.4, bf16[1,4608,256]{2,1,0:T(8,128)(2,1)S(1)} %copy-done.1), kind=kOutput, calls=%fused_computation.1 | convolution fusion | flops 456523776 | bytes 12419072 | tf_op jit(solution)/shard_map/dot_general | solution.py:29
  180.4 0.0 copy-done.3
  (3 shorter events, 0.0 us)
Async XLA Ops:
  7.2 0.8 copy-start
  7.2 124.0 %copy-start.1 = (bf16[1,4608,256]{2,1,0:T(8,128)(2,1)S(1)}, bf16[1,4608,256]{2,1,0:T(8,128)(2,1)}, u32[]{:S(2)}) copy-start(bf16[1,4608,256]{2,1,0:T(8,128)(2,1)} %param.3) | copy-start | bytes 7077892
  7.2 34.1 %reduce-scatter.2.cloned.1.call-start = ((), (), s32[]{:S(2)}) async-start(), calls=%async_computation.1 | async-start | bytes 737280 | tf_op jit(solution)/shard_map/reduce_scatter | solution.py:10
  16.4 98.2 %all-reduce.2.cloned.1.call-start = ((), (), s32[]{:S(2)}) async-start(), calls=%async_computation.2 | async-start | bytes 294912 | tf_op jit(solution)/shard_map/psum | solution.py:16
  130.3 0.8 copy-start.2
  171.6 8.8 %copy-start.3 = (f32[256,32]{0,1:T(8,128)}, f32[256,32]{0,1:T(8,128)S(1)}, u32[]{:S(2)}) copy-start(f32[256,32]{0,1:T(8,128)S(1)} %broadcast_multiply_fusion) | copy-start | bytes 98308
Sparse Core Ops, SparseCore 0:
  16.5 24.7 reduce-scatter.1
  44.6 69.8 all-reduce.1
where the time goes:
time: 188 us; the launch traced here: 187 us
  waiting for transfers between devices  98.1 us (52%)
  blocking collectives  43 us (23%)
  matrix products  23.7 us (13%)
  between operations  14.1 us (8%)
  other arithmetic  6.7 us (4%)
    psum x1, waiting for transfers between devices, shards(): p_block = lax.psum(p_block, 'dp')  73.2 us
    psum x1, blocking collectives, shards(): q_new = lax.psum(q_local, 'dp') / lax.axis_size('dp')  35.3 us
    reduce_scatter x1, waiting for transfers between devices, shards(): lax.psum_scatter(jnp.dot(merged, q_given, precision=highest, preferred_el...  24.9 us
    dot_general x1, matrix products, shards(): jnp.dot(p_hat, q_new.T, precision=highest, preferred_element_type=jnp.flo...  8.81 us
    dot_general x1, matrix products, shards(): jnp.dot(merged, q_given, precision=highest, preferred_element_type=jnp.fl...  8.45 us
    all_gather x1, blocking collectives, shards(): p_sum = lax.all_gather(p_block, 'tensor', axis=0, tiled=True)  7.7 us
    dot_general x1, matrix products, shards(): lax.dot_general(merged, p_hat, (((0,), (0,)), ((), ())), precision=highes...  5.17 us
  transfers between devices with their start and end apart: 2, of which 2 were waited for; matrix products, arithmetic and copies ran while one was open for 0% of the time, Pallas kernels for 0%

commit v1 on v0

v1 whole, which is shorter than its diff:
```python
import functools

import jax
import jax.numpy as jnp
from jax import lax
from jax.experimental import pallas as pl
from jax.experimental.pallas import tpu as pltpu
from jax.sharding import PartitionSpec as P

F32, BF16 = jnp.float32, jnp.bfloat16
VMEM = pl.BlockSpec(memory_space=pltpu.VMEM)
ANY = pl.BlockSpec(memory_space=pl.ANY)
AXES = ("dp", "tensor")
LIMIT = 24 * 2**20


def split(x, terms):
    out = []
    for _ in range(terms):
        t = x.astype(BF16)
        out.append(t)
        x = x - t.astype(F32)
    return out


def dot(a, b, contract):
    return lax.dot_general(a, b, ((contract[:1], contract[1:]), ((), ())), preferred_element_type=F32)


def fold(x, rank):
    return functools.reduce(jnp.add, [x[i : i + rank] for i in range(0, x.shape[0], rank)])


def halving_bit(dp, chip, core):
    return chip & 1


def quarters(dp, tensor):
    core, chip = tensor & 1, tensor >> 1
    mine, theirs = halving_bit(dp, chip, core), halving_bit(dp, chip, 1 - core)
    return 2 * core + mine, 2 * core + 1 - mine, 2 * (1 - core) + theirs, 2 * (1 - core) + 1 - theirs


def left_kernel(q_ref, g_hbm, e_hbm, m_ref, mh_ref, ml_ref, send_ref, keep_ref, g_buf, sems, *, chunk):
    own, other, partner_own, partner_other = quarters(lax.axis_index("dp"), lax.axis_index("tensor"))
    rank = q_ref.shape[0]
    quarter = send_ref.shape[2]
    places = ((partner_other, send_ref, 0), (partner_own, send_ref, 1), (other, keep_ref, 0), (own, keep_ref, 1))
    steps = [(pl.multiple_of(index * quarter + at, chunk), out, slot, at) for index, out, slot in places for at in range(0, quarter, chunk)]
    copies = []
    for n, (row, _, _, _) in enumerate(steps):
        rows = pl.ds(row, chunk)
        pair = (
            pltpu.make_async_copy(g_hbm.at[rows], g_buf.at[pl.ds(n * chunk, chunk)], sems.at[n, 0]),
            pltpu.make_async_copy(e_hbm.at[rows], m_ref.at[rows], sems.at[n, 1]),
        )
        for copy in pair:
            copy.start()
        copies.append(pair)
    q = jnp.concatenate(split(q_ref[...], 3), axis=0)
    for n, (row, out, slot, at) in enumerate(steps):
        for copy in copies[n]:
            copy.wait()
        rows = pl.ds(row, chunk)
        m = m_ref[rows] + g_buf[n * chunk : (n + 1) * chunk].astype(F32)
        m_ref[rows] = m
        mh, ml = split(m, 2)
        mh_ref[rows] = mh
        ml_ref[rows] = ml
        out[slot, :, at : at + chunk] = fold(dot(q, mh, (1, 1)) + dot(q, ml, (1, 1)), rank)


def right_kernel(p0, p1, p2, p3, mh_ref, ml_ref, t_ref, gram_ref):
    places = quarters(lax.axis_index("dp"), lax.axis_index("tensor"))
    rank, quarter = p0.shape
    t = gram = None
    for ref, index in zip((p0, p1, p2, p3), places, strict=True):
        rows = pl.ds(pl.multiple_of(index * quarter, quarter), quarter)
        p = jnp.concatenate(split(ref[...], 3), axis=0)
        part = dot(p, mh_ref[rows], (1, 0)) + dot(p, ml_ref[rows], (1, 0))
        square = dot(p, p, (1, 1))
        t = part if t is None else t + part
        gram = square if gram is None else gram + square
    t_ref[...] = fold(t, rank)
    gram = fold(gram, rank)
    gram_ref[...] = gram[:, :rank] + gram[:, rank : 2 * rank] + gram[:, 2 * rank :]


def factor_kernel(gram_ref, inv_ref):
    rank = gram_ref.shape[0]
    row = lax.broadcasted_iota(jnp.int32, (rank, 128), 0)
    lane = lax.broadcasted_iota(jnp.int32, (rank, 128), 1)
    eye = (lane == row + rank).astype(F32)
    a = jnp.concatenate([gram_ref[...], eye[:, rank:]], axis=1)
    pivots = jnp.zeros((rank, 1), F32)
    for k in range(rank):
        line, column = a[k : k + 1, :], a[:, k : k + 1]
        pivot = a[k : k + 1, k : k + 1]
        pivots = jnp.where(row[:, :1] == k, pivot, pivots)
        if k < rank - 1:
            a = a - jnp.where(row[:, :1] > k, column, 0.0) * (line / pivot)
    inv_ref[...] = a[:, rank : 2 * rank] / jnp.sqrt(pivots)


def hat_kernel(inv_ref, p0, p1, p2, p3, hat_ref, rows_ref):
    places = quarters(lax.axis_index("dp"), lax.axis_index("tensor"))
    rank, quarter = p0.shape
    a, b, c = split(inv_ref[...], 3)
    left = jnp.concatenate([a, a, b, a, b, c], axis=1)
    for ref, index in zip((p0, p1, p2, p3), places, strict=True):
        start = pl.multiple_of(index * quarter, quarter)
        u, v, w = split(ref[...], 3)
        hat = dot(left, jnp.concatenate([u, v, u, w, v, u], axis=0), (1, 0))
        hat_ref[:, pl.ds(start, quarter)] = hat
        u, v = split(hat, 2)
        rows_ref[pl.ds(start, quarter), :] = jnp.concatenate([u, v, u, v], axis=0).T


def error_kernel(t0_ref, t1_ref, inv_ref, rows_ref, m_ref, out_ref, q_ref, terms, *, replicas):
    block = out_ref.shape[0]
    step = pl.program_id(0)

    @pl.when(step == 0)
    def _():
        q = jnp.dot(inv_ref[...], t0_ref[...] + t1_ref[...], precision=lax.Precision.HIGHEST, preferred_element_type=F32) / replicas
        q_ref[...] = q
        u, v = split(q, 2)
        terms[...] = jnp.concatenate([u, u, v, v], axis=0)

    rows = pl.ds(pl.multiple_of(step * block, block), block)
    out_ref[...] = m_ref[rows, :] - dot(rows_ref[rows, :], terms[...], (1, 0))


def shards(gradient, error_buffer, q_given):
    replicas, tensors = lax.axis_size("dp"), lax.axis_size("tensor")
    depth, columns = gradient.shape[1:]
    rank = q_given.shape[1]
    quarter = depth // 4
    chunk = next(n for n in (384, 256, 128) if quarter % n == 0)
    steps = depth // chunk
    params = functools.partial(pltpu.CompilerParams, vmem_limit_bytes=LIMIT)

    m, mh, ml, send, keep = pl.pallas_call(
        functools.partial(left_kernel, chunk=chunk),
        out_shape=(
            pltpu.VMEM((depth, columns), F32),
            pltpu.VMEM((depth, columns), BF16),
            pltpu.VMEM((depth, columns), BF16),
            pltpu.VMEM((2, rank, quarter), F32),
            pltpu.VMEM((2, rank, quarter), F32),
        ),
        in_specs=[VMEM, ANY, ANY],
        out_specs=(VMEM,) * 5,
        scratch_shapes=[pltpu.VMEM((depth, columns), BF16), pltpu.SemaphoreType.DMA((steps, 2))],
        compiler_params=params(),
        cost_estimate=pl.CostEstimate(flops=12 * depth * columns * rank, bytes_accessed=6 * depth * columns, transcendentals=0),
        name="left_products",
    )(q_given.T, gradient[0], error_buffer[0])

    def swap(x, bit):
        return lax.ppermute(x, AXES, [(i, i ^ bit) for i in range(replicas * tensors)])

    got = swap(send, 1)
    first = 2
    acc = keep[1] + got[1] + swap(keep[0] + got[0], first)
    bit = 2 * first
    while bit < replicas * tensors:
        acc = acc + swap(acc, bit)
        bit *= 2
    p_own = acc
    p_other = swap(p_own, first)
    p_partner_own = swap(p_own, 1)
    p_partner_other = swap(p_other, 1)
    ps = (p_own, p_other, p_partner_own, p_partner_other)

    t, gram = pl.pallas_call(
        right_kernel,
        out_shape=(pltpu.VMEM((rank, columns), F32), pltpu.VMEM((rank, rank), F32)),
        in_specs=[VMEM] * 6,
        out_specs=(VMEM, VMEM),
        compiler_params=params(),
        cost_estimate=pl.CostEstimate(flops=12 * depth * columns * rank, bytes_accessed=4 * depth * columns, transcendentals=0),
        name="right_products",
    )(*ps, mh, ml)

    inverse = pl.pallas_call(
        factor_kernel,
        out_shape=pltpu.VMEM((rank, rank), F32),
        in_specs=[VMEM],
        out_specs=VMEM,
        compiler_params=params(),
        cost_estimate=pl.CostEstimate(flops=rank**3, bytes_accessed=4 * rank * rank, transcendentals=0),
        name="factor",
    )(gram)

    hat, hat_rows = pl.pallas_call(
        hat_kernel,
        out_shape=(jax.ShapeDtypeStruct((rank, depth), F32), pltpu.VMEM((depth, 4 * rank), BF16)),
        in_specs=[VMEM] * 5,
        out_specs=(VMEM, VMEM),
        compiler_params=params(),
        cost_estimate=pl.CostEstimate(flops=12 * depth * rank * rank, bytes_accessed=8 * depth * rank, transcendentals=0),
        name="left_factor",
    )(inverse, *ps)

    bit = tensors
    while 2 * bit < replicas * tensors:
        t = t + swap(t, bit)
        bit *= 2
    last = swap(t, bit)

    block = next(n for n in (512, 256, 128) if depth % n == 0)
    error, q_new = pl.pallas_call(
        functools.partial(error_kernel, replicas=replicas),
        grid=(depth // block,),
        out_shape=(jax.ShapeDtypeStruct((depth, columns), F32), jax.ShapeDtypeStruct((rank, columns), F32)),
        in_specs=[VMEM] * 5,
        out_specs=(pl.BlockSpec((block, columns), lambda i: (i, 0)), VMEM),
        scratch_shapes=[pltpu.VMEM((4 * rank, columns), BF16)],
        compiler_params=params(),
        cost_estimate=pl.CostEstimate(flops=2 * 4 * depth * rank * columns, bytes_accessed=8 * depth * columns, transcendentals=0),
        name="new_error",
    )(t, last, inverse, hat_rows, m)
    return (error[None], hat.T, q_new.T)


def solution(mesh):
    placed = (P("dp", None, "tensor"), P("dp", None, "tensor"), P("tensor", None))
    return jax.shard_map(
        shards,
        mesh=mesh,
        in_specs=placed,
        out_specs=(P("dp", None, "tensor"), P(), P("tensor", None)),
        check_vma=False,
    )
```

time: 188 us -> 69.2 us (0.37)
  waiting for transfers between devices: 98.1 us -> 27.8 us
  blocking collectives: 43 us -> 0 us
  matrix products: 23.7 us -> 0 us
  Pallas kernels: 0 us -> 19.7 us
  starting transfers between devices: 0.08 us -> 15.9 us
  between operations: 14.1 us -> 0.67 us
  other arithmetic: 6.7 us -> 0.12 us
  local copies, waits for them, and re-layouts: 1.59 us -> 4.75 us
    psum x1 -> x0, waiting for transfers between devices: 73.2 us -> none  [shards(): p_block = lax.psum(p_block, 'dp')]
    psum x1 -> x0, blocking collectives: 35.3 us -> none  [shards(): q_new = lax.psum(q_local, 'dp') / lax.axis_size('dp')]
    ppermute x0 -> x11, waiting for transfers between devices: none -> 27.8 us  [swap(): lax.ppermute(x, AXES, [(i, i ^ bit) for i in range(replicas * tensors)])]
    reduce_scatter x1 -> x0, waiting for transfers between devices: 24.9 us -> none  [shards(): lax.psum_scatter(jnp.dot(merged, q_given, precision=highest, preferred_el...]
    dot_general x4 -> x0, matrix products: 23 us -> none  [the longest x1 8.81 us: shards(): jnp.dot(p_hat, q_new.T, precision=highest, preferred_element_type=jnp.flo...]
    pallas_call x0 -> x5, Pallas kernels: none -> 19.7 us  [the longest x1 9.17 us: shards(): pl.pallas_call(functools.partial(left_kernel, chunk=chunk), out_shape=(pl...]
    ppermute x0 -> x11, starting transfers between devices: none -> 15.9 us  [swap(): lax.ppermute(x, AXES, [(i, i ^ bit) for i in range(replicas * tensors)])]
    all_gather x1 -> x0, blocking collectives: 7.7 us -> none  [shards(): p_sum = lax.all_gather(p_block, 'tensor', axis=0, tiled=True)]
  transfers between devices with their start and end apart: 2 -> 11, of which waited for: 2 -> 9; matrix products, arithmetic and copies ran while one was open for 0% -> 0% of each run, Pallas kernels for 0% -> 6%
where the time goes in v1:
time: 69.2 us; the launch traced here: 69 us
  waiting for transfers between devices  27.8 us (40%)
  Pallas kernels  19.7 us (28%)
  starting transfers between devices  15.9 us (23%)
  local copies, waits for them, and re-layouts  4.75 us (7%)
    ppermute x11, waiting for transfers between devices, swap(): lax.ppermute(x, AXES, [(i, i ^ bit) for i in range(replicas * tensors)])  27.8 us
    ppermute x11, starting transfers between devices, swap(): lax.ppermute(x, AXES, [(i, i ^ bit) for i in range(replicas * tensors)])  15.9 us
    pallas_call x1, Pallas kernels, shards(): pl.pallas_call(functools.partial(left_kernel, chunk=chunk), out_shape=(pl...  9.17 us
    pallas_call x1, Pallas kernels, shards(): pl.pallas_call(functools.partial(error_kernel, replicas=replicas), grid=(...  5.19 us
    unnamed x6, local copies, waits for them, and re-layouts  4.75 us
    pallas_call x1, Pallas kernels, shards(): pl.pallas_call(factor_kernel, out_shape=pltpu.VMEM((rank, rank), F32), in...  2.8 us
  transfers between devices with their start and end apart: 11, of which 9 were waited for; matrix products, arithmetic and copies ran while one was open for 0% of the time, Pallas kernels for 6%

profile of v1, /device:TPU:0, one launch (start us, length us, event | category | flops | bytes accessed | tf_op | source)
XLA Modules:
  0.0 69.0 jit_solution(7132447830962896589)
XLA Ops:
  0.6 0.0 copy-start
  0.6 2.3 %copy-done = f32[1,4608,256]{2,1,0:T(8,128)S(1)} copy-done((f32[1,4608,256]{2,1,0:T(8,128)S(1)}, f32[1,4608,256]{2,1,0:T(8,128)}, u32[]{:S(2)}) %copy-start) | copy-done | bytes 4718616
  3.0 0.0 copy-start.1
  3.0 1.7 %copy-done.1 = bf16[1,4608,256]{2,1,0:T(8,128)(2,1)S(1)} copy-done((bf16[1,4608,256]{2,1,0:T(8,128)(2,1)S(1)}, bf16[1,4608,256]{2,1,0:T(8,128)(2,1)}, u32[]{:S(2)}) %copy-start.1) | copy-done | bytes 2359320
  4.6 0.0 copy-start.2
  4.6 0.8 %copy-done.2 = f32[256,32]{0,1:T(8,128)S(1)} copy-done((f32[256,32]{0,1:T(8,128)S(1)}, f32[256,32]{0,1:T(8,128)}, u32[]{:S(2)}) %copy-start.2) | copy-done | bytes 32792
  5.4 9.2 %left_products.1 = (f32[4608,256]{1,0:T(8,128)S(1)}, bf16[4608,256]{1,0:T(8,128)(2,1)S(1)}, bf16[4608,256]{1,0:T(8,128)(2,1)S(1)}, f32[2,32,1152]{2,1,0:T(8,128)S(1)}, f32[2,32,1152]{2,1,0:T(8,128)S(1)}) custom-call(f32[32,256]{1,0:T(8,128)S(1)} %bitcast.14, bf16[4608,256]{1,0:T(8,128)(2,1)S(1)} %bitcast.13, f32[4608,256]{1,0:T(8,128)S(1)} %bitcast.12), custom_call_target="tpu_custom_call" | custom-call | flops 452984832 | bytes 7077888 | tf_op jit(solution)/shard_map/left_products/pallas_call | solution.py:143
  14.6 0.5 collective-permute-start
  15.1 1.2 %collective-permute-done = f32[2,32,1152]{2,1,0:T(8,128)S(1)} collective-permute-done((f32[2,32,1152]{2,1,0:T(8,128)S(1)}, f32[2,32,1152]{2,1,0:T(8,128)S(1)}, u32[]{:S(2)}, u32[]{:S(2)}) %collective-permute-start) | collective-permute-done | bytes 294944 | tf_op jit(solution)/shard_map/ppermute | solution.py:161
  16.3 2.9 %collective-permute-start.1 = (f32[32,1152]{1,0:T(8,128)S(1)}, f32[32,1152]{1,0:T(8,128)S(1)}, u32[]{:S(2)}, u32[]{:S(2)}) collective-permute-start(f32[32,1152]{1,0:T(8,128)S(1)} %fusion), channel_id=1, source_target_pairs={{0,2},{1,3},{2,0},{3,1},{4,6},{5,7},{6,4},{7,5},{8,10},{9,11},{10,... | collective-permute-start | bytes 442376 | tf_op jit(solution)/shard_map/ppermute | solution.py:161
  19.2 4.1 %collective-permute-done.1 = f32[32,1152]{1,0:T(8,128)S(1)} collective-permute-done((f32[32,1152]{1,0:T(8,128)S(1)}, f32[32,1152]{1,0:T(8,128)S(1)}, u32[]{:S(2)}, u32[]{:S(2)}) %collective-permute-start.1) | collective-permute-done | bytes 147488 | tf_op jit(solution)/shard_map/ppermute | solution.py:161
  23.4 1.8 %collective-permute-start.2 = (f32[32,1152]{1,0:T(8,128)S(1)}, f32[32,1152]{1,0:T(8,128)S(1)}, u32[]{:S(2)}, u32[]{:S(2)}) collective-permute-start(f32[32,1152]{1,0:T(8,128)S(1)} %fusion.2), channel_id=1, source_target_pairs={{0,4},{1,5},{2,6},{3,7},{4,0},{5,1},{6,2},{7,3},{8,12},{9,13},{10,... | collective-permute-start | bytes 442376 | tf_op jit(solution)/shard_map/ppermute | solution.py:161
  25.3 3.6 %collective-permute-done.2 = f32[32,1152]{1,0:T(8,128)S(1)} collective-permute-done((f32[32,1152]{1,0:T(8,128)S(1)}, f32[32,1152]{1,0:T(8,128)S(1)}, u32[]{:S(2)}, u32[]{:S(2)}) %collective-permute-start.2) | collective-permute-done | bytes 147488 | tf_op jit(solution)/shard_map/ppermute | solution.py:161
  28.9 1.7 %collective-permute-start.3 = (f32[32,1152]{1,0:T(8,128)S(1)}, f32[32,1152]{1,0:T(8,128)S(1)}, u32[]{:S(2)}, u32[]{:S(2)}) collective-permute-start(f32[32,1152]{1,0:T(8,128)S(1)} %add.35), channel_id=1, source_target_pairs={{0,8},{1,9},{2,10},{3,11},{4,12},{5,13},{6,14},{7,15},{8,0},{9,1},... | collective-permute-start | bytes 442376 | tf_op jit(solution)/shard_map/ppermute | solution.py:161
  30.6 3.5 %collective-permute-done.3 = f32[32,1152]{1,0:T(8,128)S(1)} collective-permute-done((f32[32,1152]{1,0:T(8,128)S(1)}, f32[32,1152]{1,0:T(8,128)S(1)}, u32[]{:S(2)}, u32[]{:S(2)}) %collective-permute-start.3) | collective-permute-done | bytes 147488 | tf_op jit(solution)/shard_map/ppermute | solution.py:161
  34.1 3.1 %collective-permute-start.4 = (f32[32,1152]{1,0:T(8,128)S(1)}, f32[32,1152]{1,0:T(8,128)S(1)}, u32[]{:S(2)}, u32[]{:S(2)}) collective-permute-start(f32[32,1152]{1,0:T(8,128)S(1)} %add.36), channel_id=1, source_target_pairs={{0,16},{1,17},{2,18},{3,19},{4,20},{5,21},{6,22},{7,23},{8,24},{9,... | collective-permute-start | bytes 442376 | tf_op jit(solution)/shard_map/ppermute | solution.py:161
  37.2 4.7 %collective-permute-done.4 = f32[32,1152]{1,0:T(8,128)S(1)} collective-permute-done((f32[32,1152]{1,0:T(8,128)S(1)}, f32[32,1152]{1,0:T(8,128)S(1)}, u32[]{:S(2)}, u32[]{:S(2)}) %collective-permute-start.4) | collective-permute-done | bytes 147488 | tf_op jit(solution)/shard_map/ppermute | solution.py:161
  41.9 1.6 %collective-permute-start.5 = (f32[32,1152]{1,0:T(8,128)S(1)}, f32[32,1152]{1,0:T(8,128)S(1)}, u32[]{:S(2)}, u32[]{:S(2)}) collective-permute-start(f32[32,1152]{1,0:T(8,128)S(1)} %add.37.p0), channel_id=1, source_target_pairs={{0,2},{1,3},{2,0},{3,1},{4,6},{5,7},{6,4},{7,5},{8,10},{9,11},{10,... | collective-permute-start | bytes 442376 | tf_op jit(solution)/shard_map/ppermute | solution.py:161
  43.5 0.0 collective-permute-start.6
  43.5 3.6 %collective-permute-done.5.p1 = f32[32,1152]{1,0:T(8,128)S(1)} collective-permute-done((f32[32,1152]{1,0:T(8,128)S(1)}, f32[32,1152]{1,0:T(8,128)S(1)}, u32[]{:S(2)}, u32[]{:S(2)}) %collective-permute-start.5) | collective-permute-done | bytes 147488 | tf_op jit(solution)/shard_map/ppermute | solution.py:161
  47.1 0.0 collective-permute-start.7
  47.1 0.0 collective-permute-done.6.p2
  47.1 1.4 %collective-permute-done.7.p3 = f32[32,1152]{1,0:T(8,128)S(1)} collective-permute-done((f32[32,1152]{1,0:T(8,128)S(1)}, f32[32,1152]{1,0:T(8,128)S(1)}, u32[]{:S(2)}, u32[]{:S(2)}) %collective-permute-start.7) | collective-permute-done | bytes 147488 | tf_op jit(solution)/shard_map/ppermute | solution.py:161
  48.5 1.2 %right_products.1 = (f32[32,256]{1,0:T(8,128)S(1)}, f32[32,32]{1,0:T(8,128)S(1)}) custom-call(f32[32,1152]{1,0:T(8,128)S(1)} %add.37.p0, f32[32,1152]{1,0:T(8,128)S(1)} %collective-permute-done.5.p1, f32[32,1152]{1,0:T(8,128)S(1)} %collective-permute-done.6.p2, f32[32,1152]{1,0:T(8,128)S(1)} %collective-permute-done.7.p3, ...), custom_call_target="tpu_custom_call" | custom-call | flops 452984832 | bytes 4718592 | tf_op jit(solution)/shard_map/right_products/pallas_call | solution.py:176
  49.7 1.5 %collective-permute-start.8 = (f32[32,256]{1,0:T(8,128)S(1)}, f32[32,256]{1,0:T(8,128)S(1)}, u32[]{:S(2)}, u32[]{:S(2)}) collective-permute-start(f32[32,256]{1,0:T(8,128)S(1)} %get-tuple-element.18), channel_id=1, source_target_pairs={{0,4},{1,5},{2,6},{3,7},{4,0},{5,1},{6,2},{7,3},{8,12},{9,13},{10,... | collective-permute-start | bytes 98312 | tf_op jit(solution)/shard_map/ppermute | solution.py:161
  51.2 2.4 %collective-permute-done.8 = f32[32,256]{1,0:T(8,128)S(1)} collective-permute-done((f32[32,256]{1,0:T(8,128)S(1)}, f32[32,256]{1,0:T(8,128)S(1)}, u32[]{:S(2)}, u32[]{:S(2)}) %collective-permute-start.8) | collective-permute-done | bytes 32800 | tf_op jit(solution)/shard_map/ppermute | solution.py:161
  53.6 0.7 %collective-permute-start.9 = (f32[32,256]{1,0:T(8,128)S(1)}, f32[32,256]{1,0:T(8,128)S(1)}, u32[]{:S(2)}, u32[]{:S(2)}) collective-permute-start(f32[32,256]{1,0:T(8,128)S(1)} %add.38), channel_id=1, source_target_pairs={{0,8},{1,9},{2,10},{3,11},{4,12},{5,13},{6,14},{7,15},{8,0},{9,1},... | collective-permute-start | bytes 98312 | tf_op jit(solution)/shard_map/ppermute | solution.py:161
  54.3 3.2 %collective-permute-done.9 = f32[32,256]{1,0:T(8,128)S(1)} collective-permute-done((f32[32,256]{1,0:T(8,128)S(1)}, f32[32,256]{1,0:T(8,128)S(1)}, u32[]{:S(2)}, u32[]{:S(2)}) %collective-permute-start.9) | collective-permute-done | bytes 32800 | tf_op jit(solution)/shard_map/ppermute | solution.py:161
  57.5 2.1 %collective-permute-start.10 = (f32[32,256]{1,0:T(8,128)S(1)}, f32[32,256]{1,0:T(8,128)S(1)}, u32[]{:S(2)}, u32[]{:S(2)}) collective-permute-start(f32[32,256]{1,0:T(8,128)S(1)} %add.39.t0_ref), channel_id=1, source_target_pairs={{0,16},{1,17},{2,18},{3,19},{4,20},{5,21},{6,22},{7,23},{8,24},{9,... | collective-permute-start | bytes 98312 | tf_op jit(solution)/shard_map/ppermute | solution.py:161
  59.6 2.8 %factor.1.inv_ref = f32[32,32]{1,0:T(8,128)S(1)} custom-call(f32[32,32]{1,0:T(8,128)S(1)} %get-tuple-element.19.gram_ref), custom_call_target="tpu_custom_call" | custom-call | flops 32768 | bytes 4096 | tf_op jit(solution)/shard_map/factor/pallas_call | solution.py:186
  62.4 1.4 %left_factor.1 = (f32[32,4608]{1,0:T(8,128)}, bf16[4608,128]{1,0:T(8,128)(2,1)S(1)}) custom-call(f32[32,32]{1,0:T(8,128)S(1)} %factor.1.inv_ref, f32[32,1152]{1,0:T(8,128)S(1)} %add.37.p0, f32[32,1152]{1,0:T(8,128)S(1)} %collective-permute-done.5.p1, f32[32,1152]{1,0:T(8,128)S(1)} %collective-permute-done.6.p2, f32[32,1152]{1,0:T(8,128)S(1)} %collective-permute-done.7.p3), custom_call_target="tpu_custom_call" | custom-call | flops 56623104 | bytes 1179648 | tf_op jit(solution)/shard_map/left_factor/pallas_call | solution.py:196
  63.8 0.0 collective-permute-done.10.t1_ref
  63.8 5.2 %new_error.1 = (f32[4608,256]{1,0:T(8,128)}, f32[32,256]{1,0:T(8,128)}) custom-call(f32[32,256]{1,0:T(8,128)S(1)} %add.39.t0_ref, f32[32,256]{1,0:T(8,128)S(1)} %collective-permute-done.10.t1_ref, f32[32,32]{1,0:T(8,128)S(1)} %factor.1.inv_ref, bf16[4608,128]{1,0:T(8,128)(2,1)S(1)} %get-tuple-element.20.rows_ref, f32[4608,256]{1,0:T(8,128)S(1)} %get-tuple-element.21.m_ref), custom_call_target="tpu_custom_call" | custom-call | flops 301989888 | bytes 9437184 | tf_op jit(solution)/shard_map/new_error/pallas_call | solution.py:213
  (7 shorter events, 0.1 us)
Async XLA Ops:
  0.6 2.3 %copy-start = (f32[1,4608,256]{2,1,0:T(8,128)S(1)}, f32[1,4608,256]{2,1,0:T(8,128)}, u32[]{:S(2)}) copy-start(f32[1,4608,256]{2,1,0:T(8,128)} %param.4) | copy-start | bytes 14155780
  3.0 1.7 %copy-start.1 = (bf16[1,4608,256]{2,1,0:T(8,128)(2,1)S(1)}, bf16[1,4608,256]{2,1,0:T(8,128)(2,1)}, u32[]{:S(2)}) copy-start(bf16[1,4608,256]{2,1,0:T(8,128)(2,1)} %param.3) | copy-start | bytes 7077892
  4.6 0.8 %copy-start.2 = (f32[256,32]{0,1:T(8,128)S(1)}, f32[256,32]{0,1:T(8,128)}, u32[]{:S(2)}) copy-start(f32[256,32]{0,1:T(8,128)} %param.5) | copy-start | bytes 98308
  14.6 1.7 %collective-permute-start = (f32[2,32,1152]{2,1,0:T(8,128)S(1)}, f32[2,32,1152]{2,1,0:T(8,128)S(1)}, u32[]{:S(2)}, u32[]{:S(2)}) collective-permute-start(f32[2,32,1152]{2,1,0:T(8,128)S(1)} %get-tuple-element.15), channel_id=1, source_target_pairs={{0,1},{1,0},{2,3},{3,2},{4,5},{5,4},{6,7},{7,6},{8,9},{9,8},{10,11... | collective-permute-start | bytes 884744 | tf_op jit(solution)/shard_map/ppermute | solution.py:161
  16.3 7.1 %collective-permute-start.1 = (f32[32,1152]{1,0:T(8,128)S(1)}, f32[32,1152]{1,0:T(8,128)S(1)}, u32[]{:S(2)}, u32[]{:S(2)}) collective-permute-start(f32[32,1152]{1,0:T(8,128)S(1)} %fusion), channel_id=1, source_target_pairs={{0,2},{1,3},{2,0},{3,1},{4,6},{5,7},{6,4},{7,5},{8,10},{9,11},{10,... | collective-permute-start | bytes 442376 | tf_op jit(solution)/shard_map/ppermute | solution.py:161
  23.4 5.4 %collective-permute-start.2 = (f32[32,1152]{1,0:T(8,128)S(1)}, f32[32,1152]{1,0:T(8,128)S(1)}, u32[]{:S(2)}, u32[]{:S(2)}) collective-permute-start(f32[32,1152]{1,0:T(8,128)S(1)} %fusion.2), channel_id=1, source_target_pairs={{0,4},{1,5},{2,6},{3,7},{4,0},{5,1},{6,2},{7,3},{8,12},{9,13},{10,... | collective-permute-start | bytes 442376 | tf_op jit(solution)/shard_map/ppermute | solution.py:161
  28.9 5.2 %collective-permute-start.3 = (f32[32,1152]{1,0:T(8,128)S(1)}, f32[32,1152]{1,0:T(8,128)S(1)}, u32[]{:S(2)}, u32[]{:S(2)}) collective-permute-start(f32[32,1152]{1,0:T(8,128)S(1)} %add.35), channel_id=1, source_target_pairs={{0,8},{1,9},{2,10},{3,11},{4,12},{5,13},{6,14},{7,15},{8,0},{9,1},... | collective-permute-start | bytes 442376 | tf_op jit(solution)/shard_map/ppermute | solution.py:161
  34.1 7.8 %collective-permute-start.4 = (f32[32,1152]{1,0:T(8,128)S(1)}, f32[32,1152]{1,0:T(8,128)S(1)}, u32[]{:S(2)}, u32[]{:S(2)}) collective-permute-start(f32[32,1152]{1,0:T(8,128)S(1)} %add.36), channel_id=1, source_target_pairs={{0,16},{1,17},{2,18},{3,19},{4,20},{5,21},{6,22},{7,23},{8,24},{9,... | collective-permute-start | bytes 442376 | tf_op jit(solution)/shard_map/ppermute | solution.py:161
  41.9 5.2 %collective-permute-start.5 = (f32[32,1152]{1,0:T(8,128)S(1)}, f32[32,1152]{1,0:T(8,128)S(1)}, u32[]{:S(2)}, u32[]{:S(2)}) collective-permute-start(f32[32,1152]{1,0:T(8,128)S(1)} %add.37.p0), channel_id=1, source_target_pairs={{0,2},{1,3},{2,0},{3,1},{4,6},{5,7},{6,4},{7,5},{8,10},{9,11},{10,... | collective-permute-start | bytes 442376 | tf_op jit(solution)/shard_map/ppermute | solution.py:161
  43.5 3.7 %collective-permute-start.6 = (f32[32,1152]{1,0:T(8,128)S(1)}, f32[32,1152]{1,0:T(8,128)S(1)}, u32[]{:S(2)}, u32[]{:S(2)}) collective-permute-start(f32[32,1152]{1,0:T(8,128)S(1)} %add.37.p0), channel_id=1, source_target_pairs={{0,1},{1,0},{2,3},{3,2},{4,5},{5,4},{6,7},{7,6},{8,9},{9,8},{10,11... | collective-permute-start | bytes 442376 | tf_op jit(solution)/shard_map/ppermute | solution.py:161
  47.1 1.4 %collective-permute-start.7 = (f32[32,1152]{1,0:T(8,128)S(1)}, f32[32,1152]{1,0:T(8,128)S(1)}, u32[]{:S(2)}, u32[]{:S(2)}) collective-permute-start(f32[32,1152]{1,0:T(8,128)S(1)} %collective-permute-done.5.p1), channel_id=1, source_target_pairs={{0,1},{1,0},{2,3},{3,2},{4,5},{5,4},{6,7},{7,6},{8,9},{9,8},{10,11... | collective-permute-start | bytes 442376 | tf_op jit(solution)/shard_map/ppermute | solution.py:161
  49.7 3.9 %collective-permute-start.8 = (f32[32,256]{1,0:T(8,128)S(1)}, f32[32,256]{1,0:T(8,128)S(1)}, u32[]{:S(2)}, u32[]{:S(2)}) collective-permute-start(f32[32,256]{1,0:T(8,128)S(1)} %get-tuple-element.18), channel_id=1, source_target_pairs={{0,4},{1,5},{2,6},{3,7},{4,0},{5,1},{6,2},{7,3},{8,12},{9,13},{10,... | collective-permute-start | bytes 98312 | tf_op jit(solution)/shard_map/ppermute | solution.py:161
  53.6 3.9 %collective-permute-start.9 = (f32[32,256]{1,0:T(8,128)S(1)}, f32[32,256]{1,0:T(8,128)S(1)}, u32[]{:S(2)}, u32[]{:S(2)}) collective-permute-start(f32[32,256]{1,0:T(8,128)S(1)} %add.38), channel_id=1, source_target_pairs={{0,8},{1,9},{2,10},{3,11},{4,12},{5,13},{6,14},{7,15},{8,0},{9,1},... | collective-permute-start | bytes 98312 | tf_op jit(solution)/shard_map/ppermute | solution.py:161
  57.5 6.3 %collective-permute-start.10 = (f32[32,256]{1,0:T(8,128)S(1)}, f32[32,256]{1,0:T(8,128)S(1)}, u32[]{:S(2)}, u32[]{:S(2)}) collective-permute-start(f32[32,256]{1,0:T(8,128)S(1)} %add.39.t0_ref), channel_id=1, source_target_pairs={{0,16},{1,17},{2,18},{3,19},{4,20},{5,21},{6,22},{7,23},{8,24},{9,... | collective-permute-start | bytes 98312 | tf_op jit(solution)/shard_map/ppermute | solution.py:161

commit v2 on v0

v2 whole, which is shorter than its diff:
```python
import functools

import jax
import jax.numpy as jnp
from jax import lax
from jax.experimental import pallas as pl
from jax.experimental.pallas import tpu as pltpu
from jax.sharding import PartitionSpec as P

F32, BF16 = jnp.float32, jnp.bfloat16
VMEM = pl.BlockSpec(memory_space=pltpu.VMEM)
HBM = pl.BlockSpec(memory_space=pltpu.HBM)
AXES = ("dp", "tensor")
LIMIT = 24 * 2**20


def split(x, terms):
    out = []
    for _ in range(terms):
        t = x.astype(BF16)
        out.append(t)
        x = x - t.astype(F32)
    return out


def stack(terms):
    return jnp.concatenate(terms, axis=0)


def dot(a, b, contract):
    return lax.dot_general(a, b, ((contract[:1], contract[1:]), ((), ())), preferred_element_type=F32)


def fold(x, rank):
    return functools.reduce(jnp.add, [x[i : i + rank] for i in range(0, x.shape[0], rank)])


def walks(devices):
    bits = []
    bit = 2
    while bit < devices:
        bits.append(bit)
        bit *= 2
    half = len(bits) // 2
    return bits, bits[half:] + bits[:half][::-1]


def sides(devices):
    place = lax.axis_index("dp") * lax.axis_size("tensor") + lax.axis_index("tensor")
    first, second = (walk[0].bit_length() - 1 for walk in walks(devices))
    core = place & 1
    own = [(place >> first) & 1, (place >> second) & 1]
    mine = jnp.where(core == 0, own[0], own[1])
    theirs = jnp.where(core == 0, own[1], own[0])
    return (core, mine), (1 - core, theirs)


def left_kernel(q_hbm, g_hbm, e_hbm, m_ref, mh_ref, ml_ref, send_a, send_b, keep_a, keep_b, q_buf, g_buf, q_sem, sems, *, chunk, devices):
    mine, theirs = sides(devices)
    rank, quarter = q_buf.shape[0], send_a.shape[2]
    half = rank // 2
    q_copy = pltpu.make_async_copy(q_hbm, q_buf, q_sem)
    q_copy.start()
    places = ((theirs, 0, send_a), (theirs, 1, send_b), (mine, 0, keep_a), (mine, 1, keep_b))
    steps = [(side, pl.multiple_of((2 * side[0] + k) * quarter + at, chunk), out, at) for side, k, out in places for at in range(0, quarter, chunk)]
    copies = []
    for n, (_, row, _, _) in enumerate(steps):
        rows = pl.ds(row, chunk)
        pair = (
            pltpu.make_async_copy(g_hbm.at[rows], g_buf.at[pl.ds(n * chunk, chunk)], sems.at[n, 0]),
            pltpu.make_async_copy(e_hbm.at[rows], m_ref.at[rows], sems.at[n, 1]),
        )
        for copy in pair:
            copy.start()
        copies.append(pair)
    q_copy.wait()
    factors = {}
    for side in (theirs, mine):
        ordered = stack([q_buf[pl.ds(pl.multiple_of(at * half, half), half), :] for at in (1 - side[1], side[1])])
        q = stack(split(ordered, 3))
        factors[id(side)] = jnp.concatenate([q, q], axis=1)
    for n, (side, row, out, at) in enumerate(steps):
        for copy in copies[n]:
            copy.wait()
        rows = pl.ds(row, chunk)
        m = m_ref[rows] + g_buf[n * chunk : (n + 1) * chunk].astype(F32)
        m_ref[rows] = m
        mh, ml = split(m, 2)
        mh_ref[rows] = mh
        ml_ref[rows] = ml
        p = fold(dot(jnp.concatenate([mh, ml], axis=1), factors[id(side)], (1, 1)).T, rank)
        out[0, :, at : at + chunk] = p[:half]
        out[1, :, at : at + chunk] = p[half:]


def whole(own, other, bit):
    a, b = own[...], other[...]
    return stack([jnp.where(bit == 0, a, b), jnp.where(bit == 0, b, a)])


def square(p, rank):
    g = fold(dot(p, p, (1, 1)), rank)
    return g[:, :rank] + g[:, rank : 2 * rank] + g[:, 2 * rank :]


def right_kernel(a0, a1, b0, b1, mh_ref, ml_ref, *refs, mine, devices):
    core, bit = sides(devices)[0 if mine else 1]
    quarter = a0.shape[1]
    rank = 2 * a0.shape[0]
    t = gram = None
    for k, pair in enumerate(((a0, a1), (b0, b1))):
        rows = pl.ds(pl.multiple_of((2 * core + k) * quarter, quarter), quarter)
        p = stack(split(whole(*pair, bit), 3))
        part = dot(p, mh_ref[rows], (1, 0)) + dot(p, ml_ref[rows], (1, 0))
        t = part if t is None else t + part
        if mine:
            g = square(p, rank)
            gram = g if gram is None else gram + g
    if mine:
        t_ref, gram_ref = refs
        t_ref[...] = fold(t, rank)
        gram_ref[...] = gram
    else:
        before, t_ref = refs
        t_ref[...] = before[...] + fold(t, rank)


def eliminate(a, pivots):
    rank = a.shape[0]
    row = lax.broadcasted_iota(jnp.int32, (rank, 1), 0)
    for k in pivots:
        line = a[k : k + 1, :] / a[k : k + 1, k : k + 1]
        a = a - jnp.where(row > k, a[:, k : k + 1], 0.0) * line
    return a


def factor_kernel(gram_ref, a0, a1, b0, b1, state_ref, *, devices):
    _, bit = sides(devices)[1]
    rank = gram_ref.shape[0]
    gram = gram_ref[...]
    for pair in ((a0, a1), (b0, b1)):
        gram = gram + square(stack(split(whole(*pair, bit), 3)), rank)
    row = lax.broadcasted_iota(jnp.int32, (rank, 128), 0)
    lane = lax.broadcasted_iota(jnp.int32, (rank, 128), 1)
    eye = (lane == row + rank).astype(F32)
    state_ref[...] = eliminate(jnp.concatenate([gram, eye[:, rank:]], axis=1), range(rank // 2))


def inverse_kernel(state_ref, inv_ref):
    rank = state_ref.shape[0]
    a = eliminate(state_ref[...], range(rank // 2, rank - 1))
    row = lax.broadcasted_iota(jnp.int32, a.shape, 0)
    lane = lax.broadcasted_iota(jnp.int32, a.shape, 1)
    pivots = jnp.sum(jnp.where(row == lane, a, 0.0), axis=1, keepdims=True)
    inv_ref[...] = a[:, rank : 2 * rank] / jnp.sqrt(pivots)


def hat_kernel(inv_ref, *refs, devices):
    pieces, (hat_ref, rows_ref) = refs[:8], refs[8:]
    quarter = pieces[0].shape[1]
    a, b, c = split(inv_ref[...], 3)
    left = jnp.concatenate([a, a, b, a, b, c], axis=1)
    for n, (core, bit) in enumerate(sides(devices)):
        for k in range(2):
            start = pl.multiple_of((2 * core + k) * quarter, quarter)
            u, v, w = split(whole(*pieces[4 * n + 2 * k : 4 * n + 2 * k + 2], bit), 3)
            hat = dot(left, stack([u, v, u, w, v, u]), (1, 0))
            hat_ref[:, pl.ds(start, quarter)] = hat
            u, v = split(hat, 2)
            rows_ref[pl.ds(start, quarter), :] = stack([u, v, u, v]).T


def error_kernel(t0_ref, t1_ref, inv_ref, rows_ref, m_ref, out_hbm, q_ref, buf, sems, *, replicas, block):
    q = jnp.dot(inv_ref[...], t0_ref[...] + t1_ref[...], precision=lax.Precision.HIGHEST, preferred_element_type=F32) / replicas
    q_ref[...] = q
    u, v = split(q, 2)
    terms = stack([u, u, v, v])
    copies = []
    for n in range(buf.shape[0] // block):
        rows = slice(n * block, (n + 1) * block)
        buf[rows] = m_ref[rows] - dot(rows_ref[rows], terms, (1, 0))
        copy = pltpu.make_async_copy(buf.at[pl.ds(n * block, block)], out_hbm.at[pl.ds(n * block, block)], sems.at[n])
        copy.start()
        copies.append(copy)
    for copy in copies:
        copy.wait()


def shards(gradient, error_buffer, q_given):
    replicas, tensors = lax.axis_size("dp"), lax.axis_size("tensor")
    devices = replicas * tensors
    depth, columns = gradient.shape[1:]
    rank = q_given.shape[1]
    half, quarter = rank // 2, depth // 4
    chunk = next(n for n in (384, 256, 128) if quarter % n == 0)
    steps = depth // chunk

    def call(kernel, name, flops, **kw):
        return pl.pallas_call(
            kernel,
            name=name,
            compiler_params=pltpu.CompilerParams(vmem_limit_bytes=LIMIT),
            cost_estimate=pl.CostEstimate(flops=flops, bytes_accessed=0, transcendentals=0),
            **kw,
        )

    in_hbm = [pltpu.with_memory_space_constraint(x, pltpu.HBM) for x in (q_given.T, gradient[0], error_buffer[0])]
    piece = pltpu.VMEM((2, half, quarter), F32)
    m, mh, ml, *partial = call(
        functools.partial(left_kernel, chunk=chunk, devices=devices),
        "left_products",
        12 * depth * columns * rank,
        out_shape=(pltpu.VMEM((depth, columns), F32), pltpu.VMEM((depth, columns), BF16), pltpu.VMEM((depth, columns), BF16)) + (piece,) * 4,
        in_specs=[HBM] * 3,
        out_specs=(VMEM,) * 7,
        scratch_shapes=[
            pltpu.VMEM((rank, columns), F32),
            pltpu.VMEM((depth, columns), BF16),
            pltpu.SemaphoreType.DMA(()),
            pltpu.SemaphoreType.DMA((steps, 2)),
        ],
    )(*in_hbm)

    def swap(x, bit, bit1=None):
        choice = (bit, bit if bit1 is None else bit1)
        return lax.ppermute(x, AXES, [(i, i ^ choice[i & 1]) for i in range(devices)])

    walk = list(zip(*walks(devices), strict=True))
    sums = [swap(send, 1) for send in partial[:2]]
    sums = [keep + got for keep, got in zip(partial[2:], sums, strict=True)]
    arrived = [swap(x[0], *walk[0]) for x in sums]
    sums = [x[1] + got for x, got in zip(sums, arrived, strict=True)]
    for bits in walk[1:]:
        arrived = [swap(x, *bits) for x in sums]
        sums = [x + got for x, got in zip(sums, arrived, strict=True)]
    others = [swap(x, *walk[0]) for x in sums]
    mine = (sums[0], others[0], sums[1], others[1])
    theirs = tuple(swap(x, 1) for x in mine)

    wide = (pltpu.VMEM((rank, columns), F32), pltpu.VMEM((rank, rank), F32))
    t, gram = call(
        functools.partial(right_kernel, mine=True, devices=devices),
        "right_products_own",
        6 * depth * columns * rank,
        out_shape=wide,
        in_specs=[VMEM] * 6,
        out_specs=(VMEM, VMEM),
    )(*mine, mh, ml)
    t = call(
        functools.partial(right_kernel, mine=False, devices=devices),
        "right_products_other",
        6 * depth * columns * rank,
        out_shape=wide[0],
        in_specs=[VMEM] * 7,
        out_specs=VMEM,
    )(*theirs, mh, ml, t)

    state = call(
        functools.partial(factor_kernel, devices=devices),
        "factor_first_half",
        6 * depth * columns * rank,
        out_shape=pltpu.VMEM((rank, 128), F32),
        in_specs=[VMEM] * 5,
        out_specs=VMEM,
    )(gram, *theirs)
    inverse = call(
        inverse_kernel,
        "factor_second_half",
        6 * depth * columns * rank,
        out_shape=pltpu.VMEM((rank, rank), F32),
        in_specs=[VMEM],
        out_specs=VMEM,
    )(state)
    hat, hat_rows = call(
        functools.partial(hat_kernel, devices=devices),
        "left_factor",
        6 * depth * columns * rank,
        out_shape=(jax.ShapeDtypeStruct((rank, depth), F32), pltpu.VMEM((depth, 4 * rank), BF16)),
        in_specs=[VMEM] * 9,
        out_specs=(VMEM, VMEM),
    )(inverse, *mine, *theirs)

    bits = [bit for bit in walks(devices)[0] if bit >= tensors]
    work = [state, inverse]
    got = swap(t, bits[0])
    for n, bit in enumerate(bits[1:]):
        t = t + got
        if n < len(work):
            t, _ = lax.optimization_barrier((t, work[n]))
        got = swap(t, bit)

    block = next(n for n in (512, 256, 128) if depth % n == 0)
    error, q_new = call(
        functools.partial(error_kernel, replicas=replicas, block=block),
        "new_error",
        8 * depth * rank * columns,
        out_shape=(pltpu.HBM((depth, columns), F32), jax.ShapeDtypeStruct((rank, columns), F32)),
        in_specs=[VMEM] * 5,
        out_specs=(HBM, VMEM),
        scratch_shapes=[pltpu.VMEM((depth, columns), F32), pltpu.SemaphoreType.DMA((depth // block,))],
    )(t, got, inverse, hat_rows, m)
    return (error[None], hat.T, q_new.T)


def solution(mesh):
    placed = (P("dp", None, "tensor"), P("dp", None, "tensor"), P("tensor", None))
    return jax.shard_map(
        shards,
        mesh=mesh,
        in_specs=placed,
        out_specs=(P("dp", None, "tensor"), P(), P("tensor", None)),
        check_vma=False,
    )
```

time: 188 us -> 55.2 us (0.29)
  waiting for transfers between devices: 98.1 us -> 11.7 us
  blocking collectives: 43 us -> 0 us
  starting transfers between devices: 0.08 us -> 25.7 us
  matrix products: 23.7 us -> 0 us
  Pallas kernels: 0 us -> 16.8 us
  between operations: 14.1 us -> 0.74 us
  other arithmetic: 6.7 us -> 0.13 us
    psum x1 -> x0, waiting for transfers between devices: 73.2 us -> none  [shards(): p_block = lax.psum(p_block, 'dp')]
    psum x1 -> x0, blocking collectives: 35.3 us -> none  [shards(): q_new = lax.psum(q_local, 'dp') / lax.axis_size('dp')]
    ppermute x0 -> x19, starting transfers between devices: none -> 25.7 us  [swap(): lax.ppermute(x, AXES, [(i, i ^ choice[i & 1]) for i in range(devices)])]
    reduce_scatter x1 -> x0, waiting for transfers between devices: 24.9 us -> none  [shards(): lax.psum_scatter(jnp.dot(merged, q_given, precision=highest, preferred_el...]
    dot_general x4 -> x0, matrix products: 23 us -> none  [the longest x1 8.81 us: shards(): jnp.dot(p_hat, q_new.T, precision=highest, preferred_element_type=jnp.flo...]
    pallas_call x0 -> x7, Pallas kernels: none -> 16.8 us  [the longest x1 7.97 us: shards(): call(functools.partial(left_kernel, chunk=chunk, devices=devices), 'left_...]
    ppermute x0 -> x19, waiting for transfers between devices: none -> 11.7 us  [swap(): lax.ppermute(x, AXES, [(i, i ^ choice[i & 1]) for i in range(devices)])]
    all_gather x1 -> x0, blocking collectives: 7.7 us -> none  [shards(): p_sum = lax.all_gather(p_block, 'tensor', axis=0, tiled=True)]
  transfers between devices with their start and end apart: 2 -> 19, of which waited for: 2 -> 11; matrix products, arithmetic and copies ran while one was open for 0% -> 0% of each run, Pallas kernels for 0% -> 9%
where the time goes in v2:
time: 55.2 us; the launch traced here: 55 us
  starting transfers between devices  25.7 us (47%)
  Pallas kernels  16.8 us (30%)
  waiting for transfers between devices  11.7 us (21%)
  between operations  0.74 us (1%)
    ppermute x19, starting transfers between devices, swap(): lax.ppermute(x, AXES, [(i, i ^ choice[i & 1]) for i in range(devices)])  25.7 us
    ppermute x19, waiting for transfers between devices, swap(): lax.ppermute(x, AXES, [(i, i ^ choice[i & 1]) for i in range(devices)])  11.7 us
    pallas_call x1, Pallas kernels, shards(): call(functools.partial(left_kernel, chunk=chunk, devices=devices), 'left_...  7.97 us
    pallas_call x1, Pallas kernels, shards(): call(functools.partial(error_kernel, replicas=replicas, block=block), 'ne...  3.27 us
    pallas_call x1, Pallas kernels, shards(): call(functools.partial(factor_kernel, devices=devices), 'factor_first_hal...  1.69 us
    pallas_call x1, Pallas kernels, shards(): call(functools.partial(hat_kernel, devices=devices), 'left_factor', 6 * d...  1.36 us
    pallas_call x1, Pallas kernels, shards(): call(inverse_kernel, 'factor_second_half', 6 * depth * columns * rank, ou...  1.34 us
  transfers between devices with their start and end apart: 19, of which 11 were waited for; matrix products, arithmetic and copies ran while one was open for 0% of the time, Pallas kernels for 9%

profile of v2, /device:TPU:0, one launch (start us, length us, event | category | flops | bytes accessed | tf_op | source)
XLA Modules:
  0.0 55.0 jit_solution(15250656804966001209)
XLA Ops:
  0.6 8.0 %left_products.1 = (f32[4608,256]{1,0:T(8,128)S(1)}, bf16[4608,256]{1,0:T(8,128)(2,1)S(1)}, bf16[4608,256]{1,0:T(8,128)(2,1)S(1)}, f32[2,16,1152]{2,1,0:T(8,128)...) custom-call(f32[32,256]{1,0:T(8,128)} %bitcast.20, ...), custom_call_target="tpu_custom_call" | custom-call | flops 452984832 | tf_op jit(solution)/shard_map/left_products/pallas_call | solution.py:209
  8.6 0.6 %collective-permute-start = (f32[2,16,1152]{2,1,0:T(8,128)S(1)}, f32[2,16,1152]{2,1,0:T(8,128)S(1)}, u32[]{:S(2)}, u32[]{:S(2)}) collective-permute-start(f32[2,16,1152]{2,1,0:T(8,128)S(1)} %get-tuple-element.19), channel_id=1, source_target_pairs={{0,1},{1,0},{2,3},{3,2},{4,5},{5,4},{6,7},{7,6},{8,9},{9,8},{10,11... | collective-permute-start | bytes 442376 | tf_op jit(solution)/shard_map/ppermute | solution.py:226
  9.2 0.1 collective-permute-start.8
  9.3 0.9 %collective-permute-done = f32[2,16,1152]{2,1,0:T(8,128)S(1)} collective-permute-done((f32[2,16,1152]{2,1,0:T(8,128)S(1)}, f32[2,16,1152]{2,1,0:T(8,128)S(1)}, u32[]{:S(2)}, u32[]{:S(2)}) %collective-permute-start) | collective-permute-done | bytes 147488 | tf_op jit(solution)/shard_map/ppermute | solution.py:226
  10.3 2.8 %collective-permute-start.1 = (f32[16,1152]{1,0:T(8,128)S(1)}, f32[16,1152]{1,0:T(8,128)S(1)}, u32[]{:S(2)}, u32[]{:S(2)}) collective-permute-start(f32[16,1152]{1,0:T(8,128)S(1)} %slice_bitcast_fusion.2), channel_id=1, source_target_pairs={{0,2},{1,9},{2,0},{3,11},{4,6},{5,13},{6,4},{7,15},{8,10},{9,1},{1... | collective-permute-start | bytes 221192 | tf_op jit(solution)/shard_map/ppermute | solution.py:226
  13.1 0.0 collective-permute-done.8
  13.1 0.2 collective-permute-start.9
  13.3 2.1 %collective-permute-done.1 = f32[16,1152]{1,0:T(8,128)S(1)} collective-permute-done((f32[16,1152]{1,0:T(8,128)S(1)}, f32[16,1152]{1,0:T(8,128)S(1)}, u32[]{:S(2)}, u32[]{:S(2)}) %collective-permute-start.1) | collective-permute-done | bytes 73760 | tf_op jit(solution)/shard_map/ppermute | solution.py:226
  15.4 2.1 %collective-permute-start.2 = (f32[16,1152]{1,0:T(8,128)S(1)}, f32[16,1152]{1,0:T(8,128)S(1)}, u32[]{:S(2)}, u32[]{:S(2)}) collective-permute-start(f32[16,1152]{1,0:T(8,128)S(1)} %fusion.1), channel_id=1, source_target_pairs={{0,4},{1,17},{2,6},{3,19},{4,0},{5,21},{6,2},{7,23},{8,12},{9,25},... | collective-permute-start | bytes 221192 | tf_op jit(solution)/shard_map/ppermute | solution.py:226
  17.5 0.0 collective-permute-done.9
  17.6 1.6 %collective-permute-start.10 = (f32[16,1152]{1,0:T(8,128)S(1)}, f32[16,1152]{1,0:T(8,128)S(1)}, u32[]{:S(2)}, u32[]{:S(2)}) collective-permute-start(f32[16,1152]{1,0:T(8,128)S(1)} %fusion), channel_id=1, source_target_pairs={{0,4},{1,17},{2,6},{3,19},{4,0},{5,21},{6,2},{7,23},{8,12},{9,25},... | collective-permute-start | bytes 221192 | tf_op jit(solution)/shard_map/ppermute | solution.py:226
  19.1 0.7 %collective-permute-done.2 = f32[16,1152]{1,0:T(8,128)S(1)} collective-permute-done((f32[16,1152]{1,0:T(8,128)S(1)}, f32[16,1152]{1,0:T(8,128)S(1)}, u32[]{:S(2)}, u32[]{:S(2)}) %collective-permute-start.2) | collective-permute-done | bytes 73760 | tf_op jit(solution)/shard_map/ppermute | solution.py:226
  19.9 2.1 %collective-permute-start.3 = (f32[16,1152]{1,0:T(8,128)S(1)}, f32[16,1152]{1,0:T(8,128)S(1)}, u32[]{:S(2)}, u32[]{:S(2)}) collective-permute-start(f32[16,1152]{1,0:T(8,128)S(1)} %add.38), channel_id=1, source_target_pairs={{0,8},{1,5},{2,10},{3,7},{4,12},{5,1},{6,14},{7,3},{8,0},{9,13},{1... | collective-permute-start | bytes 221192 | tf_op jit(solution)/shard_map/ppermute | solution.py:226
  22.0 0.0 collective-permute-done.10
  22.1 1.6 %collective-permute-start.11 = (f32[16,1152]{1,0:T(8,128)S(1)}, f32[16,1152]{1,0:T(8,128)S(1)}, u32[]{:S(2)}, u32[]{:S(2)}) collective-permute-start(f32[16,1152]{1,0:T(8,128)S(1)} %add.43), channel_id=1, source_target_pairs={{0,8},{1,5},{2,10},{3,7},{4,12},{5,1},{6,14},{7,3},{8,0},{9,13},{1... | collective-permute-start | bytes 221192 | tf_op jit(solution)/shard_map/ppermute | solution.py:226
  23.6 0.7 %collective-permute-done.3 = f32[16,1152]{1,0:T(8,128)S(1)} collective-permute-done((f32[16,1152]{1,0:T(8,128)S(1)}, f32[16,1152]{1,0:T(8,128)S(1)}, u32[]{:S(2)}, u32[]{:S(2)}) %collective-permute-start.3) | collective-permute-done | bytes 73760 | tf_op jit(solution)/shard_map/ppermute | solution.py:226
  24.4 3.1 %collective-permute-start.4 = (f32[16,1152]{1,0:T(8,128)S(1)}, f32[16,1152]{1,0:T(8,128)S(1)}, u32[]{:S(2)}, u32[]{:S(2)}) collective-permute-start(f32[16,1152]{1,0:T(8,128)S(1)} %add.39), channel_id=1, source_target_pairs={{0,16},{1,3},{2,18},{3,1},{4,20},{5,7},{6,22},{7,5},{8,24},{9,11},... | collective-permute-start | bytes 221192 | tf_op jit(solution)/shard_map/ppermute | solution.py:226
  27.5 0.0 collective-permute-done.11
  27.5 1.7 %collective-permute-start.12 = (f32[16,1152]{1,0:T(8,128)S(1)}, f32[16,1152]{1,0:T(8,128)S(1)}, u32[]{:S(2)}, u32[]{:S(2)}) collective-permute-start(f32[16,1152]{1,0:T(8,128)S(1)} %add.44), channel_id=1, source_target_pairs={{0,16},{1,3},{2,18},{3,1},{4,20},{5,7},{6,22},{7,5},{8,24},{9,11},... | collective-permute-start | bytes 221192 | tf_op jit(solution)/shard_map/ppermute | solution.py:226
  29.2 0.6 %collective-permute-done.4 = f32[16,1152]{1,0:T(8,128)S(1)} collective-permute-done((f32[16,1152]{1,0:T(8,128)S(1)}, f32[16,1152]{1,0:T(8,128)S(1)}, u32[]{:S(2)}, u32[]{:S(2)}) %collective-permute-start.4) | collective-permute-done | bytes 73760 | tf_op jit(solution)/shard_map/ppermute | solution.py:226
  29.9 1.9 %collective-permute-start.6 = (f32[16,1152]{1,0:T(8,128)S(1)}, f32[16,1152]{1,0:T(8,128)S(1)}, u32[]{:S(2)}, u32[]{:S(2)}) collective-permute-start(f32[16,1152]{1,0:T(8,128)S(1)} %add.40.a0.refs_0_), channel_id=1, source_target_pairs={{0,2},{1,9},{2,0},{3,11},{4,6},{5,13},{6,4},{7,15},{8,10},{9,1},{1... | collective-permute-start | bytes 221192 | tf_op jit(solution)/shard_map/ppermute | solution.py:226
  31.8 1.0 %collective-permute-done.12 = f32[16,1152]{1,0:T(8,128)S(1)} collective-permute-done((f32[16,1152]{1,0:T(8,128)S(1)}, f32[16,1152]{1,0:T(8,128)S(1)}, u32[]{:S(2)}, u32[]{:S(2)}) %collective-permute-start.12) | collective-permute-done | bytes 73760 | tf_op jit(solution)/shard_map/ppermute | solution.py:226
  32.8 1.6 %collective-permute-start.14 = (f32[16,1152]{1,0:T(8,128)S(1)}, f32[16,1152]{1,0:T(8,128)S(1)}, u32[]{:S(2)}, u32[]{:S(2)}) collective-permute-start(f32[16,1152]{1,0:T(8,128)S(1)} %add.45.b0.refs_2_), channel_id=1, source_target_pairs={{0,2},{1,9},{2,0},{3,11},{4,6},{5,13},{6,4},{7,15},{8,10},{9,1},{1... | collective-permute-start | bytes 221192 | tf_op jit(solution)/shard_map/ppermute | solution.py:226
  34.4 0.0 collective-permute-start.5
  34.4 0.5 collective-permute-start.13
  34.9 0.0 collective-permute-done.6.a1.refs_1_
  34.9 0.0 collective-permute-start.7
  34.9 2.3 %collective-permute-done.14.b1.refs_3_ = f32[16,1152]{1,0:T(8,128)S(1)} collective-permute-done((f32[16,1152]{1,0:T(8,128)S(1)}, f32[16,1152]{1,0:T(8,128)S(1)}, u32[]{:S(2)}, u32[]{:S(2)}) %collective-permute-start.14) | collective-permute-done | bytes 73760 | tf_op jit(solution)/shard_map/ppermute | solution.py:226
  37.2 0.0 collective-permute-start.15
  37.2 0.7 %right_products_own.1 = (f32[32,256]{1,0:T(8,128)S(1)}, f32[32,32]{1,0:T(8,128)S(1)}) custom-call(f32[16,1152]{1,0:T(8,128)S(1)} %add.40.a0.refs_0_, f32[16,1152]{1,0:T(8,128)S(1)} %collective-permute-done.6.a1.refs_1_, f32[16,1152]{1,0:T(8,128)S(1)} %add.45.b0.refs_2_, f32[16,1152]{1,0:T(8,128)S(1)} %collective-permute-done.14.b1.refs_3_, ...), custom_call_target="tpu_custom_call" | custom-call | flops 226492416 | tf_op jit(solution)/shard_map/right_products_own/pallas_call | solution.py:241
  37.9 0.0 collective-permute-done.5.a0.refs_4_
  37.9 0.0 collective-permute-done.13.b0.refs_6_
  37.9 0.0 collective-permute-done.7.a1.refs_5_
  38.0 0.6 %collective-permute-done.15.b1.refs_7_ = f32[16,1152]{1,0:T(8,128)S(1)} collective-permute-done((f32[16,1152]{1,0:T(8,128)S(1)}, f32[16,1152]{1,0:T(8,128)S(1)}, u32[]{:S(2)}, u32[]{:S(2)}) %collective-permute-start.15) | collective-permute-done | bytes 73760 | tf_op jit(solution)/shard_map/ppermute | solution.py:226
  38.5 0.5 right_products_other.1
  39.0 1.6 %collective-permute-start.16 = (f32[32,256]{1,0:T(8,128)S(1)}, f32[32,256]{1,0:T(8,128)S(1)}, u32[]{:S(2)}, u32[]{:S(2)}) collective-permute-start(f32[32,256]{1,0:T(8,128)S(1)} %right_products_other.1), channel_id=1, source_target_pairs={{0,4},{1,5},{2,6},{3,7},{4,0},{5,1},{6,2},{7,3},{8,12},{9,13},{10,... | collective-permute-start | bytes 98312 | tf_op jit(solution)/shard_map/ppermute | solution.py:226
  40.6 1.7 %factor_first_half.1.state_ref = f32[32,128]{1,0:T(8,128)S(1)} custom-call(f32[32,32]{1,0:T(8,128)S(1)} %get-tuple-element.25.gram_ref, f32[16,1152]{1,0:T(8,128)S(1)} %collective-permute-done.5.a0.refs_4_, f32[16,1152]{1,0:T(8,128)S(1)} %collective-permute-done.7.a1.refs_5_, f32[16,1152]{1,0:T(8,128)S(1)} %collective-permute-done.13.b0.refs_6_, ...), custom_call_target="tpu_custom_call" | custom-call | flops 226492416 | tf_op jit(solution)/shard_map/factor_first_half/pallas_call | solution.py:258
  42.3 0.7 %collective-permute-done.16 = f32[32,256]{1,0:T(8,128)S(1)} collective-permute-done((f32[32,256]{1,0:T(8,128)S(1)}, f32[32,256]{1,0:T(8,128)S(1)}, u32[]{:S(2)}, u32[]{:S(2)}) %collective-permute-start.16) | collective-permute-done | bytes 32800 | tf_op jit(solution)/shard_map/ppermute | solution.py:226
  43.0 1.9 %collective-permute-start.17 = (f32[32,256]{1,0:T(8,128)S(1)}, f32[32,256]{1,0:T(8,128)S(1)}, u32[]{:S(2)}, u32[]{:S(2)}) collective-permute-start(f32[32,256]{1,0:T(8,128)S(1)} %add.46), channel_id=1, source_target_pairs={{0,8},{1,9},{2,10},{3,11},{4,12},{5,13},{6,14},{7,15},{8,0},{9,1},... | collective-permute-start | bytes 98312 | tf_op jit(solution)/shard_map/ppermute | solution.py:226
  45.0 1.3 %factor_second_half.1.inv_ref = f32[32,32]{1,0:T(8,128)S(1)} custom-call(f32[32,128]{1,0:T(8,128)S(1)} %factor_first_half.1.state_ref), custom_call_target="tpu_custom_call" | custom-call | flops 226492416 | tf_op jit(solution)/shard_map/factor_second_half/pallas_call | solution.py:266
  46.3 0.6 %collective-permute-done.17 = f32[32,256]{1,0:T(8,128)S(1)} collective-permute-done((f32[32,256]{1,0:T(8,128)S(1)}, f32[32,256]{1,0:T(8,128)S(1)}, u32[]{:S(2)}, u32[]{:S(2)}) %collective-permute-start.17) | collective-permute-done | bytes 32800 | tf_op jit(solution)/shard_map/ppermute | solution.py:226
  46.9 2.2 %collective-permute-start.18 = (f32[32,256]{1,0:T(8,128)S(1)}, f32[32,256]{1,0:T(8,128)S(1)}, u32[]{:S(2)}, u32[]{:S(2)}) collective-permute-start(f32[32,256]{1,0:T(8,128)S(1)} %add.47.t0_ref), channel_id=1, source_target_pairs={{0,16},{1,17},{2,18},{3,19},{4,20},{5,21},{6,22},{7,23},{8,24},{9,... | collective-permute-start | bytes 98312 | tf_op jit(solution)/shard_map/ppermute | solution.py:226
  49.2 1.4 %left_factor.1 = (f32[32,4608]{1,0:T(8,128)}, bf16[4608,128]{1,0:T(8,128)(2,1)S(1)}) custom-call(f32[32,32]{1,0:T(8,128)S(1)} %factor_second_half.1.inv_ref, f32[16,1152]{1,0:T(8,128)S(1)} %add.40.a0.refs_0_, f32[16,1152]{1,0:T(8,128)S(1)} %collective-permute-done.6.a1.refs_1_, f32[16,1152]{1,0:T(8,128)S(1)} %add.45.b0.refs_2_, ...), custom_call_target="tpu_custom_call" | custom-call | flops 226492416 | tf_op jit(solution)/shard_map/left_factor/pallas_call | solution.py:274
  50.5 1.2 %collective-permute-done.18.t1_ref = f32[32,256]{1,0:T(8,128)S(1)} collective-permute-done((f32[32,256]{1,0:T(8,128)S(1)}, f32[32,256]{1,0:T(8,128)S(1)}, u32[]{:S(2)}, u32[]{:S(2)}) %collective-permute-start.18) | collective-permute-done | bytes 32800 | tf_op jit(solution)/shard_map/ppermute | solution.py:226
  51.8 3.3 %new_error.1 = (f32[4608,256]{1,0:T(8,128)}, f32[32,256]{1,0:T(8,128)}) custom-call(f32[32,256]{1,0:T(8,128)S(1)} %add.47.t0_ref, f32[32,256]{1,0:T(8,128)S(1)} %collective-permute-done.18.t1_ref, f32[32,32]{1,0:T(8,128)S(1)} %factor_second_half.1.inv_ref, bf16[4608,128]{1,0:T(8,128)(2,1)S(1)} %get-tuple-element.28.rows_ref, ...), custom_call_target="tpu_custom_call" | custom-call | flops 301989888 | tf_op jit(solution)/shard_map/new_error/pallas_call | solution.py:293
  (14 shorter events, 0.1 us)
Async XLA Ops:
  8.6 1.6 %collective-permute-start = (f32[2,16,1152]{2,1,0:T(8,128)S(1)}, f32[2,16,1152]{2,1,0:T(8,128)S(1)}, u32[]{:S(2)}, u32[]{:S(2)}) collective-permute-start(f32[2,16,1152]{2,1,0:T(8,128)S(1)} %get-tuple-element.19), channel_id=1, source_target_pairs={{0,1},{1,0},{2,3},{3,2},{4,5},{5,4},{6,7},{7,6},{8,9},{9,8},{10,11... | collective-permute-start | bytes 442376 | tf_op jit(solution)/shard_map/ppermute | solution.py:226
  9.2 3.9 %collective-permute-start.8 = (f32[2,16,1152]{2,1,0:T(8,128)S(1)}, f32[2,16,1152]{2,1,0:T(8,128)S(1)}, u32[]{:S(2)}, u32[]{:S(2)}) collective-permute-start(f32[2,16,1152]{2,1,0:T(8,128)S(1)} %get-tuple-element.21), channel_id=1, source_target_pairs={{0,1},{1,0},{2,3},{3,2},{4,5},{5,4},{6,7},{7,6},{8,9},{9,8},{10,11... | collective-permute-start | bytes 442376 | tf_op jit(solution)/shard_map/ppermute | solution.py:226
  10.3 5.2 %collective-permute-start.1 = (f32[16,1152]{1,0:T(8,128)S(1)}, f32[16,1152]{1,0:T(8,128)S(1)}, u32[]{:S(2)}, u32[]{:S(2)}) collective-permute-start(f32[16,1152]{1,0:T(8,128)S(1)} %slice_bitcast_fusion.2), channel_id=1, source_target_pairs={{0,2},{1,9},{2,0},{3,11},{4,6},{5,13},{6,4},{7,15},{8,10},{9,1},{1... | collective-permute-start | bytes 221192 | tf_op jit(solution)/shard_map/ppermute | solution.py:226
  13.1 4.4 %collective-permute-start.9 = (f32[16,1152]{1,0:T(8,128)S(1)}, f32[16,1152]{1,0:T(8,128)S(1)}, u32[]{:S(2)}, u32[]{:S(2)}) collective-permute-start(f32[16,1152]{1,0:T(8,128)S(1)} %slice_bitcast_fusion), channel_id=1, source_target_pairs={{0,2},{1,9},{2,0},{3,11},{4,6},{5,13},{6,4},{7,15},{8,10},{9,1},{1... | collective-permute-start | bytes 221192 | tf_op jit(solution)/shard_map/ppermute | solution.py:226
  15.4 4.4 %collective-permute-start.2 = (f32[16,1152]{1,0:T(8,128)S(1)}, f32[16,1152]{1,0:T(8,128)S(1)}, u32[]{:S(2)}, u32[]{:S(2)}) collective-permute-start(f32[16,1152]{1,0:T(8,128)S(1)} %fusion.1), channel_id=1, source_target_pairs={{0,4},{1,17},{2,6},{3,19},{4,0},{5,21},{6,2},{7,23},{8,12},{9,25},... | collective-permute-start | bytes 221192 | tf_op jit(solution)/shard_map/ppermute | solution.py:226
  17.6 4.5 %collective-permute-start.10 = (f32[16,1152]{1,0:T(8,128)S(1)}, f32[16,1152]{1,0:T(8,128)S(1)}, u32[]{:S(2)}, u32[]{:S(2)}) collective-permute-start(f32[16,1152]{1,0:T(8,128)S(1)} %fusion), channel_id=1, source_target_pairs={{0,4},{1,17},{2,6},{3,19},{4,0},{5,21},{6,2},{7,23},{8,12},{9,25},... | collective-permute-start | bytes 221192 | tf_op jit(solution)/shard_map/ppermute | solution.py:226
  19.9 4.5 %collective-permute-start.3 = (f32[16,1152]{1,0:T(8,128)S(1)}, f32[16,1152]{1,0:T(8,128)S(1)}, u32[]{:S(2)}, u32[]{:S(2)}) collective-permute-start(f32[16,1152]{1,0:T(8,128)S(1)} %add.38), channel_id=1, source_target_pairs={{0,8},{1,5},{2,10},{3,7},{4,12},{5,1},{6,14},{7,3},{8,0},{9,13},{1... | collective-permute-start | bytes 221192 | tf_op jit(solution)/shard_map/ppermute | solution.py:226
  22.1 5.4 %collective-permute-start.11 = (f32[16,1152]{1,0:T(8,128)S(1)}, f32[16,1152]{1,0:T(8,128)S(1)}, u32[]{:S(2)}, u32[]{:S(2)}) collective-permute-start(f32[16,1152]{1,0:T(8,128)S(1)} %add.43), channel_id=1, source_target_pairs={{0,8},{1,5},{2,10},{3,7},{4,12},{5,1},{6,14},{7,3},{8,0},{9,13},{1... | collective-permute-start | bytes 221192 | tf_op jit(solution)/shard_map/ppermute | solution.py:226
  24.4 5.5 %collective-permute-start.4 = (f32[16,1152]{1,0:T(8,128)S(1)}, f32[16,1152]{1,0:T(8,128)S(1)}, u32[]{:S(2)}, u32[]{:S(2)}) collective-permute-start(f32[16,1152]{1,0:T(8,128)S(1)} %add.39), channel_id=1, source_target_pairs={{0,16},{1,3},{2,18},{3,1},{4,20},{5,7},{6,22},{7,5},{8,24},{9,11},... | collective-permute-start | bytes 221192 | tf_op jit(solution)/shard_map/ppermute | solution.py:226
  27.5 5.3 %collective-permute-start.12 = (f32[16,1152]{1,0:T(8,128)S(1)}, f32[16,1152]{1,0:T(8,128)S(1)}, u32[]{:S(2)}, u32[]{:S(2)}) collective-permute-start(f32[16,1152]{1,0:T(8,128)S(1)} %add.44), channel_id=1, source_target_pairs={{0,16},{1,3},{2,18},{3,1},{4,20},{5,7},{6,22},{7,5},{8,24},{9,11},... | collective-permute-start | bytes 221192 | tf_op jit(solution)/shard_map/ppermute | solution.py:226
  29.9 5.0 %collective-permute-start.6 = (f32[16,1152]{1,0:T(8,128)S(1)}, f32[16,1152]{1,0:T(8,128)S(1)}, u32[]{:S(2)}, u32[]{:S(2)}) collective-permute-start(f32[16,1152]{1,0:T(8,128)S(1)} %add.40.a0.refs_0_), channel_id=1, source_target_pairs={{0,2},{1,9},{2,0},{3,11},{4,6},{5,13},{6,4},{7,15},{8,10},{9,1},{1... | collective-permute-start | bytes 221192 | tf_op jit(solution)/shard_map/ppermute | solution.py:226
  32.8 4.4 %collective-permute-start.14 = (f32[16,1152]{1,0:T(8,128)S(1)}, f32[16,1152]{1,0:T(8,128)S(1)}, u32[]{:S(2)}, u32[]{:S(2)}) collective-permute-start(f32[16,1152]{1,0:T(8,128)S(1)} %add.45.b0.refs_2_), channel_id=1, source_target_pairs={{0,2},{1,9},{2,0},{3,11},{4,6},{5,13},{6,4},{7,15},{8,10},{9,1},{1... | collective-permute-start | bytes 221192 | tf_op jit(solution)/shard_map/ppermute | solution.py:226
  34.4 3.5 %collective-permute-start.5 = (f32[16,1152]{1,0:T(8,128)S(1)}, f32[16,1152]{1,0:T(8,128)S(1)}, u32[]{:S(2)}, u32[]{:S(2)}) collective-permute-start(f32[16,1152]{1,0:T(8,128)S(1)} %add.40.a0.refs_0_), channel_id=1, source_target_pairs={{0,1},{1,0},{2,3},{3,2},{4,5},{5,4},{6,7},{7,6},{8,9},{9,8},{10,11... | collective-permute-start | bytes 221192 | tf_op jit(solution)/shard_map/ppermute | solution.py:226
  34.4 3.6 %collective-permute-start.13 = (f32[16,1152]{1,0:T(8,128)S(1)}, f32[16,1152]{1,0:T(8,128)S(1)}, u32[]{:S(2)}, u32[]{:S(2)}) collective-permute-start(f32[16,1152]{1,0:T(8,128)S(1)} %add.45.b0.refs_2_), channel_id=1, source_target_pairs={{0,1},{1,0},{2,3},{3,2},{4,5},{5,4},{6,7},{7,6},{8,9},{9,8},{10,11... | collective-permute-start | bytes 221192 | tf_op jit(solution)/shard_map/ppermute | solution.py:226
  34.9 3.1 %collective-permute-start.7 = (f32[16,1152]{1,0:T(8,128)S(1)}, f32[16,1152]{1,0:T(8,128)S(1)}, u32[]{:S(2)}, u32[]{:S(2)}) collective-permute-start(f32[16,1152]{1,0:T(8,128)S(1)} %collective-permute-done.6.a1.refs_1_), channel_id=1, source_target_pairs={{0,1},{1,0},{2,3},{3,2},{4,5},{5,4},{6,7},{7,6},{8,9},{9,8},{10,11... | collective-permute-start | bytes 221192 | tf_op jit(solution)/shard_map/ppermute | solution.py:226
  37.2 1.3 %collective-permute-start.15 = (f32[16,1152]{1,0:T(8,128)S(1)}, f32[16,1152]{1,0:T(8,128)S(1)}, u32[]{:S(2)}, u32[]{:S(2)}) collective-permute-start(f32[16,1152]{1,0:T(8,128)S(1)} %collective-permute-done.14.b1.refs_3_), channel_id=1, source_target_pairs={{0,1},{1,0},{2,3},{3,2},{4,5},{5,4},{6,7},{7,6},{8,9},{9,8},{10,11... | collective-permute-start | bytes 221192 | tf_op jit(solution)/shard_map/ppermute | solution.py:226
  39.0 4.0 %collective-permute-start.16 = (f32[32,256]{1,0:T(8,128)S(1)}, f32[32,256]{1,0:T(8,128)S(1)}, u32[]{:S(2)}, u32[]{:S(2)}) collective-permute-start(f32[32,256]{1,0:T(8,128)S(1)} %right_products_other.1), channel_id=1, source_target_pairs={{0,4},{1,5},{2,6},{3,7},{4,0},{5,1},{6,2},{7,3},{8,12},{9,13},{10,... | collective-permute-start | bytes 98312 | tf_op jit(solution)/shard_map/ppermute | solution.py:226
  43.0 3.9 %collective-permute-start.17 = (f32[32,256]{1,0:T(8,128)S(1)}, f32[32,256]{1,0:T(8,128)S(1)}, u32[]{:S(2)}, u32[]{:S(2)}) collective-permute-start(f32[32,256]{1,0:T(8,128)S(1)} %add.46), channel_id=1, source_target_pairs={{0,8},{1,9},{2,10},{3,11},{4,12},{5,13},{6,14},{7,15},{8,0},{9,1},... | collective-permute-start | bytes 98312 | tf_op jit(solution)/shard_map/ppermute | solution.py:226
  46.9 4.8 %collective-permute-start.18 = (f32[32,256]{1,0:T(8,128)S(1)}, f32[32,256]{1,0:T(8,128)S(1)}, u32[]{:S(2)}, u32[]{:S(2)}) collective-permute-start(f32[32,256]{1,0:T(8,128)S(1)} %add.47.t0_ref), channel_id=1, source_target_pairs={{0,16},{1,17},{2,18},{3,19},{4,20},{5,21},{6,22},{7,23},{8,24},{9,... | collective-permute-start | bytes 98312 | tf_op jit(solution)/shard_map/ppermute | solution.py:226

commit v3 on v2

v3 whole, which is shorter than its diff:
```python
import functools

import jax
import jax.numpy as jnp
from jax import lax
from jax.experimental import pallas as pl
from jax.experimental.pallas import tpu as pltpu
from jax.sharding import PartitionSpec as P

F32, BF16 = jnp.float32, jnp.bfloat16
VMEM = pl.BlockSpec(memory_space=pltpu.VMEM)
HBM = pl.BlockSpec(memory_space=pltpu.HBM)
AXES = ("dp", "tensor")
LIMIT = 12 * 2**20


def split(x, terms):
    out = []
    for _ in range(terms):
        t = x.astype(BF16)
        out.append(t)
        x = x - t.astype(F32)
    return out


def stack(terms):
    return jnp.concatenate(terms, axis=0)


def dot(a, b, contract):
    return lax.dot_general(a, b, ((contract[:1], contract[1:]), ((), ())), preferred_element_type=F32)


def fold(x, rank):
    return functools.reduce(jnp.add, [x[i : i + rank] for i in range(0, x.shape[0], rank)])


def six_left(x):
    a, b, c = split(x, 3)
    return jnp.concatenate([a, a, b, a, b, c], axis=1)


def six_right(x):
    u, v, w = split(x, 3)
    return stack([u, v, u, w, v, u])


def walks(devices):
    bits = []
    bit = 2
    while bit < devices:
        bits.append(bit)
        bit *= 2
    half = len(bits) // 2
    return bits, bits[half:] + bits[:half][::-1]


def sides(devices):
    place = lax.axis_index("dp") * lax.axis_size("tensor") + lax.axis_index("tensor")
    first, second = (walk[0].bit_length() - 1 for walk in walks(devices))
    core = place & 1
    own = [(place >> first) & 1, (place >> second) & 1]
    mine = jnp.where(core == 0, own[0], own[1])
    theirs = jnp.where(core == 0, own[1], own[0])
    return (core, mine), (1 - core, theirs)


def order(devices):
    mine, theirs = sides(devices)
    return tuple(2 * side[0] + k for k in range(2) for side in (theirs, mine))


def copies_of(quarter, rows, g_hbm, e_hbm, g_to, e_to, sems):
    at = pl.ds(pl.multiple_of(quarter * rows, rows), rows)
    return (
        pltpu.make_async_copy(g_hbm.at[at], g_to, sems.at[0]),
        pltpu.make_async_copy(e_hbm.at[at], e_to, sems.at[1]),
    )


def products(q, m, mh_ref, ml_ref, at, outs):
    rows = m.shape[0]
    mh, ml = split(m, 2)
    mh_ref[at : at + rows] = mh
    ml_ref[at : at + rows] = ml
    p = fold(dot(q, mh, (1, 1)) + dot(q, ml, (1, 1)), outs[0].shape[0])
    width = outs[0].shape[1]
    for n, out in enumerate(outs):
        out[...] = p[:, n * width : (n + 1) * width]


def start(pairs):
    for pair in pairs:
        for copy in pair:
            copy.start()


def wait(pairs):
    for pair in pairs:
        for copy in pair:
            copy.wait()


def left_kernel(q_hbm, g_hbm, e_hbm, m_ref, mh_ref, ml_ref, e_ref, g_ref, send, keep, q_buf, g_buf, q_sem, sems, *, devices):
    rows = send.shape[2]
    q_copy = pltpu.make_async_copy(q_hbm, q_buf, q_sem)
    q_copy.start()
    copies = []
    for n, quarter in enumerate(order(devices)):
        at = pl.ds(n % 2 * rows, rows)
        to = (g_buf.at[at], m_ref.at[at]) if n < 2 else (g_ref.at[at], e_ref.at[at])
        copies.append(copies_of(quarter, rows, g_hbm, e_hbm, *to, sems.at[n]))
    start(copies[:3])
    q_copy.wait()
    factors = factors_of(q_buf, devices)
    for n, out in enumerate((send, keep)):
        wait(copies[n : n + 1])
        if n == 0:
            start(copies[3:])
        at = slice(n * rows, (n + 1) * rows)
        m = m_ref[at] + g_buf[at].astype(F32)
        m_ref[at] = m
        products(factors[n], m, mh_ref, ml_ref, at, out)
    wait(copies[2:])


def left_rest_kernel(q_ref, e_ref, g_ref, m_ref, mh_ref, ml_ref, send, keep, *, devices):
    rows = send.shape[2]
    factors = factors_of(q_ref, devices)
    for n, out in enumerate((send, keep)):
        at = slice(n * rows, (n + 1) * rows)
        m = e_ref[at] + g_ref[at].astype(F32)
        m_ref[at] = m
        products(factors[n], m, mh_ref, ml_ref, at, out)


def factors_of(q_ref, devices):
    half = q_ref.shape[0] // 2
    out = []
    for _, bit in sides(devices)[::-1]:
        out.append(stack(split(stack([q_ref[pl.ds(pl.multiple_of(at * half, half), half), :] for at in (1 - bit, bit)]), 3)))
    return out


def products(q, m, mh_ref, ml_ref, at, out):
    mh, ml = split(m, 2)
    mh_ref[at] = mh
    ml_ref[at] = ml
    half = out.shape[1]
    p = fold(dot(q, mh, (1, 1)) + dot(q, ml, (1, 1)), 2 * half)
    out[0] = p[:half]
    out[1] = p[half:]


def whole(own, other, bit):
    a, b = own[...], other[...]
    return stack([jnp.where(bit == 0, a, b), jnp.where(bit == 0, b, a)])


def square(p, rank):
    g = fold(dot(p, p, (1, 1)), rank)
    return g[:, :rank] + g[:, rank : 2 * rank] + g[:, 2 * rank :]


def terms_of(pieces):
    return jnp.concatenate([stack(split(x, 3)) for x in pieces], axis=1)


def pair_up(refs, owners, devices):
    return [whole(refs[2 * n], refs[2 * n + 1], sides(devices)[owner][1]) for n, owner in enumerate(owners)]


def right_kernel(*refs, owners, start, first, devices):
    pieces, (mh_ref, ml_ref, *rest) = refs[: 2 * len(owners)], refs[2 * len(owners) :]
    rows = pieces[0].shape[1]
    rank = 2 * pieces[0].shape[0]
    p = terms_of(pair_up(pieces, owners, devices))
    at = slice(start * rows, (start + len(owners)) * rows)
    t = fold(dot(p, mh_ref[at], (1, 0)) + dot(p, ml_ref[at], (1, 0)), rank)
    if first:
        t_ref, gram_ref = rest
        t_ref[...] = t
        gram_ref[...] = square(p, rank)
    else:
        before, t_ref = rest
        t_ref[...] = before[...] + t


def eliminate(a, pivots):
    rank = a.shape[0]
    row = lax.broadcasted_iota(jnp.int32, (rank, 1), 0)
    for k in pivots:
        line = a[k : k + 1, :] / a[k : k + 1, k : k + 1]
        a = a - jnp.where(row > k, a[:, k : k + 1], 0.0) * line
    return a


def factor_kernel(gram_ref, *refs, devices):
    pieces, (state_ref,) = refs[:4], refs[4:]
    rank = gram_ref.shape[0]
    gram = gram_ref[...] + square(terms_of(pair_up(pieces, (1, 0), devices)), rank)
    row = lax.broadcasted_iota(jnp.int32, (rank, 128), 0)
    lane = lax.broadcasted_iota(jnp.int32, (rank, 128), 1)
    eye = (lane == row + rank).astype(F32)
    state_ref[...] = eliminate(jnp.concatenate([gram, eye[:, rank:]], axis=1), range(rank // 2))


def inverse_kernel(state_ref, inv_ref):
    rank = state_ref.shape[0]
    a = eliminate(state_ref[...], range(rank // 2, rank - 1))
    row = lax.broadcasted_iota(jnp.int32, a.shape, 0)
    lane = lax.broadcasted_iota(jnp.int32, a.shape, 1)
    pivots = jnp.sum(jnp.where(row == lane, a, 0.0), axis=1, keepdims=True)
    inv_ref[...] = a[:, rank : 2 * rank] / jnp.sqrt(pivots)


def hat_kernel(inv_ref, *refs, devices):
    hat_ref, rows_ref = refs[8:]
    rows = refs[0].shape[1]
    pieces = pair_up(refs[:8], (1, 0, 1, 0), devices)
    inverse = inv_ref[...]
    left, back = six_left(inverse), six_left(inverse.T)
    for n, quarter in enumerate(order(devices)):
        hat = dot(left, six_right(pieces[n]), (1, 0))
        hat_ref[:, pl.ds(pl.multiple_of(quarter * rows, rows), rows)] = hat
        u, v = split(dot(back, six_right(hat), (1, 0)), 2)
        rows_ref[n * rows : (n + 1) * rows, :] = stack([u, v, u, v]).T


def error_kernel(t0_ref, t1_ref, inv_ref, rows_ref, m_ref, m2_ref, out_hbm, q_hbm, buf, q_buf, sems, q_sem, *, replicas, block, devices):
    t = (t0_ref[...] + t1_ref[...]) / replicas
    u, v = split(t, 2)
    terms = stack([u, u, v, v])
    quarters = order(devices)
    rows = buf.shape[0] // 4
    copies = []
    for n in range(buf.shape[0] // block):
        at = n * block
        quarter, inside = at // rows, at % rows
        source, shift = (m_ref, 0) if quarter < 2 else (m2_ref, 2 * rows)
        buf[at : at + block] = source[at - shift : at - shift + block] - dot(rows_ref[at : at + block], terms, (1, 0))
        to = pl.ds(pl.multiple_of(quarters[quarter] * rows + inside, block), block)
        copy = pltpu.make_async_copy(buf.at[pl.ds(at, block)], out_hbm.at[to], sems.at[n])
        copy.start()
        copies.append(copy)
    q_buf[...] = dot(six_left(inv_ref[...]), six_right(t), (1, 0))
    copies.append(pltpu.make_async_copy(q_buf, q_hbm, q_sem))
    copies[-1].start()
    for copy in copies:
        copy.wait()


def shards(gradient, error_buffer, q_given):
    replicas, tensors = lax.axis_size("dp"), lax.axis_size("tensor")
    devices = replicas * tensors
    depth, columns = gradient.shape[1:]
    rank = q_given.shape[1]
    rows = depth // 4

    def call(kernel, name, flops, **kw):
        made = pl.pallas_call(
            kernel,
            name=name,
            compiler_params=pltpu.CompilerParams(vmem_limit_bytes=LIMIT),
            cost_estimate=pl.CostEstimate(flops=flops, bytes_accessed=0, transcendentals=0),
            **kw,
        )
        spaces = [pltpu.HBM if spec is HBM else pltpu.VMEM for spec in kw["in_specs"]]
        return lambda *args: made(*(pltpu.with_memory_space_constraint(x, space) for x, space in zip(args, spaces, strict=True)))

    piece = pltpu.VMEM((2, rank // 2, rows), F32)
    small = pltpu.VMEM((rank, rank), F32)
    wide = pltpu.VMEM((rank, columns), F32)
    work = 6 * depth * columns * rank

    merged = tuple(pltpu.VMEM((2 * rows, columns), kind) for kind in (F32, BF16, BF16))

    m, mh, ml, e2, g2, send_a, keep_a = call(
        functools.partial(left_kernel, devices=devices),
        "left_products",
        work,
        out_shape=merged + merged[:2] + (piece,) * 2,
        in_specs=[HBM] * 3,
        out_specs=(VMEM,) * 7,
        scratch_shapes=[
            pltpu.VMEM((rank, columns), F32),
            pltpu.VMEM((2 * rows, columns), BF16),
            pltpu.SemaphoreType.DMA(()),
            pltpu.SemaphoreType.DMA((4, 2)),
        ],
    )(q_given.T, gradient[0], error_buffer[0])
    m2, mh2, ml2, send_b, keep_b = call(
        functools.partial(left_rest_kernel, devices=devices),
        "left_products_rest",
        work,
        out_shape=merged + (piece,) * 2,
        in_specs=[VMEM] * 3,
        out_specs=(VMEM,) * 5,
    )(q_given.T, e2, g2)

    def swap(x, bit, bit1=None):
        choice = (bit, bit if bit1 is None else bit1)
        return lax.ppermute(x, AXES, [(i, i ^ choice[i & 1]) for i in range(devices)])

    walk = list(zip(*walks(devices), strict=True))
    sums = [keep + swap(send, 1) for send, keep in ((send_a, keep_a), (send_b, keep_b))]
    arrived = [swap(x[0], *walk[0]) for x in sums]
    own = [x[1] + y for x, y in zip(sums, arrived, strict=True)]
    for bits in walk[1:]:
        arrived = [swap(x, *bits) for x in own]
        own = [x + y for x, y in zip(own, arrived, strict=True)]
    other = [swap(x, *walk[0]) for x in own]
    mine = list(zip(own, other, strict=True))
    theirs = [tuple(swap(x, 1) for x in pair) for pair in mine]

    def right(name, owners, start, pieces, *args):
        first = len(args) == 2
        return call(
            functools.partial(right_kernel, owners=owners, start=start, first=first, devices=devices),
            name,
            work,
            out_shape=(wide, small) if first else wide,
            in_specs=[VMEM] * (len(pieces) + len(args)),
            out_specs=(VMEM, VMEM) if first else VMEM,
        )(*pieces, *args)

    t, gram = right("right_products", (1, 0), 0, theirs[0] + mine[0], mh, ml)
    t = right("right_products_own", (0,), 1, mine[1], mh2, ml2, t)
    t = right("right_products_other", (1,), 0, theirs[1], mh2, ml2, t)

    state = call(
        functools.partial(factor_kernel, devices=devices),
        "factor_first_half",
        work,
        out_shape=pltpu.VMEM((rank, 128), F32),
        in_specs=[VMEM] * 5,
        out_specs=VMEM,
    )(gram, *theirs[1], *mine[1])
    inverse = call(inverse_kernel, "factor_second_half", work, out_shape=small, in_specs=[VMEM], out_specs=VMEM)(state)
    hat, hat_rows = call(
        functools.partial(hat_kernel, devices=devices),
        "left_factor",
        work,
        out_shape=(jax.ShapeDtypeStruct((rank, depth), F32), pltpu.VMEM((depth, 4 * rank), BF16)),
        in_specs=[VMEM] * 9,
        out_specs=(VMEM, VMEM),
    )(inverse, *theirs[0], *mine[0], *theirs[1], *mine[1])

    bits = [bit for bit in walks(devices)[0] if bit >= tensors]
    beside = [state, inverse]
    got = swap(t, bits[0])
    for n, bit in enumerate(bits[1:]):
        t = t + got
        if n < len(beside):
            t, _ = lax.optimization_barrier((t, beside[n]))
        got = swap(t, bit)

    block = rows // 3
    error, q_new = call(
        functools.partial(error_kernel, replicas=replicas, block=block, devices=devices),
        "new_error",
        work,
        out_shape=(pltpu.HBM((depth, columns), F32), pltpu.HBM((rank, columns), F32)),
        in_specs=[VMEM] * 6,
        out_specs=(HBM, HBM),
        scratch_shapes=[
            pltpu.VMEM((depth, columns), F32),
            pltpu.VMEM((rank, columns), F32),
            pltpu.SemaphoreType.DMA((depth // block,)),
            pltpu.SemaphoreType.DMA(()),
        ],
    )(t, got, inverse, hat_rows, m, m2)
    return (error[None], hat.T, q_new.T)


def solution(mesh):
    placed = (P("dp", None, "tensor"), P("dp", None, "tensor"), P("tensor", None))
    return jax.shard_map(
        shards,
        mesh=mesh,
        in_specs=placed,
        out_specs=(P("dp", None, "tensor"), P(), P("tensor", None)),
        check_vma=False,
    )
```

time: 55.2 us -> 49.9 us (0.904)
  Pallas kernels: 16.8 us -> 12.9 us
  waiting for transfers between devices: 11.7 us -> 9.37 us
  starting transfers between devices: 25.7 us -> 26.6 us
    pallas_call x7 -> x9, Pallas kernels: 16.8 us -> 12.9 us  [call(): made(*(pltpu.with_memory_space_constraint(x, space) for x, space in zip(a...]
    ppermute x19, waiting for transfers between devices: 11.7 us -> 9.37 us  [swap(): lax.ppermute(x, AXES, [(i, i ^ choice[i & 1]) for i in range(devices)])]
    ppermute x19, starting transfers between devices: 25.7 us -> 26.6 us  [swap(): lax.ppermute(x, AXES, [(i, i ^ choice[i & 1]) for i in range(devices)])]
  transfers between devices with their start and end apart: 19 -> 19, of which waited for: 11 -> 11; matrix products, arithmetic and copies ran while one was open for 0% -> 0% of each run, Pallas kernels for 9% -> 13%
where the time goes in v3:
time: 49.9 us; the launch traced here: 49.8 us
  starting transfers between devices  26.6 us (53%)
  Pallas kernels  12.9 us (26%)
  waiting for transfers between devices  9.37 us (19%)
  between operations  0.74 us (1%)
    ppermute x19, starting transfers between devices, swap(): lax.ppermute(x, AXES, [(i, i ^ choice[i & 1]) for i in range(devices)])  26.6 us
    pallas_call x9, Pallas kernels, call(): made(*(pltpu.with_memory_space_constraint(x, space) for x, space in zip(a...  12.9 us
    ppermute x19, waiting for transfers between devices, swap(): lax.ppermute(x, AXES, [(i, i ^ choice[i & 1]) for i in range(devices)])  9.37 us
  transfers between devices with their start and end apart: 19, of which 11 were waited for; matrix products, arithmetic and copies ran while one was open for 0% of the time, Pallas kernels for 13%

profile of v3, /device:TPU:0, one launch (start us, length us, event | category | flops | bytes accessed | tf_op | source)
XLA Modules:
  0.0 49.8 jit_solution(17889187249149831420)
XLA Ops:
  0.6 0.0 copy-start
  0.6 3.4 %left_products.1 = (f32[2304,256]{1,0:T(8,128)S(1)}, bf16[2304,256]{1,0:T(8,128)(2,1)S(1)}, bf16[2304,256]{1,0:T(8,128)(2,1)S(1)}, f32[2304,256]{1,0:T(8,128)S(1...) custom-call(f32[32,256]{1,0:T(8,128)} %bitcast.18, ...), custom_call_target="tpu_custom_call" | custom-call | flops 226492416 | tf_op jit(solution)/shard_map/left_products/pallas_call | solution.py:269
  4.0 0.5 %collective-permute-start.8 = (f32[2,16,1152]{2,1,0:T(8,128)S(1)}, f32[2,16,1152]{2,1,0:T(8,128)S(1)}, u32[]{:S(2)}, u32[]{:S(2)}) collective-permute-start(f32[2,16,1152]{2,1,0:T(8,128)S(1)} %get-tuple-element.30), channel_id=1, source_target_pairs={{0,1},{1,0},{2,3},{3,2},{4,5},{5,4},{6,7},{7,6},{8,9},{9,8},{10,11... | collective-permute-start | bytes 442376 | tf_op jit(solution)/shard_map/ppermute | solution.py:303
  4.5 0.9 %left_products_rest.1 = (f32[2304,256]{1,0:T(8,128)S(1)}, bf16[2304,256]{1,0:T(8,128)(2,1)S(1)}, bf16[2304,256]{1,0:T(8,128)(2,1)S(1)}, f32[2,16,1152]{2,1,0:T(8,128)S(1)}, f32[2,16,1152]{2,1,0:T(8,128)S(1)}) custom-call(f32[32,256]{1,0:T(8,128)S(1)} %bitcast.19, f32[2304,256]{1,0:T(8,128)S(1)} %get-tuple-element.23.e_ref, ...), custom_call_target="tpu_custom_call" | custom-call | flops 226492416 | tf_op jit(solution)/shard_map/left_products_rest/pallas_call | solution.py:269
  5.4 0.1 collective-permute-start
  5.5 0.0 collective-permute-done.8
  5.6 3.0 %collective-permute-start.9 = (f32[16,1152]{1,0:T(8,128)S(1)}, f32[16,1152]{1,0:T(8,128)S(1)}, u32[]{:S(2)}, u32[]{:S(2)}) collective-permute-start(f32[16,1152]{1,0:T(8,128)S(1)} %slice_bitcast_fusion), channel_id=1, source_target_pairs={{0,2},{1,9},{2,0},{3,11},{4,6},{5,13},{6,4},{7,15},{8,10},{9,1},{1... | collective-permute-start | bytes 221192 | tf_op jit(solution)/shard_map/ppermute | solution.py:303
  8.6 0.0 collective-permute-done
  8.6 1.0 %collective-permute-start.1 = (f32[16,1152]{1,0:T(8,128)S(1)}, f32[16,1152]{1,0:T(8,128)S(1)}, u32[]{:S(2)}, u32[]{:S(2)}) collective-permute-start(f32[16,1152]{1,0:T(8,128)S(1)} %slice_bitcast_fusion.2), channel_id=1, source_target_pairs={{0,2},{1,9},{2,0},{3,11},{4,6},{5,13},{6,4},{7,15},{8,10},{9,1},{1... | collective-permute-start | bytes 221192 | tf_op jit(solution)/shard_map/ppermute | solution.py:303
  9.6 1.3 %collective-permute-done.9 = f32[16,1152]{1,0:T(8,128)S(1)} collective-permute-done((f32[16,1152]{1,0:T(8,128)S(1)}, f32[16,1152]{1,0:T(8,128)S(1)}, u32[]{:S(2)}, u32[]{:S(2)}) %collective-permute-start.9) | collective-permute-done | bytes 73760 | tf_op jit(solution)/shard_map/ppermute | solution.py:303
  10.9 2.1 %collective-permute-start.10 = (f32[16,1152]{1,0:T(8,128)S(1)}, f32[16,1152]{1,0:T(8,128)S(1)}, u32[]{:S(2)}, u32[]{:S(2)}) collective-permute-start(f32[16,1152]{1,0:T(8,128)S(1)} %fusion), channel_id=1, source_target_pairs={{0,4},{1,17},{2,6},{3,19},{4,0},{5,21},{6,2},{7,23},{8,12},{9,25},... | collective-permute-start | bytes 221192 | tf_op jit(solution)/shard_map/ppermute | solution.py:303
  13.0 0.0 collective-permute-done.1
  13.0 1.6 %collective-permute-start.2 = (f32[16,1152]{1,0:T(8,128)S(1)}, f32[16,1152]{1,0:T(8,128)S(1)}, u32[]{:S(2)}, u32[]{:S(2)}) collective-permute-start(f32[16,1152]{1,0:T(8,128)S(1)} %fusion.1), channel_id=1, source_target_pairs={{0,4},{1,17},{2,6},{3,19},{4,0},{5,21},{6,2},{7,23},{8,12},{9,25},... | collective-permute-start | bytes 221192 | tf_op jit(solution)/shard_map/ppermute | solution.py:303
  14.6 0.7 %collective-permute-done.10 = f32[16,1152]{1,0:T(8,128)S(1)} collective-permute-done((f32[16,1152]{1,0:T(8,128)S(1)}, f32[16,1152]{1,0:T(8,128)S(1)}, u32[]{:S(2)}, u32[]{:S(2)}) %collective-permute-start.10) | collective-permute-done | bytes 73760 | tf_op jit(solution)/shard_map/ppermute | solution.py:303
  15.4 2.1 %collective-permute-start.11 = (f32[16,1152]{1,0:T(8,128)S(1)}, f32[16,1152]{1,0:T(8,128)S(1)}, u32[]{:S(2)}, u32[]{:S(2)}) collective-permute-start(f32[16,1152]{1,0:T(8,128)S(1)} %add.43), channel_id=1, source_target_pairs={{0,8},{1,5},{2,10},{3,7},{4,12},{5,1},{6,14},{7,3},{8,0},{9,13},{1... | collective-permute-start | bytes 221192 | tf_op jit(solution)/shard_map/ppermute | solution.py:303
  17.5 0.1 collective-permute-done.2
  17.6 1.6 %collective-permute-start.3 = (f32[16,1152]{1,0:T(8,128)S(1)}, f32[16,1152]{1,0:T(8,128)S(1)}, u32[]{:S(2)}, u32[]{:S(2)}) collective-permute-start(f32[16,1152]{1,0:T(8,128)S(1)} %add.38), channel_id=1, source_target_pairs={{0,8},{1,5},{2,10},{3,7},{4,12},{5,1},{6,14},{7,3},{8,0},{9,13},{1... | collective-permute-start | bytes 221192 | tf_op jit(solution)/shard_map/ppermute | solution.py:303
  19.2 0.6 %collective-permute-done.11 = f32[16,1152]{1,0:T(8,128)S(1)} collective-permute-done((f32[16,1152]{1,0:T(8,128)S(1)}, f32[16,1152]{1,0:T(8,128)S(1)}, u32[]{:S(2)}, u32[]{:S(2)}) %collective-permute-start.11) | collective-permute-done | bytes 73760 | tf_op jit(solution)/shard_map/ppermute | solution.py:303
  19.9 3.1 %collective-permute-start.12 = (f32[16,1152]{1,0:T(8,128)S(1)}, f32[16,1152]{1,0:T(8,128)S(1)}, u32[]{:S(2)}, u32[]{:S(2)}) collective-permute-start(f32[16,1152]{1,0:T(8,128)S(1)} %add.44), channel_id=1, source_target_pairs={{0,16},{1,3},{2,18},{3,1},{4,20},{5,7},{6,22},{7,5},{8,24},{9,11},... | collective-permute-start | bytes 221192 | tf_op jit(solution)/shard_map/ppermute | solution.py:303
  23.0 0.0 collective-permute-done.3
  23.0 1.8 %collective-permute-start.4 = (f32[16,1152]{1,0:T(8,128)S(1)}, f32[16,1152]{1,0:T(8,128)S(1)}, u32[]{:S(2)}, u32[]{:S(2)}) collective-permute-start(f32[16,1152]{1,0:T(8,128)S(1)} %add.39), channel_id=1, source_target_pairs={{0,16},{1,3},{2,18},{3,1},{4,20},{5,7},{6,22},{7,5},{8,24},{9,11},... | collective-permute-start | bytes 221192 | tf_op jit(solution)/shard_map/ppermute | solution.py:303
  24.8 0.6 %collective-permute-done.12 = f32[16,1152]{1,0:T(8,128)S(1)} collective-permute-done((f32[16,1152]{1,0:T(8,128)S(1)}, f32[16,1152]{1,0:T(8,128)S(1)}, u32[]{:S(2)}, u32[]{:S(2)}) %collective-permute-start.12) | collective-permute-done | bytes 73760 | tf_op jit(solution)/shard_map/ppermute | solution.py:303
  25.4 1.9 %collective-permute-start.14 = (f32[16,1152]{1,0:T(8,128)S(1)}, f32[16,1152]{1,0:T(8,128)S(1)}, u32[]{:S(2)}, u32[]{:S(2)}) collective-permute-start(f32[16,1152]{1,0:T(8,128)S(1)} %add.45.refs_2_), channel_id=1, source_target_pairs={{0,2},{1,9},{2,0},{3,11},{4,6},{5,13},{6,4},{7,15},{8,10},{9,1},{1... | collective-permute-start | bytes 221192 | tf_op jit(solution)/shard_map/ppermute | solution.py:303
  27.3 1.0 %collective-permute-done.4 = f32[16,1152]{1,0:T(8,128)S(1)} collective-permute-done((f32[16,1152]{1,0:T(8,128)S(1)}, f32[16,1152]{1,0:T(8,128)S(1)}, u32[]{:S(2)}, u32[]{:S(2)}) %collective-permute-start.4) | collective-permute-done | bytes 73760 | tf_op jit(solution)/shard_map/ppermute | solution.py:303
  28.3 1.6 %collective-permute-start.6 = (f32[16,1152]{1,0:T(8,128)S(1)}, f32[16,1152]{1,0:T(8,128)S(1)}, u32[]{:S(2)}, u32[]{:S(2)}) collective-permute-start(f32[16,1152]{1,0:T(8,128)S(1)} %add.40.refs_0_.refs_2_.refs_6_), channel_id=1, source_target_pairs={{0,2},{1,9},{2,0},{3,11},{4,6},{5,13},{6,4},{7,15},{8,10},{9,1},{1... | collective-permute-start | bytes 221192 | tf_op jit(solution)/shard_map/ppermute | solution.py:303
  29.9 0.0 collective-permute-start.13
  29.9 0.0 collective-permute-done.14.refs_3_
  29.9 0.5 %collective-permute-start.15 = (f32[16,1152]{1,0:T(8,128)S(1)}, f32[16,1152]{1,0:T(8,128)S(1)}, u32[]{:S(2)}, u32[]{:S(2)}) collective-permute-start(f32[16,1152]{1,0:T(8,128)S(1)} %collective-permute-done.14.refs_3_), channel_id=1, source_target_pairs={{0,1},{1,0},{2,3},{3,2},{4,5},{5,4},{6,7},{7,6},{8,9},{9,8},{10,11... | collective-permute-start | bytes 221192 | tf_op jit(solution)/shard_map/ppermute | solution.py:303
  30.4 0.0 collective-permute-start.5
  30.4 2.3 %collective-permute-done.6.refs_1_.refs_3_.refs_7_ = f32[16,1152]{1,0:T(8,128)S(1)} collective-permute-done((f32[16,1152]{1,0:T(8,128)S(1)}, f32[16,1152]{1,0:T(8,128)S(1)}, u32[]{:S(2)}, u32[]{:S(2)}) %collective-permute-start.6) | collective-permute-done | bytes 73760 | tf_op jit(solution)/shard_map/ppermute | solution.py:303
  32.7 0.0 collective-permute-start.7
  32.7 0.0 collective-permute-done.13.refs_0_
  32.7 0.0 collective-permute-done.15.refs_1_
  32.7 0.7 %right_products.1 = (f32[32,256]{1,0:T(8,128)S(1)}, f32[32,32]{1,0:T(8,128)S(1)}) custom-call(f32[16,1152]{1,0:T(8,128)S(1)} %collective-permute-done.13.refs_0_, f32[16,1152]{1,0:T(8,128)S(1)} %collective-permute-done.15.refs_1_, f32[16,1152]{1,0:T(8,128)S(1)} %add.45.refs_2_, f32[16,1152]{1,0:T(8,128)S(1)} %collective-permute-done.14.refs_3_, ...), custom_call_target="tpu_custom_call" | custom-call | flops 226492416 | tf_op jit(solution)/shard_map/right_products/pallas_call | solution.py:269
  33.4 0.3 right_products_own.1.refs_4_
  33.7 0.0 collective-permute-done.5.refs_0_.refs_4_
  33.8 0.2 collective-permute-done.7.refs_1_.refs_5_
  34.0 0.3 right_products_other.1
  34.3 1.6 %collective-permute-start.16 = (f32[32,256]{1,0:T(8,128)S(1)}, f32[32,256]{1,0:T(8,128)S(1)}, u32[]{:S(2)}, u32[]{:S(2)}) collective-permute-start(f32[32,256]{1,0:T(8,128)S(1)} %right_products_other.1), channel_id=1, source_target_pairs={{0,4},{1,5},{2,6},{3,7},{4,0},{5,1},{6,2},{7,3},{8,12},{9,13},{10,... | collective-permute-start | bytes 98312 | tf_op jit(solution)/shard_map/ppermute | solution.py:303
  35.9 1.7 %factor_first_half.1.state_ref = f32[32,128]{1,0:T(8,128)S(1)} custom-call(f32[32,32]{1,0:T(8,128)S(1)} %get-tuple-element.34.gram_ref, f32[16,1152]{1,0:T(8,128)S(1)} %collective-permute-done.5.refs_0_.refs_4_, f32[16,1152]{1,0:T(8,128)S(1)} %collective-permute-done.7.refs_1_.refs_5_, f32[16,1152]{1,0:T(8,128)S(1)} %add.40.refs_0_.refs_2_.refs_6_, ...), custom_call_target="tpu_custom_call" | custom-call | flops 226492416 | tf_op jit(solution)/shard_map/factor_first_half/pallas_call | solution.py:269
  37.5 0.7 %collective-permute-done.16 = f32[32,256]{1,0:T(8,128)S(1)} collective-permute-done((f32[32,256]{1,0:T(8,128)S(1)}, f32[32,256]{1,0:T(8,128)S(1)}, u32[]{:S(2)}, u32[]{:S(2)}) %collective-permute-start.16) | collective-permute-done | bytes 32800 | tf_op jit(solution)/shard_map/ppermute | solution.py:303
  38.3 2.2 %collective-permute-start.17 = (f32[32,256]{1,0:T(8,128)S(1)}, f32[32,256]{1,0:T(8,128)S(1)}, u32[]{:S(2)}, u32[]{:S(2)}) collective-permute-start(f32[32,256]{1,0:T(8,128)S(1)} %add.46), channel_id=1, source_target_pairs={{0,8},{1,9},{2,10},{3,11},{4,12},{5,13},{6,14},{7,15},{8,0},{9,1},... | collective-permute-start | bytes 98312 | tf_op jit(solution)/shard_map/ppermute | solution.py:303
  40.5 1.3 %factor_second_half.1.inv_ref = f32[32,32]{1,0:T(8,128)S(1)} custom-call(f32[32,128]{1,0:T(8,128)S(1)} %factor_first_half.1.state_ref), custom_call_target="tpu_custom_call" | custom-call | flops 226492416 | tf_op jit(solution)/shard_map/factor_second_half/pallas_call | solution.py:269
  41.9 0.5 %collective-permute-done.17 = f32[32,256]{1,0:T(8,128)S(1)} collective-permute-done((f32[32,256]{1,0:T(8,128)S(1)}, f32[32,256]{1,0:T(8,128)S(1)}, u32[]{:S(2)}, u32[]{:S(2)}) %collective-permute-start.17) | collective-permute-done | bytes 32800 | tf_op jit(solution)/shard_map/ppermute | solution.py:303
  42.4 1.9 %collective-permute-start.18 = (f32[32,256]{1,0:T(8,128)S(1)}, f32[32,256]{1,0:T(8,128)S(1)}, u32[]{:S(2)}, u32[]{:S(2)}) collective-permute-start(f32[32,256]{1,0:T(8,128)S(1)} %add.47.t0_ref), channel_id=1, source_target_pairs={{0,16},{1,17},{2,18},{3,19},{4,20},{5,21},{6,22},{7,23},{8,24},{9,... | collective-permute-start | bytes 98312 | tf_op jit(solution)/shard_map/ppermute | solution.py:303
  44.3 1.8 %left_factor.1 = (f32[32,4608]{1,0:T(8,128)}, bf16[4608,128]{1,0:T(8,128)(2,1)S(1)}) custom-call(f32[32,32]{1,0:T(8,128)S(1)} %factor_second_half.1.inv_ref, f32[16,1152]{1,0:T(8,128)S(1)} %collective-permute-done.13.refs_0_, f32[16,1152]{1,0:T(8,128)S(1)} %collective-permute-done.15.refs_1_, f32[16,1152]{1,0:T(8,128)S(1)} %add.45.refs_2_, ...), custom_call_target="tpu_custom_call" | custom-call | flops 226492416 | tf_op jit(solution)/shard_map/left_factor/pallas_call | solution.py:269
  46.2 1.1 %collective-permute-done.18.t1_ref = f32[32,256]{1,0:T(8,128)S(1)} collective-permute-done((f32[32,256]{1,0:T(8,128)S(1)}, f32[32,256]{1,0:T(8,128)S(1)}, u32[]{:S(2)}, u32[]{:S(2)}) %collective-permute-start.18) | collective-permute-done | bytes 32800 | tf_op jit(solution)/shard_map/ppermute | solution.py:303
  47.2 2.5 %new_error.1 = (f32[4608,256]{1,0:T(8,128)}, f32[32,256]{1,0:T(8,128)}) custom-call(f32[32,256]{1,0:T(8,128)S(1)} %add.47.t0_ref, f32[32,256]{1,0:T(8,128)S(1)} %collective-permute-done.18.t1_ref, f32[32,32]{1,0:T(8,128)S(1)} %factor_second_half.1.inv_ref, bf16[4608,128]{1,0:T(8,128)(2,1)S(1)} %get-tuple-element.37.rows_ref, ...), custom_call_target="tpu_custom_call" | custom-call | flops 226492416 | tf_op jit(solution)/shard_map/new_error/pallas_call | solution.py:269
  (15 shorter events, 0.1 us)
Async XLA Ops:
  0.6 3.9 %copy-start = (f32[256,32]{0,1:T(8,128)S(1)}, f32[256,32]{0,1:T(8,128)}, u32[]{:S(2)}) copy-start(f32[256,32]{0,1:T(8,128)} %param.5) | copy-start | bytes 98308
  4.0 1.5 %collective-permute-start.8 = (f32[2,16,1152]{2,1,0:T(8,128)S(1)}, f32[2,16,1152]{2,1,0:T(8,128)S(1)}, u32[]{:S(2)}, u32[]{:S(2)}) collective-permute-start(f32[2,16,1152]{2,1,0:T(8,128)S(1)} %get-tuple-element.30), channel_id=1, source_target_pairs={{0,1},{1,0},{2,3},{3,2},{4,5},{5,4},{6,7},{7,6},{8,9},{9,8},{10,11... | collective-permute-start | bytes 442376 | tf_op jit(solution)/shard_map/ppermute | solution.py:303
  5.4 3.1 %collective-permute-start = (f32[2,16,1152]{2,1,0:T(8,128)S(1)}, f32[2,16,1152]{2,1,0:T(8,128)S(1)}, u32[]{:S(2)}, u32[]{:S(2)}) collective-permute-start(f32[2,16,1152]{2,1,0:T(8,128)S(1)} %get-tuple-element.26), channel_id=1, source_target_pairs={{0,1},{1,0},{2,3},{3,2},{4,5},{5,4},{6,7},{7,6},{8,9},{9,8},{10,11... | collective-permute-start | bytes 442376 | tf_op jit(solution)/shard_map/ppermute | solution.py:303
  5.6 5.3 %collective-permute-start.9 = (f32[16,1152]{1,0:T(8,128)S(1)}, f32[16,1152]{1,0:T(8,128)S(1)}, u32[]{:S(2)}, u32[]{:S(2)}) collective-permute-start(f32[16,1152]{1,0:T(8,128)S(1)} %slice_bitcast_fusion), channel_id=1, source_target_pairs={{0,2},{1,9},{2,0},{3,11},{4,6},{5,13},{6,4},{7,15},{8,10},{9,1},{1... | collective-permute-start | bytes 221192 | tf_op jit(solution)/shard_map/ppermute | solution.py:303
  8.6 4.4 %collective-permute-start.1 = (f32[16,1152]{1,0:T(8,128)S(1)}, f32[16,1152]{1,0:T(8,128)S(1)}, u32[]{:S(2)}, u32[]{:S(2)}) collective-permute-start(f32[16,1152]{1,0:T(8,128)S(1)} %slice_bitcast_fusion.2), channel_id=1, source_target_pairs={{0,2},{1,9},{2,0},{3,11},{4,6},{5,13},{6,4},{7,15},{8,10},{9,1},{1... | collective-permute-start | bytes 221192 | tf_op jit(solution)/shard_map/ppermute | solution.py:303
  10.9 4.4 %collective-permute-start.10 = (f32[16,1152]{1,0:T(8,128)S(1)}, f32[16,1152]{1,0:T(8,128)S(1)}, u32[]{:S(2)}, u32[]{:S(2)}) collective-permute-start(f32[16,1152]{1,0:T(8,128)S(1)} %fusion), channel_id=1, source_target_pairs={{0,4},{1,17},{2,6},{3,19},{4,0},{5,21},{6,2},{7,23},{8,12},{9,25},... | collective-permute-start | bytes 221192 | tf_op jit(solution)/shard_map/ppermute | solution.py:303
  13.0 4.6 %collective-permute-start.2 = (f32[16,1152]{1,0:T(8,128)S(1)}, f32[16,1152]{1,0:T(8,128)S(1)}, u32[]{:S(2)}, u32[]{:S(2)}) collective-permute-start(f32[16,1152]{1,0:T(8,128)S(1)} %fusion.1), channel_id=1, source_target_pairs={{0,4},{1,17},{2,6},{3,19},{4,0},{5,21},{6,2},{7,23},{8,12},{9,25},... | collective-permute-start | bytes 221192 | tf_op jit(solution)/shard_map/ppermute | solution.py:303
  15.4 4.5 %collective-permute-start.11 = (f32[16,1152]{1,0:T(8,128)S(1)}, f32[16,1152]{1,0:T(8,128)S(1)}, u32[]{:S(2)}, u32[]{:S(2)}) collective-permute-start(f32[16,1152]{1,0:T(8,128)S(1)} %add.43), channel_id=1, source_target_pairs={{0,8},{1,5},{2,10},{3,7},{4,12},{5,1},{6,14},{7,3},{8,0},{9,13},{1... | collective-permute-start | bytes 221192 | tf_op jit(solution)/shard_map/ppermute | solution.py:303
  17.6 5.3 %collective-permute-start.3 = (f32[16,1152]{1,0:T(8,128)S(1)}, f32[16,1152]{1,0:T(8,128)S(1)}, u32[]{:S(2)}, u32[]{:S(2)}) collective-permute-start(f32[16,1152]{1,0:T(8,128)S(1)} %add.38), channel_id=1, source_target_pairs={{0,8},{1,5},{2,10},{3,7},{4,12},{5,1},{6,14},{7,3},{8,0},{9,13},{1... | collective-permute-start | bytes 221192 | tf_op jit(solution)/shard_map/ppermute | solution.py:303
  19.9 5.5 %collective-permute-start.12 = (f32[16,1152]{1,0:T(8,128)S(1)}, f32[16,1152]{1,0:T(8,128)S(1)}, u32[]{:S(2)}, u32[]{:S(2)}) collective-permute-start(f32[16,1152]{1,0:T(8,128)S(1)} %add.44), channel_id=1, source_target_pairs={{0,16},{1,3},{2,18},{3,1},{4,20},{5,7},{6,22},{7,5},{8,24},{9,11},... | collective-permute-start | bytes 221192 | tf_op jit(solution)/shard_map/ppermute | solution.py:303
  23.0 5.3 %collective-permute-start.4 = (f32[16,1152]{1,0:T(8,128)S(1)}, f32[16,1152]{1,0:T(8,128)S(1)}, u32[]{:S(2)}, u32[]{:S(2)}) collective-permute-start(f32[16,1152]{1,0:T(8,128)S(1)} %add.39), channel_id=1, source_target_pairs={{0,16},{1,3},{2,18},{3,1},{4,20},{5,7},{6,22},{7,5},{8,24},{9,11},... | collective-permute-start | bytes 221192 | tf_op jit(solution)/shard_map/ppermute | solution.py:303
  25.4 4.5 %collective-permute-start.14 = (f32[16,1152]{1,0:T(8,128)S(1)}, f32[16,1152]{1,0:T(8,128)S(1)}, u32[]{:S(2)}, u32[]{:S(2)}) collective-permute-start(f32[16,1152]{1,0:T(8,128)S(1)} %add.45.refs_2_), channel_id=1, source_target_pairs={{0,2},{1,9},{2,0},{3,11},{4,6},{5,13},{6,4},{7,15},{8,10},{9,1},{1... | collective-permute-start | bytes 221192 | tf_op jit(solution)/shard_map/ppermute | solution.py:303
  28.3 4.4 %collective-permute-start.6 = (f32[16,1152]{1,0:T(8,128)S(1)}, f32[16,1152]{1,0:T(8,128)S(1)}, u32[]{:S(2)}, u32[]{:S(2)}) collective-permute-start(f32[16,1152]{1,0:T(8,128)S(1)} %add.40.refs_0_.refs_2_.refs_6_), channel_id=1, source_target_pairs={{0,2},{1,9},{2,0},{3,11},{4,6},{5,13},{6,4},{7,15},{8,10},{9,1},{1... | collective-permute-start | bytes 221192 | tf_op jit(solution)/shard_map/ppermute | solution.py:303
  29.9 2.9 %collective-permute-start.13 = (f32[16,1152]{1,0:T(8,128)S(1)}, f32[16,1152]{1,0:T(8,128)S(1)}, u32[]{:S(2)}, u32[]{:S(2)}) collective-permute-start(f32[16,1152]{1,0:T(8,128)S(1)} %add.45.refs_2_), channel_id=1, source_target_pairs={{0,1},{1,0},{2,3},{3,2},{4,5},{5,4},{6,7},{7,6},{8,9},{9,8},{10,11... | collective-permute-start | bytes 221192 | tf_op jit(solution)/shard_map/ppermute | solution.py:303
  29.9 2.9 %collective-permute-start.15 = (f32[16,1152]{1,0:T(8,128)S(1)}, f32[16,1152]{1,0:T(8,128)S(1)}, u32[]{:S(2)}, u32[]{:S(2)}) collective-permute-start(f32[16,1152]{1,0:T(8,128)S(1)} %collective-permute-done.14.refs_3_), channel_id=1, source_target_pairs={{0,1},{1,0},{2,3},{3,2},{4,5},{5,4},{6,7},{7,6},{8,9},{9,8},{10,11... | collective-permute-start | bytes 221192 | tf_op jit(solution)/shard_map/ppermute | solution.py:303
  30.4 3.4 %collective-permute-start.5 = (f32[16,1152]{1,0:T(8,128)S(1)}, f32[16,1152]{1,0:T(8,128)S(1)}, u32[]{:S(2)}, u32[]{:S(2)}) collective-permute-start(f32[16,1152]{1,0:T(8,128)S(1)} %add.40.refs_0_.refs_2_.refs_6_), channel_id=1, source_target_pairs={{0,1},{1,0},{2,3},{3,2},{4,5},{5,4},{6,7},{7,6},{8,9},{9,8},{10,11... | collective-permute-start | bytes 221192 | tf_op jit(solution)/shard_map/ppermute | solution.py:303
  32.7 1.3 %collective-permute-start.7 = (f32[16,1152]{1,0:T(8,128)S(1)}, f32[16,1152]{1,0:T(8,128)S(1)}, u32[]{:S(2)}, u32[]{:S(2)}) collective-permute-start(f32[16,1152]{1,0:T(8,128)S(1)} %collective-permute-done.6.refs_1_.refs_3_.refs_7_), channel_id=1, source_target_pairs={{0,1},{1,0},{2,3},{3,2},{4,5},{5,4},{6,7},{7,6},{8,9},{9,8},{10,11... | collective-permute-start | bytes 221192 | tf_op jit(solution)/shard_map/ppermute | solution.py:303
  34.3 4.0 %collective-permute-start.16 = (f32[32,256]{1,0:T(8,128)S(1)}, f32[32,256]{1,0:T(8,128)S(1)}, u32[]{:S(2)}, u32[]{:S(2)}) collective-permute-start(f32[32,256]{1,0:T(8,128)S(1)} %right_products_other.1), channel_id=1, source_target_pairs={{0,4},{1,5},{2,6},{3,7},{4,0},{5,1},{6,2},{7,3},{8,12},{9,13},{10,... | collective-permute-start | bytes 98312 | tf_op jit(solution)/shard_map/ppermute | solution.py:303
  38.3 4.1 %collective-permute-start.17 = (f32[32,256]{1,0:T(8,128)S(1)}, f32[32,256]{1,0:T(8,128)S(1)}, u32[]{:S(2)}, u32[]{:S(2)}) collective-permute-start(f32[32,256]{1,0:T(8,128)S(1)} %add.46), channel_id=1, source_target_pairs={{0,8},{1,9},{2,10},{3,11},{4,12},{5,13},{6,14},{7,15},{8,0},{9,1},... | collective-permute-start | bytes 98312 | tf_op jit(solution)/shard_map/ppermute | solution.py:303
  42.4 4.8 %collective-permute-start.18 = (f32[32,256]{1,0:T(8,128)S(1)}, f32[32,256]{1,0:T(8,128)S(1)}, u32[]{:S(2)}, u32[]{:S(2)}) collective-permute-start(f32[32,256]{1,0:T(8,128)S(1)} %add.47.t0_ref), channel_id=1, source_target_pairs={{0,16},{1,17},{2,18},{3,19},{4,20},{5,21},{6,22},{7,23},{8,24},{9,... | collective-permute-start | bytes 98312 | tf_op jit(solution)/shard_map/ppermute | solution.py:303

commit v4 on v3

v4 whole, which is shorter than its diff:
```python
import functools

import jax
import jax.numpy as jnp
from jax import lax
from jax.experimental import pallas as pl
from jax.experimental.pallas import tpu as pltpu
from jax.sharding import PartitionSpec as P

F32, BF16 = jnp.float32, jnp.bfloat16
VMEM = pl.BlockSpec(memory_space=pltpu.VMEM)
HBM = pl.BlockSpec(memory_space=pltpu.HBM)
AXES = ("dp", "tensor")
LIMIT = 12 * 2**20
UNITS = 6


def split(x, terms):
    out = []
    for _ in range(terms):
        t = x.astype(BF16)
        out.append(t)
        x = x - t.astype(F32)
    return out


def stack(terms):
    return jnp.concatenate(terms, axis=0)


def dot(a, b, contract):
    return lax.dot_general(a, b, ((contract[:1], contract[1:]), ((), ())), preferred_element_type=F32)


def fold(x, rank):
    return functools.reduce(jnp.add, [x[i : i + rank] for i in range(0, x.shape[0], rank)])


def six_left(x):
    a, b, c = split(x, 3)
    return jnp.concatenate([a, a, b, a, b, c], axis=1)


def six_right(x):
    u, v, w = split(x, 3)
    return stack([u, v, u, w, v, u])


def walks(devices):
    bits = []
    bit = 2
    while bit < devices:
        bits.append(bit)
        bit *= 2
    walk = bits[::2] + bits[1::2]
    return walk, walk[1:] + walk[:1]


def sides(devices):
    place = lax.axis_index("dp") * lax.axis_size("tensor") + lax.axis_index("tensor")
    core = place & 1
    first, second = ((place >> (walk[0].bit_length() - 1)) & 1 for walk in walks(devices))
    return (1 - core, jnp.where(core == 0, second, first)), (core, jnp.where(core == 0, first, second))


def start(pairs):
    for pair in pairs:
        for copy in pair:
            copy.start()


def wait(pairs):
    for pair in pairs:
        for copy in pair:
            copy.wait()


def left_kernel(q_hbm, g_hbm, e_hbm, m_ref, mh_ref, ml_ref, e_ref, g_ref, send_a, send_b, q_buf, g_buf, q_sem, sems, *, devices):
    theirs, mine = sides(devices)
    half = e_ref.shape[0]
    block = half // 2
    q_copy = pltpu.make_async_copy(q_hbm, q_buf, q_sem)
    q_copy.start()
    copies = []
    for n in range(4):
        source = pl.ds(pl.multiple_of((mine if n > 1 else theirs)[0] * half + n % 2 * block, block), block)
        to = pl.ds(n % 2 * block, block)
        copies.append(
            (
                pltpu.make_async_copy(g_hbm.at[source], (g_ref if n > 1 else g_buf).at[to], sems.at[n, 0]),
                pltpu.make_async_copy(e_hbm.at[source], (e_ref if n > 1 else m_ref).at[to], sems.at[n, 1]),
            )
        )
    start(copies[:3])
    q_copy.wait()
    q = stack(split(q_buf[...], 3))
    for n in range(2):
        wait(copies[n : n + 1])
        if n == 0:
            start(copies[3:])
        at = slice(n * block, (n + 1) * block)
        m = m_ref[at] + g_buf[at].astype(F32)
        m_ref[at] = m
        place(products(q, m, mh_ref, ml_ref, at), n * block, theirs[1], send_a, send_b)
    wait(copies[2:])


def left_rest_kernel(q_ref, e_ref, g_ref, m_ref, mh_ref, ml_ref, keep_a, keep_b, *, devices):
    _, (_, bit) = sides(devices)
    half = e_ref.shape[0]
    block = half // 2
    q = stack(split(q_ref[...], 3))
    for n in range(2):
        at = slice(n * block, (n + 1) * block)
        m = e_ref[at] + g_ref[at].astype(F32)
        m_ref[at] = m
        place(products(q, m, mh_ref, ml_ref, at), n * block, bit, keep_a, keep_b)


def place(p, start, bit, out_a, out_b):
    rows = out_b.shape[1]
    at = 0
    while at < p.shape[1]:
        unit, inside = (start + at) // rows, (start + at) % rows
        width = min(rows - inside, p.shape[1] - at)
        columns = slice(inside, inside + width)
        if unit == 2:
            out_b[:, columns] = p[:, at : at + width]
        else:
            out_a[1 - bit if unit == 0 else bit, :, columns] = p[:, at : at + width]
        at += width


def products(q, m, mh_ref, ml_ref, at):
    mh, ml = split(m, 2)
    mh_ref[at] = mh
    ml_ref[at] = ml
    return fold(dot(q, mh, (1, 1)) + dot(q, ml, (1, 1)), q.shape[0] // 3)


def square(p, rank):
    g = fold(dot(p, p, (1, 1)), rank)
    return g[:, :rank] + g[:, rank : 2 * rank] + g[:, 2 * rank :]


def terms_of(pieces):
    return jnp.concatenate([stack(split(x[...], 3)) for x in pieces], axis=1)


def unit_at(n, rows):
    return pl.ds(n * rows if isinstance(n, int) else pl.multiple_of(n * rows, rows), rows)


def right_early_kernel(a1, b0, a3, b1, mh_ref, ml_ref, mh2_ref, ml2_ref, t_ref, gram_ref, *, devices):
    rank, rows = a1.shape
    (_, their_bit), (_, bit) = sides(devices)
    t = gram = 0.0
    for ref, unit, hs, ls in ((a3, bit, mh2_ref, ml2_ref), (b1, 2, mh2_ref, ml2_ref), (a1, their_bit, mh_ref, ml_ref), (b0, 2, mh_ref, ml_ref)):
        at = unit_at(unit, rows)
        p = terms_of((ref,))
        t = t + dot(p, hs[at], (1, 0)) + dot(p, ls[at], (1, 0))
        gram = gram + square(p, rank)
    t_ref[...] = fold(t, rank)
    gram_ref[...] = gram


def right_kernel(p_ref, mh_ref, ml_ref, before, t_ref, *, side, devices):
    rank, rows = p_ref.shape
    p = terms_of((p_ref,))
    at = unit_at(1 - sides(devices)[side][1], rows)
    t_ref[...] = before[...] + fold(dot(p, mh_ref[at], (1, 0)) + dot(p, ml_ref[at], (1, 0)), rank)


def eliminate(a, pivots):
    rank = a.shape[0]
    row = lax.broadcasted_iota(jnp.int32, (rank, 1), 0)
    for k in pivots:
        line = a[k : k + 1, :] / a[k : k + 1, k : k + 1]
        a = a - jnp.where(row > k, a[:, k : k + 1], 0.0) * line
    return a


def factor_kernel(gram_ref, a0, a2, state_ref):
    rank = gram_ref.shape[0]
    gram = gram_ref[...] + square(terms_of((a0, a2)), rank)
    row = lax.broadcasted_iota(jnp.int32, (rank, 128), 0)
    lane = lax.broadcasted_iota(jnp.int32, (rank, 128), 1)
    eye = (lane == row + rank).astype(F32)
    state_ref[...] = eliminate(jnp.concatenate([gram, eye[:, rank:]], axis=1), range(rank // 2))


def inverse_kernel(state_ref, inv_ref):
    rank = state_ref.shape[0]
    a = eliminate(state_ref[...], range(rank // 2, rank - 1))
    row = lax.broadcasted_iota(jnp.int32, a.shape, 0)
    lane = lax.broadcasted_iota(jnp.int32, a.shape, 1)
    pivots = jnp.sum(jnp.where(row == lane, a, 0.0), axis=1, keepdims=True)
    inv_ref[...] = a[:, rank : 2 * rank] / jnp.sqrt(pivots)


def hat_kernel(inv_ref, *refs, devices):
    pieces, (hat_hbm, rows_ref, hat_buf, sems) = refs[:UNITS], refs[UNITS:]
    rows = pieces[0].shape[1]
    inverse = inv_ref[...]
    left, back = six_left(inverse), six_left(inverse.T)
    copies, units = [], []
    for n, (core, bit) in enumerate(sides(devices)):
        for k, unit in enumerate((1 - bit, bit, 2)):
            i = 3 * n + k
            units.append(3 * n + unit)
            at = pl.ds(i * rows, rows)
            hat_buf[:, at] = dot(left, six_right(pieces[i][...]), (1, 0))
            copies.append(pltpu.make_async_copy(hat_buf.at[:, at], hat_hbm.at[:, unit_at(3 * core + unit, rows)], sems.at[i]))
            copies[-1].start()
    for i in range(UNITS):
        u, v = split(dot(back, six_right(hat_buf[:, i * rows : (i + 1) * rows]), (1, 0)), 2)
        rows_ref[unit_at(units[i], rows), :] = stack([u, v, u, v]).T
    for copy in copies:
        copy.wait()


def error_kernel(t0_ref, t1_ref, inv_ref, rows_ref, m_ref, m2_ref, out_hbm, q_hbm, buf, q_buf, sems, q_sem, *, replicas, block, devices):
    t = (t0_ref[...] + t1_ref[...]) / replicas
    u, v = split(t, 2)
    terms = stack([u, u, v, v])
    half = m_ref.shape[0]
    copies = []
    for source, side, shift in ((m_ref, 0, 0), (m2_ref, 1, half)):
        for at in range(0, half, block):
            here = slice(shift + at, shift + at + block)
            buf[here] = source[at : at + block] - dot(rows_ref[here], terms, (1, 0))
            to = pl.ds(pl.multiple_of(sides(devices)[side][0] * half + at, block), block)
            copies.append(pltpu.make_async_copy(buf.at[pl.ds(shift + at, block)], out_hbm.at[to], sems.at[len(copies)]))
            copies[-1].start()
    q_buf[...] = dot(six_left(inv_ref[...]), six_right(t), (1, 0))
    copies.append(pltpu.make_async_copy(q_buf, q_hbm, q_sem))
    copies[-1].start()
    for copy in copies:
        copy.wait()


def shards(gradient, error_buffer, q_given):
    replicas, tensors = lax.axis_size("dp"), lax.axis_size("tensor")
    devices = replicas * tensors
    depth, columns = gradient.shape[1:]
    rank = q_given.shape[1]
    rows = depth // UNITS

    def call(kernel, name, flops, **kw):
        made = pl.pallas_call(
            kernel,
            name=name,
            compiler_params=pltpu.CompilerParams(vmem_limit_bytes=LIMIT),
            cost_estimate=pl.CostEstimate(flops=flops, bytes_accessed=0, transcendentals=0),
            **kw,
        )
        spaces = [pltpu.HBM if spec is HBM else pltpu.VMEM for spec in kw["in_specs"]]
        return lambda *args: made(*(pltpu.with_memory_space_constraint(x, space) for x, space in zip(args, spaces, strict=True)))

    unit = pltpu.VMEM((rank, rows), F32)
    small = pltpu.VMEM((rank, rank), F32)
    wide = pltpu.VMEM((rank, columns), F32)
    work = 6 * depth * columns * rank

    merged = tuple(pltpu.VMEM((depth // 2, columns), kind) for kind in (F32, BF16, BF16))
    two = pltpu.VMEM((2, rank, rows), F32)
    m, mh, ml, e_own, g_own, send_a, send_b = call(
        functools.partial(left_kernel, devices=devices),
        "left_products",
        work,
        out_shape=merged + merged[:2] + (two, unit),
        in_specs=[HBM] * 3,
        out_specs=(VMEM,) * 7,
        scratch_shapes=[
            pltpu.VMEM((rank, columns), F32),
            pltpu.VMEM((depth // 2, columns), BF16),
            pltpu.SemaphoreType.DMA(()),
            pltpu.SemaphoreType.DMA((4, 2)),
        ],
    )(q_given.T, gradient[0], error_buffer[0])
    m2, mh2, ml2, keep_a, keep_b = call(
        functools.partial(left_rest_kernel, devices=devices),
        "left_products_rest",
        work,
        out_shape=merged + (two, unit),
        in_specs=[VMEM] * 3,
        out_specs=(VMEM,) * 5,
    )(q_given.T, e_own, g_own)

    def swap(x, bit, bit1=None):
        choice = (bit, bit if bit1 is None else bit1)
        return lax.ppermute(x, AXES, [(i, i ^ choice[i & 1]) for i in range(devices)])

    walk = list(zip(*walks(devices), strict=True))
    both = keep_a + swap(send_a, 1)
    b1 = keep_b + swap(send_b, 1)
    sent, a3 = both[0], both[1]
    for n, bits in enumerate(walk):
        arrived = swap(sent if n == 0 else a3, *bits), swap(b1, *bits)
        a3, b1 = a3 + arrived[0], b1 + arrived[1]
    a2 = swap(a3, *walk[0])
    a1, b0, a0 = swap(a3, 1), swap(b1, 1), swap(a2, 1)

    t, gram = call(
        functools.partial(right_early_kernel, devices=devices),
        "right_products",
        work,
        out_shape=(wide, small),
        in_specs=[VMEM] * 8,
        out_specs=(VMEM, VMEM),
    )(a1, b0, a3, b1, mh, ml, mh2, ml2)
    for side, name, x, hs, ls in ((1, "own", a2, mh2, ml2), (0, "other", a0, mh, ml)):
        t = call(
            functools.partial(right_kernel, side=side, devices=devices),
            "right_products_" + name,
            work,
            out_shape=wide,
            in_specs=[VMEM] * 4,
            out_specs=VMEM,
        )(x, hs, ls, t)

    state = call(
        factor_kernel,
        "factor_first_half",
        work,
        out_shape=pltpu.VMEM((rank, 128), F32),
        in_specs=[VMEM] * 3,
        out_specs=VMEM,
    )(gram, a0, a2)
    inverse = call(inverse_kernel, "factor_second_half", work, out_shape=small, in_specs=[VMEM], out_specs=VMEM)(state)
    hat, hat_rows = call(
        functools.partial(hat_kernel, devices=devices),
        "left_factor",
        work,
        out_shape=(pltpu.HBM((rank, depth), F32), pltpu.VMEM((depth, 4 * rank), BF16)),
        in_specs=[VMEM] * (1 + UNITS),
        out_specs=(HBM, VMEM),
        scratch_shapes=[pltpu.VMEM((rank, depth), F32), pltpu.SemaphoreType.DMA((UNITS,))],
    )(inverse, a0, a1, b0, a2, a3, b1)

    bits = sorted(bit for bit in walks(devices)[0] if bit >= tensors)
    beside = [state, inverse]
    got = swap(t, bits[0])
    for n, bit in enumerate(bits[1:]):
        t = t + got
        if n < len(beside):
            t, _ = lax.optimization_barrier((t, beside[n]))
        got = swap(t, bit)

    block = rows // 2
    error, q_new = call(
        functools.partial(error_kernel, replicas=replicas, block=block, devices=devices),
        "new_error",
        work,
        out_shape=(pltpu.HBM((depth, columns), F32), pltpu.HBM((rank, columns), F32)),
        in_specs=[VMEM] * 6,
        out_specs=(HBM, HBM),
        scratch_shapes=[
            pltpu.VMEM((depth, columns), F32),
            pltpu.VMEM((rank, columns), F32),
            pltpu.SemaphoreType.DMA((depth // block,)),
            pltpu.SemaphoreType.DMA(()),
        ],
    )(t, got, inverse, hat_rows, m, m2)
    return (error[None], hat.T, q_new.T)


def solution(mesh):
    placed = (P("dp", None, "tensor"), P("dp", None, "tensor"), P("tensor", None))
    return jax.shard_map(
        shards,
        mesh=mesh,
        in_specs=placed,
        out_specs=(P("dp", None, "tensor"), P(), P("tensor", None)),
        check_vma=False,
    )
```

time: 49.9 us -> 48.6 us (0.974)
  Pallas kernels: 12.9 us -> 12.3 us
  waiting for transfers between devices: 9.37 us -> 8.8 us
    pallas_call x9, Pallas kernels: 12.9 us -> 12.3 us  [call(): made(*(pltpu.with_memory_space_constraint(x, space) for x, space in zip(a...]
    ppermute x19 -> x17, waiting for transfers between devices: 9.37 us -> 8.8 us  [swap(): lax.ppermute(x, AXES, [(i, i ^ choice[i & 1]) for i in range(devices)])]
    ppermute x19 -> x17, starting transfers between devices: 26.6 us -> 26.4 us  [swap(): lax.ppermute(x, AXES, [(i, i ^ choice[i & 1]) for i in range(devices)])]
  transfers between devices with their start and end apart: 19 -> 17, of which waited for: 11 -> 11; matrix products, arithmetic and copies ran while one was open for 0% -> 0% of each run, Pallas kernels for 13% -> 13%
where the time goes in v4:
time: 48.6 us; the launch traced here: 48.4 us
  starting transfers between devices  26.4 us (54%)
  Pallas kernels  12.3 us (25%)
  waiting for transfers between devices  8.8 us (18%)
  between operations  0.77 us (2%)
    ppermute x17, starting transfers between devices, swap(): lax.ppermute(x, AXES, [(i, i ^ choice[i & 1]) for i in range(devices)])  26.4 us
    pallas_call x9, Pallas kernels, call(): made(*(pltpu.with_memory_space_constraint(x, space) for x, space in zip(a...  12.3 us
    ppermute x17, waiting for transfers between devices, swap(): lax.ppermute(x, AXES, [(i, i ^ choice[i & 1]) for i in range(devices)])  8.8 us
  transfers between devices with their start and end apart: 17, of which 11 were waited for; matrix products, arithmetic and copies ran while one was open for 0% of the time, Pallas kernels for 13%

profile of v4, /device:TPU:0, one launch (start us, length us, event | category | flops | bytes accessed | tf_op | source)
XLA Modules:
  0.0 48.4 jit_solution(34927318193778882)
XLA Ops:
  0.6 0.0 copy-start
  0.6 3.4 %left_products.1 = (f32[2304,256]{1,0:T(8,128)S(1)}, bf16[2304,256]{1,0:T(8,128)(2,1)S(1)}, bf16[2304,256]{1,0:T(8,128)(2,1)S(1)}, f32[2304,256]{1,0:T(8,128)S(1...) custom-call(f32[32,256]{1,0:T(8,128)} %bitcast.12, ...), custom_call_target="tpu_custom_call" | custom-call | flops 226492416 | tf_op jit(solution)/shard_map/left_products/pallas_call | solution.py:258
  4.0 0.5 %collective-permute-start = (f32[2,32,768]{2,1,0:T(8,128)S(1)}, f32[2,32,768]{2,1,0:T(8,128)S(1)}, u32[]{:S(2)}, u32[]{:S(2)}) collective-permute-start(f32[2,32,768]{2,1,0:T(8,128)S(1)} %get-tuple-element.26), channel_id=1, source_target_pairs={{0,1},{1,0},{2,3},{3,2},{4,5},{5,4},{6,7},{7,6},{8,9},{9,8},{10,11... | collective-permute-start | bytes 589832 | tf_op jit(solution)/shard_map/ppermute | solution.py:292
  4.5 0.1 collective-permute-start.8
  4.6 0.0 copy-done
  4.6 0.9 %left_products_rest.1 = (f32[2304,256]{1,0:T(8,128)S(1)}, bf16[2304,256]{1,0:T(8,128)(2,1)S(1)}, bf16[2304,256]{1,0:T(8,128)(2,1)S(1)}, f32[2,32,768]{2,1,0:T(8,128)S(1)}, f32[32,768]{1,0:T(8,128)S(1)}) custom-call(f32[32,256]{1,0:T(8,128)S(1)} %bitcast.13, f32[2304,256]{1,0:T(8,128)S(1)} %get-tuple-element.23.e_ref, ...), custom_call_target="tpu_custom_call" | custom-call | flops 226492416 | tf_op jit(solution)/shard_map/left_products_rest/pallas_call | solution.py:258
  5.5 0.1 collective-permute-done
  5.6 2.9 %collective-permute-start.1 = (f32[32,768]{1,0:T(8,128)S(1)}, f32[32,768]{1,0:T(8,128)S(1)}, u32[]{:S(2)}, u32[]{:S(2)}) collective-permute-start(f32[32,768]{1,0:T(8,128)S(1)} %slice_bitcast_fusion), channel_id=1, source_target_pairs={{0,2},{1,9},{2,0},{3,11},{4,6},{5,13},{6,4},{7,15},{8,10},{9,1},{1... | collective-permute-start | bytes 294920 | tf_op jit(solution)/shard_map/ppermute | solution.py:292
  8.6 0.0 collective-permute-done.8
  8.6 0.1 collective-permute-start.9
  8.7 2.5 %collective-permute-done.1 = f32[32,768]{1,0:T(8,128)S(1)} collective-permute-done((f32[32,768]{1,0:T(8,128)S(1)}, f32[32,768]{1,0:T(8,128)S(1)}, u32[]{:S(2)}, u32[]{:S(2)}) %collective-permute-start.1) | collective-permute-done | bytes 98336 | tf_op jit(solution)/shard_map/ppermute | solution.py:292
  11.2 2.2 %collective-permute-start.2 = (f32[32,768]{1,0:T(8,128)S(1)}, f32[32,768]{1,0:T(8,128)S(1)}, u32[]{:S(2)}, u32[]{:S(2)}) collective-permute-start(f32[32,768]{1,0:T(8,128)S(1)} %fusion), channel_id=1, source_target_pairs={{0,8},{1,5},{2,10},{3,7},{4,12},{5,1},{6,14},{7,3},{8,0},{9,13},{1... | collective-permute-start | bytes 294920 | tf_op jit(solution)/shard_map/ppermute | solution.py:292
  13.4 0.0 collective-permute-done.9
  13.4 1.6 %collective-permute-start.10 = (f32[32,768]{1,0:T(8,128)S(1)}, f32[32,768]{1,0:T(8,128)S(1)}, u32[]{:S(2)}, u32[]{:S(2)}) collective-permute-start(f32[32,768]{1,0:T(8,128)S(1)} %add.42), channel_id=1, source_target_pairs={{0,8},{1,5},{2,10},{3,7},{4,12},{5,1},{6,14},{7,3},{8,0},{9,13},{1... | collective-permute-start | bytes 294920 | tf_op jit(solution)/shard_map/ppermute | solution.py:292
  14.9 1.0 %collective-permute-done.2 = f32[32,768]{1,0:T(8,128)S(1)} collective-permute-done((f32[32,768]{1,0:T(8,128)S(1)}, f32[32,768]{1,0:T(8,128)S(1)}, u32[]{:S(2)}, u32[]{:S(2)}) %collective-permute-start.2) | collective-permute-done | bytes 98336 | tf_op jit(solution)/shard_map/ppermute | solution.py:292
  16.0 2.0 %collective-permute-start.3 = (f32[32,768]{1,0:T(8,128)S(1)}, f32[32,768]{1,0:T(8,128)S(1)}, u32[]{:S(2)}, u32[]{:S(2)}) collective-permute-start(f32[32,768]{1,0:T(8,128)S(1)} %add.38), channel_id=1, source_target_pairs={{0,4},{1,17},{2,6},{3,19},{4,0},{5,21},{6,2},{7,23},{8,12},{9,25},... | collective-permute-start | bytes 294920 | tf_op jit(solution)/shard_map/ppermute | solution.py:292
  18.0 0.1 collective-permute-done.10
  18.1 1.6 %collective-permute-start.11 = (f32[32,768]{1,0:T(8,128)S(1)}, f32[32,768]{1,0:T(8,128)S(1)}, u32[]{:S(2)}, u32[]{:S(2)}) collective-permute-start(f32[32,768]{1,0:T(8,128)S(1)} %add.43), channel_id=1, source_target_pairs={{0,4},{1,17},{2,6},{3,19},{4,0},{5,21},{6,2},{7,23},{8,12},{9,25},... | collective-permute-start | bytes 294920 | tf_op jit(solution)/shard_map/ppermute | solution.py:292
  19.7 1.0 %collective-permute-done.3 = f32[32,768]{1,0:T(8,128)S(1)} collective-permute-done((f32[32,768]{1,0:T(8,128)S(1)}, f32[32,768]{1,0:T(8,128)S(1)}, u32[]{:S(2)}, u32[]{:S(2)}) %collective-permute-start.3) | collective-permute-done | bytes 98336 | tf_op jit(solution)/shard_map/ppermute | solution.py:292
  20.7 3.1 %collective-permute-start.4 = (f32[32,768]{1,0:T(8,128)S(1)}, f32[32,768]{1,0:T(8,128)S(1)}, u32[]{:S(2)}, u32[]{:S(2)}) collective-permute-start(f32[32,768]{1,0:T(8,128)S(1)} %add.39), channel_id=1, source_target_pairs={{0,16},{1,3},{2,18},{3,1},{4,20},{5,7},{6,22},{7,5},{8,24},{9,11},... | collective-permute-start | bytes 294920 | tf_op jit(solution)/shard_map/ppermute | solution.py:292
  23.8 0.0 collective-permute-done.11
  23.8 2.6 %collective-permute-start.12 = (f32[32,768]{1,0:T(8,128)S(1)}, f32[32,768]{1,0:T(8,128)S(1)}, u32[]{:S(2)}, u32[]{:S(2)}) collective-permute-start(f32[32,768]{1,0:T(8,128)S(1)} %add.44), channel_id=1, source_target_pairs={{0,16},{1,3},{2,18},{3,1},{4,20},{5,7},{6,22},{7,5},{8,24},{9,11},... | collective-permute-start | bytes 294920 | tf_op jit(solution)/shard_map/ppermute | solution.py:292
  26.4 0.0 collective-permute-done.4
  26.4 1.9 %collective-permute-start.5 = (f32[32,768]{1,0:T(8,128)S(1)}, f32[32,768]{1,0:T(8,128)S(1)}, u32[]{:S(2)}, u32[]{:S(2)}) collective-permute-start(f32[32,768]{1,0:T(8,128)S(1)} %add.40.a3.refs_4_), channel_id=1, source_target_pairs={{0,2},{1,9},{2,0},{3,11},{4,6},{5,13},{6,4},{7,15},{8,10},{9,1},{1... | collective-permute-start | bytes 294920 | tf_op jit(solution)/shard_map/ppermute | solution.py:292
  28.3 1.1 %collective-permute-done.12 = f32[32,768]{1,0:T(8,128)S(1)} collective-permute-done((f32[32,768]{1,0:T(8,128)S(1)}, f32[32,768]{1,0:T(8,128)S(1)}, u32[]{:S(2)}, u32[]{:S(2)}) %collective-permute-start.12) | collective-permute-done | bytes 98336 | tf_op jit(solution)/shard_map/ppermute | solution.py:292
  29.4 0.1 collective-permute-start.13
  29.5 0.5 %collective-permute-start.7 = (f32[32,768]{1,0:T(8,128)S(1)}, f32[32,768]{1,0:T(8,128)S(1)}, u32[]{:S(2)}, u32[]{:S(2)}) collective-permute-start(f32[32,768]{1,0:T(8,128)S(1)} %add.40.a3.refs_4_), channel_id=1, source_target_pairs={{0,1},{1,0},{2,3},{3,2},{4,5},{5,4},{6,7},{7,6},{8,9},{9,8},{10,11... | collective-permute-start | bytes 294920 | tf_op jit(solution)/shard_map/ppermute | solution.py:292
  30.0 1.1 %collective-permute-done.5.p_ref.a2.refs_3_ = f32[32,768]{1,0:T(8,128)S(1)} collective-permute-done((f32[32,768]{1,0:T(8,128)S(1)}, f32[32,768]{1,0:T(8,128)S(1)}, u32[]{:S(2)}, u32[]{:S(2)}) %collective-permute-start.5) | collective-permute-done | bytes 98336 | tf_op jit(solution)/shard_map/ppermute | solution.py:292
  31.1 0.0 collective-permute-start.6
  31.1 0.0 collective-permute-done.13.b0.refs_2_
  31.1 0.0 collective-permute-done.7.a1.refs_1_
  31.1 0.8 %right_products.1 = (f32[32,256]{1,0:T(8,128)S(1)}, f32[32,32]{1,0:T(8,128)S(1)}) custom-call(f32[32,768]{1,0:T(8,128)S(1)} %collective-permute-done.7.a1.refs_1_, f32[32,768]{1,0:T(8,128)S(1)} %collective-permute-done.13.b0.refs_2_, f32[32,768]{1,0:T(8,128)S(1)} %add.40.a3.refs_4_, f32[32,768]{1,0:T(8,128)S(1)} %add.45.b1.refs_5_, ...), custom_call_target="tpu_custom_call" | custom-call | flops 226492416 | tf_op jit(solution)/shard_map/right_products/pallas_call | solution.py:258
  31.9 0.3 right_products_own.1.before
  32.2 0.2 collective-permute-done.6.p_ref.a0.refs_0_
  32.4 0.3 right_products_other.1
  32.7 1.9 %collective-permute-start.14 = (f32[32,256]{1,0:T(8,128)S(1)}, f32[32,256]{1,0:T(8,128)S(1)}, u32[]{:S(2)}, u32[]{:S(2)}) collective-permute-start(f32[32,256]{1,0:T(8,128)S(1)} %right_products_other.1), channel_id=1, source_target_pairs={{0,4},{1,5},{2,6},{3,7},{4,0},{5,1},{6,2},{7,3},{8,12},{9,13},{10,... | collective-permute-start | bytes 98312 | tf_op jit(solution)/shard_map/ppermute | solution.py:292
  34.6 1.6 %factor_first_half.1.state_ref = f32[32,128]{1,0:T(8,128)S(1)} custom-call(f32[32,32]{1,0:T(8,128)S(1)} %get-tuple-element.34.gram_ref, f32[32,768]{1,0:T(8,128)S(1)} %collective-permute-done.6.p_ref.a0.refs_0_, f32[32,768]{1,0:T(8,128)S(1)} %collective-permute-done.5.p_ref.a2.refs_3_), custom_call_target="tpu_custom_call" | custom-call | flops 226492416 | tf_op jit(solution)/shard_map/factor_first_half/pallas_call | solution.py:258
  36.2 0.5 %collective-permute-done.14 = f32[32,256]{1,0:T(8,128)S(1)} collective-permute-done((f32[32,256]{1,0:T(8,128)S(1)}, f32[32,256]{1,0:T(8,128)S(1)}, u32[]{:S(2)}, u32[]{:S(2)}) %collective-permute-start.14) | collective-permute-done | bytes 32800 | tf_op jit(solution)/shard_map/ppermute | solution.py:292
  36.6 2.0 %collective-permute-start.15 = (f32[32,256]{1,0:T(8,128)S(1)}, f32[32,256]{1,0:T(8,128)S(1)}, u32[]{:S(2)}, u32[]{:S(2)}) collective-permute-start(f32[32,256]{1,0:T(8,128)S(1)} %add.46), channel_id=1, source_target_pairs={{0,8},{1,9},{2,10},{3,11},{4,12},{5,13},{6,14},{7,15},{8,0},{9,1},... | collective-permute-start | bytes 98312 | tf_op jit(solution)/shard_map/ppermute | solution.py:292
  38.7 1.3 %factor_second_half.1.inv_ref = f32[32,32]{1,0:T(8,128)S(1)} custom-call(f32[32,128]{1,0:T(8,128)S(1)} %factor_first_half.1.state_ref), custom_call_target="tpu_custom_call" | custom-call | flops 226492416 | tf_op jit(solution)/shard_map/factor_second_half/pallas_call | solution.py:258
  40.0 0.5 %collective-permute-done.15 = f32[32,256]{1,0:T(8,128)S(1)} collective-permute-done((f32[32,256]{1,0:T(8,128)S(1)}, f32[32,256]{1,0:T(8,128)S(1)}, u32[]{:S(2)}, u32[]{:S(2)}) %collective-permute-start.15) | collective-permute-done | bytes 32800 | tf_op jit(solution)/shard_map/ppermute | solution.py:292
  40.6 3.4 %collective-permute-start.16 = (f32[32,256]{1,0:T(8,128)S(1)}, f32[32,256]{1,0:T(8,128)S(1)}, u32[]{:S(2)}, u32[]{:S(2)}) collective-permute-start(f32[32,256]{1,0:T(8,128)S(1)} %add.47.t0_ref), channel_id=1, source_target_pairs={{0,16},{1,17},{2,18},{3,19},{4,20},{5,21},{6,22},{7,23},{8,24},{9,... | collective-permute-start | bytes 98312 | tf_op jit(solution)/shard_map/ppermute | solution.py:292
  44.0 1.2 %left_factor.1 = (f32[32,4608]{1,0:T(8,128)}, bf16[4608,128]{1,0:T(8,128)(2,1)S(1)}) custom-call(f32[32,32]{1,0:T(8,128)S(1)} %factor_second_half.1.inv_ref, f32[32,768]{1,0:T(8,128)S(1)} %collective-permute-done.6.p_ref.a0.refs_0_, f32[32,768]{1,0:T(8,128)S(1)} %collective-permute-done.7.a1.refs_1_, f32[32,768]{1,0:T(8,128)S(1)} %collective-permute-done.13.b0.refs_2_, ...), custom_call_target="tpu_custom_call" | custom-call | flops 226492416 | tf_op jit(solution)/shard_map/left_factor/pallas_call | solution.py:258
  45.2 0.6 %collective-permute-done.16.t1_ref = f32[32,256]{1,0:T(8,128)S(1)} collective-permute-done((f32[32,256]{1,0:T(8,128)S(1)}, f32[32,256]{1,0:T(8,128)S(1)}, u32[]{:S(2)}, u32[]{:S(2)}) %collective-permute-start.16) | collective-permute-done | bytes 32800 | tf_op jit(solution)/shard_map/ppermute | solution.py:292
  45.9 2.5 %new_error.1 = (f32[4608,256]{1,0:T(8,128)}, f32[32,256]{1,0:T(8,128)}) custom-call(f32[32,256]{1,0:T(8,128)S(1)} %add.47.t0_ref, f32[32,256]{1,0:T(8,128)S(1)} %collective-permute-done.16.t1_ref, f32[32,32]{1,0:T(8,128)S(1)} %factor_second_half.1.inv_ref, bf16[4608,128]{1,0:T(8,128)(2,1)S(1)} %get-tuple-element.37.rows_ref, ...), custom_call_target="tpu_custom_call" | custom-call | flops 226492416 | tf_op jit(solution)/shard_map/new_error/pallas_call | solution.py:258
  (13 shorter events, 0.2 us)
Async XLA Ops:
  0.6 4.0 %copy-start = (f32[256,32]{0,1:T(8,128)S(1)}, f32[256,32]{0,1:T(8,128)}, u32[]{:S(2)}) copy-start(f32[256,32]{0,1:T(8,128)} %param.5) | copy-start | bytes 98308
  4.0 1.6 %collective-permute-start = (f32[2,32,768]{2,1,0:T(8,128)S(1)}, f32[2,32,768]{2,1,0:T(8,128)S(1)}, u32[]{:S(2)}, u32[]{:S(2)}) collective-permute-start(f32[2,32,768]{2,1,0:T(8,128)S(1)} %get-tuple-element.26), channel_id=1, source_target_pairs={{0,1},{1,0},{2,3},{3,2},{4,5},{5,4},{6,7},{7,6},{8,9},{9,8},{10,11... | collective-permute-start | bytes 589832 | tf_op jit(solution)/shard_map/ppermute | solution.py:292
  4.5 4.0 %collective-permute-start.8 = (f32[32,768]{1,0:T(8,128)S(1)}, f32[32,768]{1,0:T(8,128)S(1)}, u32[]{:S(2)}, u32[]{:S(2)}) collective-permute-start(f32[32,768]{1,0:T(8,128)S(1)} %get-tuple-element.32), channel_id=1, source_target_pairs={{0,1},{1,0},{2,3},{3,2},{4,5},{5,4},{6,7},{7,6},{8,9},{9,8},{10,11... | collective-permute-start | bytes 294920 | tf_op jit(solution)/shard_map/ppermute | solution.py:292
  5.6 5.5 %collective-permute-start.1 = (f32[32,768]{1,0:T(8,128)S(1)}, f32[32,768]{1,0:T(8,128)S(1)}, u32[]{:S(2)}, u32[]{:S(2)}) collective-permute-start(f32[32,768]{1,0:T(8,128)S(1)} %slice_bitcast_fusion), channel_id=1, source_target_pairs={{0,2},{1,9},{2,0},{3,11},{4,6},{5,13},{6,4},{7,15},{8,10},{9,1},{1... | collective-permute-start | bytes 294920 | tf_op jit(solution)/shard_map/ppermute | solution.py:292
  8.6 4.8 %collective-permute-start.9 = (f32[32,768]{1,0:T(8,128)S(1)}, f32[32,768]{1,0:T(8,128)S(1)}, u32[]{:S(2)}, u32[]{:S(2)}) collective-permute-start(f32[32,768]{1,0:T(8,128)S(1)} %add.41), channel_id=1, source_target_pairs={{0,2},{1,9},{2,0},{3,11},{4,6},{5,13},{6,4},{7,15},{8,10},{9,1},{1... | collective-permute-start | bytes 294920 | tf_op jit(solution)/shard_map/ppermute | solution.py:292
  11.2 4.8 %collective-permute-start.2 = (f32[32,768]{1,0:T(8,128)S(1)}, f32[32,768]{1,0:T(8,128)S(1)}, u32[]{:S(2)}, u32[]{:S(2)}) collective-permute-start(f32[32,768]{1,0:T(8,128)S(1)} %fusion), channel_id=1, source_target_pairs={{0,8},{1,5},{2,10},{3,7},{4,12},{5,1},{6,14},{7,3},{8,0},{9,13},{1... | collective-permute-start | bytes 294920 | tf_op jit(solution)/shard_map/ppermute | solution.py:292
  13.4 4.7 %collective-permute-start.10 = (f32[32,768]{1,0:T(8,128)S(1)}, f32[32,768]{1,0:T(8,128)S(1)}, u32[]{:S(2)}, u32[]{:S(2)}) collective-permute-start(f32[32,768]{1,0:T(8,128)S(1)} %add.42), channel_id=1, source_target_pairs={{0,8},{1,5},{2,10},{3,7},{4,12},{5,1},{6,14},{7,3},{8,0},{9,13},{1... | collective-permute-start | bytes 294920 | tf_op jit(solution)/shard_map/ppermute | solution.py:292
  16.0 4.7 %collective-permute-start.3 = (f32[32,768]{1,0:T(8,128)S(1)}, f32[32,768]{1,0:T(8,128)S(1)}, u32[]{:S(2)}, u32[]{:S(2)}) collective-permute-start(f32[32,768]{1,0:T(8,128)S(1)} %add.38), channel_id=1, source_target_pairs={{0,4},{1,17},{2,6},{3,19},{4,0},{5,21},{6,2},{7,23},{8,12},{9,25},... | collective-permute-start | bytes 294920 | tf_op jit(solution)/shard_map/ppermute | solution.py:292
  18.1 5.7 %collective-permute-start.11 = (f32[32,768]{1,0:T(8,128)S(1)}, f32[32,768]{1,0:T(8,128)S(1)}, u32[]{:S(2)}, u32[]{:S(2)}) collective-permute-start(f32[32,768]{1,0:T(8,128)S(1)} %add.43), channel_id=1, source_target_pairs={{0,4},{1,17},{2,6},{3,19},{4,0},{5,21},{6,2},{7,23},{8,12},{9,25},... | collective-permute-start | bytes 294920 | tf_op jit(solution)/shard_map/ppermute | solution.py:292
  20.7 5.7 %collective-permute-start.4 = (f32[32,768]{1,0:T(8,128)S(1)}, f32[32,768]{1,0:T(8,128)S(1)}, u32[]{:S(2)}, u32[]{:S(2)}) collective-permute-start(f32[32,768]{1,0:T(8,128)S(1)} %add.39), channel_id=1, source_target_pairs={{0,16},{1,3},{2,18},{3,1},{4,20},{5,7},{6,22},{7,5},{8,24},{9,11},... | collective-permute-start | bytes 294920 | tf_op jit(solution)/shard_map/ppermute | solution.py:292
  23.8 5.6 %collective-permute-start.12 = (f32[32,768]{1,0:T(8,128)S(1)}, f32[32,768]{1,0:T(8,128)S(1)}, u32[]{:S(2)}, u32[]{:S(2)}) collective-permute-start(f32[32,768]{1,0:T(8,128)S(1)} %add.44), channel_id=1, source_target_pairs={{0,16},{1,3},{2,18},{3,1},{4,20},{5,7},{6,22},{7,5},{8,24},{9,11},... | collective-permute-start | bytes 294920 | tf_op jit(solution)/shard_map/ppermute | solution.py:292
  26.4 4.7 %collective-permute-start.5 = (f32[32,768]{1,0:T(8,128)S(1)}, f32[32,768]{1,0:T(8,128)S(1)}, u32[]{:S(2)}, u32[]{:S(2)}) collective-permute-start(f32[32,768]{1,0:T(8,128)S(1)} %add.40.a3.refs_4_), channel_id=1, source_target_pairs={{0,2},{1,9},{2,0},{3,11},{4,6},{5,13},{6,4},{7,15},{8,10},{9,1},{1... | collective-permute-start | bytes 294920 | tf_op jit(solution)/shard_map/ppermute | solution.py:292
  29.4 1.7 %collective-permute-start.13 = (f32[32,768]{1,0:T(8,128)S(1)}, f32[32,768]{1,0:T(8,128)S(1)}, u32[]{:S(2)}, u32[]{:S(2)}) collective-permute-start(f32[32,768]{1,0:T(8,128)S(1)} %add.45.b1.refs_5_), channel_id=1, source_target_pairs={{0,1},{1,0},{2,3},{3,2},{4,5},{5,4},{6,7},{7,6},{8,9},{9,8},{10,11... | collective-permute-start | bytes 294920 | tf_op jit(solution)/shard_map/ppermute | solution.py:292
  29.5 1.6 %collective-permute-start.7 = (f32[32,768]{1,0:T(8,128)S(1)}, f32[32,768]{1,0:T(8,128)S(1)}, u32[]{:S(2)}, u32[]{:S(2)}) collective-permute-start(f32[32,768]{1,0:T(8,128)S(1)} %add.40.a3.refs_4_), channel_id=1, source_target_pairs={{0,1},{1,0},{2,3},{3,2},{4,5},{5,4},{6,7},{7,6},{8,9},{9,8},{10,11... | collective-permute-start | bytes 294920 | tf_op jit(solution)/shard_map/ppermute | solution.py:292
  31.1 1.3 %collective-permute-start.6 = (f32[32,768]{1,0:T(8,128)S(1)}, f32[32,768]{1,0:T(8,128)S(1)}, u32[]{:S(2)}, u32[]{:S(2)}) collective-permute-start(f32[32,768]{1,0:T(8,128)S(1)} %collective-permute-done.5.p_ref.a2.refs_3_), channel_id=1, source_target_pairs={{0,1},{1,0},{2,3},{3,2},{4,5},{5,4},{6,7},{7,6},{8,9},{9,8},{10,11... | collective-permute-start | bytes 294920 | tf_op jit(solution)/shard_map/ppermute | solution.py:292
  32.7 4.0 %collective-permute-start.14 = (f32[32,256]{1,0:T(8,128)S(1)}, f32[32,256]{1,0:T(8,128)S(1)}, u32[]{:S(2)}, u32[]{:S(2)}) collective-permute-start(f32[32,256]{1,0:T(8,128)S(1)} %right_products_other.1), channel_id=1, source_target_pairs={{0,4},{1,5},{2,6},{3,7},{4,0},{5,1},{6,2},{7,3},{8,12},{9,13},{10,... | collective-permute-start | bytes 98312 | tf_op jit(solution)/shard_map/ppermute | solution.py:292
  36.6 3.9 %collective-permute-start.15 = (f32[32,256]{1,0:T(8,128)S(1)}, f32[32,256]{1,0:T(8,128)S(1)}, u32[]{:S(2)}, u32[]{:S(2)}) collective-permute-start(f32[32,256]{1,0:T(8,128)S(1)} %add.46), channel_id=1, source_target_pairs={{0,8},{1,9},{2,10},{3,11},{4,12},{5,13},{6,14},{7,15},{8,0},{9,1},... | collective-permute-start | bytes 98312 | tf_op jit(solution)/shard_map/ppermute | solution.py:292
  40.6 5.3 %collective-permute-start.16 = (f32[32,256]{1,0:T(8,128)S(1)}, f32[32,256]{1,0:T(8,128)S(1)}, u32[]{:S(2)}, u32[]{:S(2)}) collective-permute-start(f32[32,256]{1,0:T(8,128)S(1)} %add.47.t0_ref), channel_id=1, source_target_pairs={{0,16},{1,17},{2,18},{3,19},{4,20},{5,21},{6,22},{7,23},{8,24},{9,... | collective-permute-start | bytes 98312 | tf_op jit(solution)/shard_map/ppermute | solution.py:292

commit v5 on v4

--- a/solution.py
+++ b/solution.py
@@ -56,11 +56,17 @@
     return walk, walk[1:] + walk[:1]
 
 
+def role(place):
+    return place.bit_count() & 1
+
+
 def sides(devices):
     place = lax.axis_index("dp") * lax.axis_size("tensor") + lax.axis_index("tensor")
-    core = place & 1
+    half = 0
+    for n in range(devices.bit_length() - 1):
+        half = half ^ ((place >> n) & 1)
     first, second = ((place >> (walk[0].bit_length() - 1)) & 1 for walk in walks(devices))
-    return (1 - core, jnp.where(core == 0, second, first)), (core, jnp.where(core == 0, first, second))
+    return (1 - half, jnp.where(half == 0, second, first)), (half, jnp.where(half == 0, first, second))
 
 
 def start(pairs):
@@ -287,18 +293,20 @@
         out_specs=(VMEM,) * 5,
     )(q_given.T, e_own, g_own)
 
-    def swap(x, bit, bit1=None):
-        choice = (bit, bit if bit1 is None else bit1)
-        return lax.ppermute(x, AXES, [(i, i ^ choice[i & 1]) for i in range(devices)])
+    def swap(x, bit):
+        return lax.ppermute(x, AXES, [(i, i ^ bit) for i in range(devices)])
+
+    def cross(x, *bits):
+        return lax.ppermute(x, AXES, [(i, i ^ 1 ^ bits[role(i)]) for i in range(devices)])
 
     walk = list(zip(*walks(devices), strict=True))
     both = keep_a + swap(send_a, 1)
     b1 = keep_b + swap(send_b, 1)
     sent, a3 = both[0], both[1]
     for n, bits in enumerate(walk):
-        arrived = swap(sent if n == 0 else a3, *bits), swap(b1, *bits)
+        arrived = cross(sent if n == 0 else a3, *bits), cross(b1, *bits)
         a3, b1 = a3 + arrived[0], b1 + arrived[1]
-    a2 = swap(a3, *walk[0])
+    a2 = cross(a3, *walk[0])
     a1, b0, a0 = swap(a3, 1), swap(b1, 1), swap(a2, 1)
 
     t, gram = call(

time: 48.6 us -> 47 us (0.967)
  starting transfers between devices: 26.4 us -> 22.5 us
  waiting for transfers between devices: 8.8 us -> 11.2 us
    ppermute x17, starting transfers between devices: 26.4 us -> 22.5 us  [the longest x9 15.5 us: cross(): lax.ppermute(x, AXES, [(i, i ^ 1 ^ bits[role(i)]) for i in range(devices)])]
    ppermute x17, waiting for transfers between devices: 8.8 us -> 11.2 us  [the longest x9 7.85 us: cross(): lax.ppermute(x, AXES, [(i, i ^ 1 ^ bits[role(i)]) for i in range(devices)])]
  transfers between devices with their start and end apart: 17 -> 17, of which waited for: 11 -> 13; matrix products, arithmetic and copies ran while one was open for 0% -> 0% of each run, Pallas kernels for 13% -> 13%
where the time goes in v5:
time: 47 us; the launch traced here: 46.9 us
  starting transfers between devices  22.5 us (48%)
  Pallas kernels  12.3 us (26%)
  waiting for transfers between devices  11.2 us (24%)
  between operations  0.78 us (2%)
    ppermute x9, starting transfers between devices, cross(): lax.ppermute(x, AXES, [(i, i ^ 1 ^ bits[role(i)]) for i in range(devices)])  15.5 us
    pallas_call x9, Pallas kernels, call(): made(*(pltpu.with_memory_space_constraint(x, space) for x, space in zip(a...  12.3 us
    ppermute x9, waiting for transfers between devices, cross(): lax.ppermute(x, AXES, [(i, i ^ 1 ^ bits[role(i)]) for i in range(devices)])  7.85 us
    ppermute x8, starting transfers between devices, swap(): return lax.ppermute(x, AXES, [(i, i ^ bit) for i in range(devices)])  6.98 us
    ppermute x8, waiting for transfers between devices, swap(): return lax.ppermute(x, AXES, [(i, i ^ bit) for i in range(devices)])  3.39 us
  transfers between devices with their start and end apart: 17, of which 13 were waited for; matrix products, arithmetic and copies ran while one was open for 0% of the time, Pallas kernels for 13%

profile of v5, /device:TPU:0, one launch (start us, length us, event | category | flops | bytes accessed | tf_op | source)
XLA Modules:
  0.0 46.9 jit_solution(2932491084865467947)
XLA Ops:
  0.6 0.0 copy-start
  0.6 3.4 %left_products.1 = (f32[2304,256]{1,0:T(8,128)S(1)}, bf16[2304,256]{1,0:T(8,128)(2,1)S(1)}, bf16[2304,256]{1,0:T(8,128)(2,1)S(1)}, f32[2304,256]{1,0:T(8,128)S(1...) custom-call(f32[32,256]{1,0:T(8,128)} %bitcast.12, ...), custom_call_target="tpu_custom_call" | custom-call | flops 226492416 | tf_op jit(solution)/shard_map/left_products/pallas_call | solution.py:264
  4.0 0.5 %collective-permute-start = (f32[2,32,768]{2,1,0:T(8,128)S(1)}, f32[2,32,768]{2,1,0:T(8,128)S(1)}, u32[]{:S(2)}, u32[]{:S(2)}) collective-permute-start(f32[2,32,768]{2,1,0:T(8,128)S(1)} %get-tuple-element.26), channel_id=1, source_target_pairs={{0,1},{1,0},{2,3},{3,2},{4,5},{5,4},{6,7},{7,6},{8,9},{9,8},{10,11... | collective-permute-start | bytes 589832 | tf_op jit(solution)/shard_map/ppermute | solution.py:297
  4.5 0.1 collective-permute-start.8
  4.6 0.0 copy-done
  4.6 0.9 %left_products_rest.1 = (f32[2304,256]{1,0:T(8,128)S(1)}, bf16[2304,256]{1,0:T(8,128)(2,1)S(1)}, bf16[2304,256]{1,0:T(8,128)(2,1)S(1)}, f32[2,32,768]{2,1,0:T(8,128)S(1)}, f32[32,768]{1,0:T(8,128)S(1)}) custom-call(f32[32,256]{1,0:T(8,128)S(1)} %bitcast.13, f32[2304,256]{1,0:T(8,128)S(1)} %get-tuple-element.23.e_ref, ...), custom_call_target="tpu_custom_call" | custom-call | flops 226492416 | tf_op jit(solution)/shard_map/left_products_rest/pallas_call | solution.py:264
  5.5 0.1 collective-permute-done
  5.6 2.7 %collective-permute-start.1 = (f32[32,768]{1,0:T(8,128)S(1)}, f32[32,768]{1,0:T(8,128)S(1)}, u32[]{:S(2)}, u32[]{:S(2)}) collective-permute-start(f32[32,768]{1,0:T(8,128)S(1)} %slice_bitcast_fusion), channel_id=1, source_target_pairs={{0,3},{1,8},{2,11},{3,0},{4,13},{5,6},{6,5},{7,14},{8,1},{9,10},{1... | collective-permute-start | bytes 294920 | tf_op jit(solution)/shard_map/ppermute | solution.py:300
  8.3 0.0 collective-permute-done.8
  8.3 0.2 collective-permute-start.9
  8.5 2.1 %collective-permute-done.1 = f32[32,768]{1,0:T(8,128)S(1)} collective-permute-done((f32[32,768]{1,0:T(8,128)S(1)}, f32[32,768]{1,0:T(8,128)S(1)}, u32[]{:S(2)}, u32[]{:S(2)}) %collective-permute-start.1) | collective-permute-done | bytes 98336 | tf_op jit(solution)/shard_map/ppermute | solution.py:300
  10.6 2.2 %collective-permute-start.2 = (f32[32,768]{1,0:T(8,128)S(1)}, f32[32,768]{1,0:T(8,128)S(1)}, u32[]{:S(2)}, u32[]{:S(2)}) collective-permute-start(f32[32,768]{1,0:T(8,128)S(1)} %fusion), channel_id=1, source_target_pairs={{0,9},{1,4},{2,7},{3,10},{4,1},{5,12},{6,15},{7,2},{8,13},{9,0},{1... | collective-permute-start | bytes 294920 | tf_op jit(solution)/shard_map/ppermute | solution.py:300
  12.8 0.0 collective-permute-done.9
  12.8 1.2 %collective-permute-start.10 = (f32[32,768]{1,0:T(8,128)S(1)}, f32[32,768]{1,0:T(8,128)S(1)}, u32[]{:S(2)}, u32[]{:S(2)}) collective-permute-start(f32[32,768]{1,0:T(8,128)S(1)} %add.42), channel_id=1, source_target_pairs={{0,9},{1,4},{2,7},{3,10},{4,1},{5,12},{6,15},{7,2},{8,13},{9,0},{1... | collective-permute-start | bytes 294920 | tf_op jit(solution)/shard_map/ppermute | solution.py:300
  14.1 1.0 %collective-permute-done.2 = f32[32,768]{1,0:T(8,128)S(1)} collective-permute-done((f32[32,768]{1,0:T(8,128)S(1)}, f32[32,768]{1,0:T(8,128)S(1)}, u32[]{:S(2)}, u32[]{:S(2)}) %collective-permute-start.2) | collective-permute-done | bytes 98336 | tf_op jit(solution)/shard_map/ppermute | solution.py:300
  15.1 1.5 %collective-permute-start.3 = (f32[32,768]{1,0:T(8,128)S(1)}, f32[32,768]{1,0:T(8,128)S(1)}, u32[]{:S(2)}, u32[]{:S(2)}) collective-permute-start(f32[32,768]{1,0:T(8,128)S(1)} %add.38), channel_id=1, source_target_pairs={{0,5},{1,16},{2,19},{3,6},{4,21},{5,0},{6,3},{7,22},{8,25},{9,12},... | collective-permute-start | bytes 294920 | tf_op jit(solution)/shard_map/ppermute | solution.py:300
  16.6 0.4 collective-permute-done.10
  17.0 1.3 %collective-permute-start.11 = (f32[32,768]{1,0:T(8,128)S(1)}, f32[32,768]{1,0:T(8,128)S(1)}, u32[]{:S(2)}, u32[]{:S(2)}) collective-permute-start(f32[32,768]{1,0:T(8,128)S(1)} %add.43), channel_id=1, source_target_pairs={{0,5},{1,16},{2,19},{3,6},{4,21},{5,0},{6,3},{7,22},{8,25},{9,12},... | collective-permute-start | bytes 294920 | tf_op jit(solution)/shard_map/ppermute | solution.py:300
  18.2 1.0 %collective-permute-done.3 = f32[32,768]{1,0:T(8,128)S(1)} collective-permute-done((f32[32,768]{1,0:T(8,128)S(1)}, f32[32,768]{1,0:T(8,128)S(1)}, u32[]{:S(2)}, u32[]{:S(2)}) %collective-permute-start.3) | collective-permute-done | bytes 98336 | tf_op jit(solution)/shard_map/ppermute | solution.py:300
  19.3 2.8 %collective-permute-start.4 = (f32[32,768]{1,0:T(8,128)S(1)}, f32[32,768]{1,0:T(8,128)S(1)}, u32[]{:S(2)}, u32[]{:S(2)}) collective-permute-start(f32[32,768]{1,0:T(8,128)S(1)} %add.39), channel_id=1, source_target_pairs={{0,17},{1,2},{2,1},{3,18},{4,7},{5,20},{6,23},{7,4},{8,11},{9,24},... | collective-permute-start | bytes 294920 | tf_op jit(solution)/shard_map/ppermute | solution.py:300
  22.1 0.0 collective-permute-done.11
  22.1 1.6 %collective-permute-start.12 = (f32[32,768]{1,0:T(8,128)S(1)}, f32[32,768]{1,0:T(8,128)S(1)}, u32[]{:S(2)}, u32[]{:S(2)}) collective-permute-start(f32[32,768]{1,0:T(8,128)S(1)} %add.44), channel_id=1, source_target_pairs={{0,17},{1,2},{2,1},{3,18},{4,7},{5,20},{6,23},{7,4},{8,11},{9,24},... | collective-permute-start | bytes 294920 | tf_op jit(solution)/shard_map/ppermute | solution.py:300
  23.7 1.6 %collective-permute-done.4 = f32[32,768]{1,0:T(8,128)S(1)} collective-permute-done((f32[32,768]{1,0:T(8,128)S(1)}, f32[32,768]{1,0:T(8,128)S(1)}, u32[]{:S(2)}, u32[]{:S(2)}) %collective-permute-start.4) | collective-permute-done | bytes 98336 | tf_op jit(solution)/shard_map/ppermute | solution.py:300
  25.4 2.0 %collective-permute-start.5 = (f32[32,768]{1,0:T(8,128)S(1)}, f32[32,768]{1,0:T(8,128)S(1)}, u32[]{:S(2)}, u32[]{:S(2)}) collective-permute-start(f32[32,768]{1,0:T(8,128)S(1)} %add.40.a3.refs_4_), channel_id=1, source_target_pairs={{0,3},{1,8},{2,11},{3,0},{4,13},{5,6},{6,5},{7,14},{8,1},{9,10},{1... | collective-permute-start | bytes 294920 | tf_op jit(solution)/shard_map/ppermute | solution.py:300
  27.4 1.3 %collective-permute-done.12 = f32[32,768]{1,0:T(8,128)S(1)} collective-permute-done((f32[32,768]{1,0:T(8,128)S(1)}, f32[32,768]{1,0:T(8,128)S(1)}, u32[]{:S(2)}, u32[]{:S(2)}) %collective-permute-start.12) | collective-permute-done | bytes 98336 | tf_op jit(solution)/shard_map/ppermute | solution.py:300
  28.7 0.1 collective-permute-start.13
  28.8 0.5 %collective-permute-start.7 = (f32[32,768]{1,0:T(8,128)S(1)}, f32[32,768]{1,0:T(8,128)S(1)}, u32[]{:S(2)}, u32[]{:S(2)}) collective-permute-start(f32[32,768]{1,0:T(8,128)S(1)} %add.40.a3.refs_4_), channel_id=1, source_target_pairs={{0,1},{1,0},{2,3},{3,2},{4,5},{5,4},{6,7},{7,6},{8,9},{9,8},{10,11... | collective-permute-start | bytes 294920 | tf_op jit(solution)/shard_map/ppermute | solution.py:297
  29.3 0.4 collective-permute-done.5.p_ref.a2.refs_3_
  29.7 0.1 collective-permute-start.6
  29.8 0.3 collective-permute-done.13.b0.refs_2_
  30.1 0.2 collective-permute-done.7.a1.refs_1_
  30.2 0.8 %right_products.1 = (f32[32,256]{1,0:T(8,128)S(1)}, f32[32,32]{1,0:T(8,128)S(1)}) custom-call(f32[32,768]{1,0:T(8,128)S(1)} %collective-permute-done.7.a1.refs_1_, f32[32,768]{1,0:T(8,128)S(1)} %collective-permute-done.13.b0.refs_2_, f32[32,768]{1,0:T(8,128)S(1)} %add.40.a3.refs_4_, f32[32,768]{1,0:T(8,128)S(1)} %add.45.b1.refs_5_, ...), custom_call_target="tpu_custom_call" | custom-call | flops 226492416 | tf_op jit(solution)/shard_map/right_products/pallas_call | solution.py:264
  31.0 0.3 right_products_own.1.before
  31.3 0.0 collective-permute-done.6.p_ref.a0.refs_0_
  31.3 0.3 right_products_other.1
  31.6 1.7 %collective-permute-start.14 = (f32[32,256]{1,0:T(8,128)S(1)}, f32[32,256]{1,0:T(8,128)S(1)}, u32[]{:S(2)}, u32[]{:S(2)}) collective-permute-start(f32[32,256]{1,0:T(8,128)S(1)} %right_products_other.1), channel_id=1, source_target_pairs={{0,4},{1,5},{2,6},{3,7},{4,0},{5,1},{6,2},{7,3},{8,12},{9,13},{10,... | collective-permute-start | bytes 98312 | tf_op jit(solution)/shard_map/ppermute | solution.py:297
  33.3 1.6 %factor_first_half.1.state_ref = f32[32,128]{1,0:T(8,128)S(1)} custom-call(f32[32,32]{1,0:T(8,128)S(1)} %get-tuple-element.34.gram_ref, f32[32,768]{1,0:T(8,128)S(1)} %collective-permute-done.6.p_ref.a0.refs_0_, f32[32,768]{1,0:T(8,128)S(1)} %collective-permute-done.5.p_ref.a2.refs_3_), custom_call_target="tpu_custom_call" | custom-call | flops 226492416 | tf_op jit(solution)/shard_map/factor_first_half/pallas_call | solution.py:264
  34.9 0.7 %collective-permute-done.14 = f32[32,256]{1,0:T(8,128)S(1)} collective-permute-done((f32[32,256]{1,0:T(8,128)S(1)}, f32[32,256]{1,0:T(8,128)S(1)}, u32[]{:S(2)}, u32[]{:S(2)}) %collective-permute-start.14) | collective-permute-done | bytes 32800 | tf_op jit(solution)/shard_map/ppermute | solution.py:297
  35.6 1.3 %collective-permute-start.15 = (f32[32,256]{1,0:T(8,128)S(1)}, f32[32,256]{1,0:T(8,128)S(1)}, u32[]{:S(2)}, u32[]{:S(2)}) collective-permute-start(f32[32,256]{1,0:T(8,128)S(1)} %add.46), channel_id=1, source_target_pairs={{0,8},{1,9},{2,10},{3,11},{4,12},{5,13},{6,14},{7,15},{8,0},{9,1},... | collective-permute-start | bytes 98312 | tf_op jit(solution)/shard_map/ppermute | solution.py:297
  36.9 1.3 %factor_second_half.1.inv_ref = f32[32,32]{1,0:T(8,128)S(1)} custom-call(f32[32,128]{1,0:T(8,128)S(1)} %factor_first_half.1.state_ref), custom_call_target="tpu_custom_call" | custom-call | flops 226492416 | tf_op jit(solution)/shard_map/factor_second_half/pallas_call | solution.py:264
  38.2 1.3 %collective-permute-done.15 = f32[32,256]{1,0:T(8,128)S(1)} collective-permute-done((f32[32,256]{1,0:T(8,128)S(1)}, f32[32,256]{1,0:T(8,128)S(1)}, u32[]{:S(2)}, u32[]{:S(2)}) %collective-permute-start.15) | collective-permute-done | bytes 32800 | tf_op jit(solution)/shard_map/ppermute | solution.py:297
  39.5 2.7 %collective-permute-start.16 = (f32[32,256]{1,0:T(8,128)S(1)}, f32[32,256]{1,0:T(8,128)S(1)}, u32[]{:S(2)}, u32[]{:S(2)}) collective-permute-start(f32[32,256]{1,0:T(8,128)S(1)} %add.47.t0_ref), channel_id=1, source_target_pairs={{0,16},{1,17},{2,18},{3,19},{4,20},{5,21},{6,22},{7,23},{8,24},{9,... | collective-permute-start | bytes 98312 | tf_op jit(solution)/shard_map/ppermute | solution.py:297
  42.3 1.2 %left_factor.1 = (f32[32,4608]{1,0:T(8,128)}, bf16[4608,128]{1,0:T(8,128)(2,1)S(1)}) custom-call(f32[32,32]{1,0:T(8,128)S(1)} %factor_second_half.1.inv_ref, f32[32,768]{1,0:T(8,128)S(1)} %collective-permute-done.6.p_ref.a0.refs_0_, f32[32,768]{1,0:T(8,128)S(1)} %collective-permute-done.7.a1.refs_1_, f32[32,768]{1,0:T(8,128)S(1)} %collective-permute-done.13.b0.refs_2_, ...), custom_call_target="tpu_custom_call" | custom-call | flops 226492416 | tf_op jit(solution)/shard_map/left_factor/pallas_call | solution.py:264
  43.5 0.8 %collective-permute-done.16.t1_ref = f32[32,256]{1,0:T(8,128)S(1)} collective-permute-done((f32[32,256]{1,0:T(8,128)S(1)}, f32[32,256]{1,0:T(8,128)S(1)}, u32[]{:S(2)}, u32[]{:S(2)}) %collective-permute-start.16) | collective-permute-done | bytes 32800 | tf_op jit(solution)/shard_map/ppermute | solution.py:297
  44.4 2.5 %new_error.1 = (f32[4608,256]{1,0:T(8,128)}, f32[32,256]{1,0:T(8,128)}) custom-call(f32[32,256]{1,0:T(8,128)S(1)} %add.47.t0_ref, f32[32,256]{1,0:T(8,128)S(1)} %collective-permute-done.16.t1_ref, f32[32,32]{1,0:T(8,128)S(1)} %factor_second_half.1.inv_ref, bf16[4608,128]{1,0:T(8,128)(2,1)S(1)} %get-tuple-element.37.rows_ref, ...), custom_call_target="tpu_custom_call" | custom-call | flops 226492416 | tf_op jit(solution)/shard_map/new_error/pallas_call | solution.py:264
  (13 shorter events, 0.2 us)
Async XLA Ops:
  0.6 4.0 %copy-start = (f32[256,32]{0,1:T(8,128)S(1)}, f32[256,32]{0,1:T(8,128)}, u32[]{:S(2)}) copy-start(f32[256,32]{0,1:T(8,128)} %param.5) | copy-start | bytes 98308
  4.0 1.6 %collective-permute-start = (f32[2,32,768]{2,1,0:T(8,128)S(1)}, f32[2,32,768]{2,1,0:T(8,128)S(1)}, u32[]{:S(2)}, u32[]{:S(2)}) collective-permute-start(f32[2,32,768]{2,1,0:T(8,128)S(1)} %get-tuple-element.26), channel_id=1, source_target_pairs={{0,1},{1,0},{2,3},{3,2},{4,5},{5,4},{6,7},{7,6},{8,9},{9,8},{10,11... | collective-permute-start | bytes 589832 | tf_op jit(solution)/shard_map/ppermute | solution.py:297
  4.5 3.8 %collective-permute-start.8 = (f32[32,768]{1,0:T(8,128)S(1)}, f32[32,768]{1,0:T(8,128)S(1)}, u32[]{:S(2)}, u32[]{:S(2)}) collective-permute-start(f32[32,768]{1,0:T(8,128)S(1)} %get-tuple-element.32), channel_id=1, source_target_pairs={{0,1},{1,0},{2,3},{3,2},{4,5},{5,4},{6,7},{7,6},{8,9},{9,8},{10,11... | collective-permute-start | bytes 294920 | tf_op jit(solution)/shard_map/ppermute | solution.py:297
  5.6 5.0 %collective-permute-start.1 = (f32[32,768]{1,0:T(8,128)S(1)}, f32[32,768]{1,0:T(8,128)S(1)}, u32[]{:S(2)}, u32[]{:S(2)}) collective-permute-start(f32[32,768]{1,0:T(8,128)S(1)} %slice_bitcast_fusion), channel_id=1, source_target_pairs={{0,3},{1,8},{2,11},{3,0},{4,13},{5,6},{6,5},{7,14},{8,1},{9,10},{1... | collective-permute-start | bytes 294920 | tf_op jit(solution)/shard_map/ppermute | solution.py:300
  8.3 4.5 %collective-permute-start.9 = (f32[32,768]{1,0:T(8,128)S(1)}, f32[32,768]{1,0:T(8,128)S(1)}, u32[]{:S(2)}, u32[]{:S(2)}) collective-permute-start(f32[32,768]{1,0:T(8,128)S(1)} %add.41), channel_id=1, source_target_pairs={{0,3},{1,8},{2,11},{3,0},{4,13},{5,6},{6,5},{7,14},{8,1},{9,10},{1... | collective-permute-start | bytes 294920 | tf_op jit(solution)/shard_map/ppermute | solution.py:300
  10.6 4.5 %collective-permute-start.2 = (f32[32,768]{1,0:T(8,128)S(1)}, f32[32,768]{1,0:T(8,128)S(1)}, u32[]{:S(2)}, u32[]{:S(2)}) collective-permute-start(f32[32,768]{1,0:T(8,128)S(1)} %fusion), channel_id=1, source_target_pairs={{0,9},{1,4},{2,7},{3,10},{4,1},{5,12},{6,15},{7,2},{8,13},{9,0},{1... | collective-permute-start | bytes 294920 | tf_op jit(solution)/shard_map/ppermute | solution.py:300
  12.8 4.1 %collective-permute-start.10 = (f32[32,768]{1,0:T(8,128)S(1)}, f32[32,768]{1,0:T(8,128)S(1)}, u32[]{:S(2)}, u32[]{:S(2)}) collective-permute-start(f32[32,768]{1,0:T(8,128)S(1)} %add.42), channel_id=1, source_target_pairs={{0,9},{1,4},{2,7},{3,10},{4,1},{5,12},{6,15},{7,2},{8,13},{9,0},{1... | collective-permute-start | bytes 294920 | tf_op jit(solution)/shard_map/ppermute | solution.py:300
  15.1 4.1 %collective-permute-start.3 = (f32[32,768]{1,0:T(8,128)S(1)}, f32[32,768]{1,0:T(8,128)S(1)}, u32[]{:S(2)}, u32[]{:S(2)}) collective-permute-start(f32[32,768]{1,0:T(8,128)S(1)} %add.38), channel_id=1, source_target_pairs={{0,5},{1,16},{2,19},{3,6},{4,21},{5,0},{6,3},{7,22},{8,25},{9,12},... | collective-permute-start | bytes 294920 | tf_op jit(solution)/shard_map/ppermute | solution.py:300
  17.0 5.1 %collective-permute-start.11 = (f32[32,768]{1,0:T(8,128)S(1)}, f32[32,768]{1,0:T(8,128)S(1)}, u32[]{:S(2)}, u32[]{:S(2)}) collective-permute-start(f32[32,768]{1,0:T(8,128)S(1)} %add.43), channel_id=1, source_target_pairs={{0,5},{1,16},{2,19},{3,6},{4,21},{5,0},{6,3},{7,22},{8,25},{9,12},... | collective-permute-start | bytes 294920 | tf_op jit(solution)/shard_map/ppermute | solution.py:300
  19.3 6.1 %collective-permute-start.4 = (f32[32,768]{1,0:T(8,128)S(1)}, f32[32,768]{1,0:T(8,128)S(1)}, u32[]{:S(2)}, u32[]{:S(2)}) collective-permute-start(f32[32,768]{1,0:T(8,128)S(1)} %add.39), channel_id=1, source_target_pairs={{0,17},{1,2},{2,1},{3,18},{4,7},{5,20},{6,23},{7,4},{8,11},{9,24},... | collective-permute-start | bytes 294920 | tf_op jit(solution)/shard_map/ppermute | solution.py:300
  22.1 6.6 %collective-permute-start.12 = (f32[32,768]{1,0:T(8,128)S(1)}, f32[32,768]{1,0:T(8,128)S(1)}, u32[]{:S(2)}, u32[]{:S(2)}) collective-permute-start(f32[32,768]{1,0:T(8,128)S(1)} %add.44), channel_id=1, source_target_pairs={{0,17},{1,2},{2,1},{3,18},{4,7},{5,20},{6,23},{7,4},{8,11},{9,24},... | collective-permute-start | bytes 294920 | tf_op jit(solution)/shard_map/ppermute | solution.py:300
  25.4 4.3 %collective-permute-start.5 = (f32[32,768]{1,0:T(8,128)S(1)}, f32[32,768]{1,0:T(8,128)S(1)}, u32[]{:S(2)}, u32[]{:S(2)}) collective-permute-start(f32[32,768]{1,0:T(8,128)S(1)} %add.40.a3.refs_4_), channel_id=1, source_target_pairs={{0,3},{1,8},{2,11},{3,0},{4,13},{5,6},{6,5},{7,14},{8,1},{9,10},{1... | collective-permute-start | bytes 294920 | tf_op jit(solution)/shard_map/ppermute | solution.py:300
  28.7 1.4 %collective-permute-start.13 = (f32[32,768]{1,0:T(8,128)S(1)}, f32[32,768]{1,0:T(8,128)S(1)}, u32[]{:S(2)}, u32[]{:S(2)}) collective-permute-start(f32[32,768]{1,0:T(8,128)S(1)} %add.45.b1.refs_5_), channel_id=1, source_target_pairs={{0,1},{1,0},{2,3},{3,2},{4,5},{5,4},{6,7},{7,6},{8,9},{9,8},{10,11... | collective-permute-start | bytes 294920 | tf_op jit(solution)/shard_map/ppermute | solution.py:297
  28.8 1.4 %collective-permute-start.7 = (f32[32,768]{1,0:T(8,128)S(1)}, f32[32,768]{1,0:T(8,128)S(1)}, u32[]{:S(2)}, u32[]{:S(2)}) collective-permute-start(f32[32,768]{1,0:T(8,128)S(1)} %add.40.a3.refs_4_), channel_id=1, source_target_pairs={{0,1},{1,0},{2,3},{3,2},{4,5},{5,4},{6,7},{7,6},{8,9},{9,8},{10,11... | collective-permute-start | bytes 294920 | tf_op jit(solution)/shard_map/ppermute | solution.py:297
  29.7 1.6 %collective-permute-start.6 = (f32[32,768]{1,0:T(8,128)S(1)}, f32[32,768]{1,0:T(8,128)S(1)}, u32[]{:S(2)}, u32[]{:S(2)}) collective-permute-start(f32[32,768]{1,0:T(8,128)S(1)} %collective-permute-done.5.p_ref.a2.refs_3_), channel_id=1, source_target_pairs={{0,1},{1,0},{2,3},{3,2},{4,5},{5,4},{6,7},{7,6},{8,9},{9,8},{10,11... | collective-permute-start | bytes 294920 | tf_op jit(solution)/shard_map/ppermute | solution.py:297
  31.6 4.0 %collective-permute-start.14 = (f32[32,256]{1,0:T(8,128)S(1)}, f32[32,256]{1,0:T(8,128)S(1)}, u32[]{:S(2)}, u32[]{:S(2)}) collective-permute-start(f32[32,256]{1,0:T(8,128)S(1)} %right_products_other.1), channel_id=1, source_target_pairs={{0,4},{1,5},{2,6},{3,7},{4,0},{5,1},{6,2},{7,3},{8,12},{9,13},{10,... | collective-permute-start | bytes 98312 | tf_op jit(solution)/shard_map/ppermute | solution.py:297
  35.6 3.9 %collective-permute-start.15 = (f32[32,256]{1,0:T(8,128)S(1)}, f32[32,256]{1,0:T(8,128)S(1)}, u32[]{:S(2)}, u32[]{:S(2)}) collective-permute-start(f32[32,256]{1,0:T(8,128)S(1)} %add.46), channel_id=1, source_target_pairs={{0,8},{1,9},{2,10},{3,11},{4,12},{5,13},{6,14},{7,15},{8,0},{9,1},... | collective-permute-start | bytes 98312 | tf_op jit(solution)/shard_map/ppermute | solution.py:297
  39.5 4.8 %collective-permute-start.16 = (f32[32,256]{1,0:T(8,128)S(1)}, f32[32,256]{1,0:T(8,128)S(1)}, u32[]{:S(2)}, u32[]{:S(2)}) collective-permute-start(f32[32,256]{1,0:T(8,128)S(1)} %add.47.t0_ref), channel_id=1, source_target_pairs={{0,16},{1,17},{2,18},{3,19},{4,20},{5,21},{6,22},{7,23},{8,24},{9,... | collective-permute-start | bytes 98312 | tf_op jit(solution)/shard_map/ppermute | solution.py:297

commit v6 on v5

--- a/solution.py
+++ b/solution.py
@@ -347,13 +347,15 @@
     )(inverse, a0, a1, b0, a2, a3, b1)
 
     bits = sorted(bit for bit in walks(devices)[0] if bit >= tensors)
+    turns = len(bits) // 2 * 2
     beside = [state, inverse]
-    got = swap(t, bits[0])
-    for n, bit in enumerate(bits[1:]):
-        t = t + got
-        if n < len(beside):
-            t, _ = lax.optimization_barrier((t, beside[n]))
-        got = swap(t, bit)
+    parts = t, None
+    for n, bit in enumerate(bits):
+        if n:
+            t = parts[0] + parts[1]
+            if n <= len(beside):
+                t, _ = lax.optimization_barrier((t, beside[n - 1]))
+        parts = (swap(t, 1), swap(t, 1 ^ bit)) if n < turns else (t, swap(t, bit))
 
     block = rows // 2
     error, q_new = call(
@@ -369,7 +371,7 @@
             pltpu.SemaphoreType.DMA((depth // block,)),
             pltpu.SemaphoreType.DMA(()),
         ],
-    )(t, got, inverse, hat_rows, m, m2)
+    )(*parts, inverse, hat_rows, m, m2)
     return (error[None], hat.T, q_new.T)
 
 

time: 47 us -> 46 us (0.979)
  waiting for transfers between devices: 11.2 us -> 9.6 us
  starting transfers between devices: 22.5 us -> 23.1 us
    ppermute x8 -> x10, waiting for transfers between devices: 3.39 us -> 1.75 us  [swap(): return lax.ppermute(x, AXES, [(i, i ^ bit) for i in range(devices)])]
    ppermute x8 -> x10, starting transfers between devices: 6.98 us -> 7.59 us  [swap(): return lax.ppermute(x, AXES, [(i, i ^ bit) for i in range(devices)])]
  transfers between devices with their start and end apart: 17 -> 19, of which waited for: 13 -> 12; matrix products, arithmetic and copies ran while one was open for 0% -> 0% of each run, Pallas kernels for 13% -> 13%
where the time goes in v6:
time: 46 us; the launch traced here: 45.9 us
  starting transfers between devices  23.1 us (50%)
  Pallas kernels  12.3 us (27%)
  waiting for transfers between devices  9.6 us (21%)
  between operations  0.8 us (2%)
    ppermute x9, starting transfers between devices, cross(): lax.ppermute(x, AXES, [(i, i ^ 1 ^ bits[role(i)]) for i in range(devices)])  15.5 us
    pallas_call x9, Pallas kernels, call(): made(*(pltpu.with_memory_space_constraint(x, space) for x, space in zip(a...  12.3 us
    ppermute x9, waiting for transfers between devices, cross(): lax.ppermute(x, AXES, [(i, i ^ 1 ^ bits[role(i)]) for i in range(devices)])  7.85 us
    ppermute x10, starting transfers between devices, swap(): return lax.ppermute(x, AXES, [(i, i ^ bit) for i in range(devices)])  7.59 us
    ppermute x10, waiting for transfers between devices, swap(): return lax.ppermute(x, AXES, [(i, i ^ bit) for i in range(devices)])  1.75 us
  transfers between devices with their start and end apart: 19, of which 12 were waited for; matrix products, arithmetic and copies ran while one was open for 0% of the time, Pallas kernels for 13%

profile of v6, /device:TPU:0, one launch (start us, length us, event | category | flops | bytes accessed | tf_op | source)
XLA Modules:
  0.0 45.9 jit_solution(6027529302135064374)
XLA Ops:
  0.6 0.0 copy-start
  0.6 3.4 %left_products.1 = (f32[2304,256]{1,0:T(8,128)S(1)}, bf16[2304,256]{1,0:T(8,128)(2,1)S(1)}, bf16[2304,256]{1,0:T(8,128)(2,1)S(1)}, f32[2304,256]{1,0:T(8,128)S(1...) custom-call(f32[32,256]{1,0:T(8,128)} %bitcast.12, ...), custom_call_target="tpu_custom_call" | custom-call | flops 226492416 | tf_op jit(solution)/shard_map/left_products/pallas_call | solution.py:264
  4.0 0.5 %collective-permute-start = (f32[2,32,768]{2,1,0:T(8,128)S(1)}, f32[2,32,768]{2,1,0:T(8,128)S(1)}, u32[]{:S(2)}, u32[]{:S(2)}) collective-permute-start(f32[2,32,768]{2,1,0:T(8,128)S(1)} %get-tuple-element.26), channel_id=1, source_target_pairs={{0,1},{1,0},{2,3},{3,2},{4,5},{5,4},{6,7},{7,6},{8,9},{9,8},{10,11... | collective-permute-start | bytes 589832 | tf_op jit(solution)/shard_map/ppermute | solution.py:297
  4.5 0.1 collective-permute-start.8
  4.6 0.9 %left_products_rest.1 = (f32[2304,256]{1,0:T(8,128)S(1)}, bf16[2304,256]{1,0:T(8,128)(2,1)S(1)}, bf16[2304,256]{1,0:T(8,128)(2,1)S(1)}, f32[2,32,768]{2,1,0:T(8,128)S(1)}, f32[32,768]{1,0:T(8,128)S(1)}) custom-call(f32[32,256]{1,0:T(8,128)S(1)} %bitcast.13, f32[2304,256]{1,0:T(8,128)S(1)} %get-tuple-element.23.e_ref, ...), custom_call_target="tpu_custom_call" | custom-call | flops 226492416 | tf_op jit(solution)/shard_map/left_products_rest/pallas_call | solution.py:264
  5.5 0.1 collective-permute-done
  5.6 2.7 %collective-permute-start.1 = (f32[32,768]{1,0:T(8,128)S(1)}, f32[32,768]{1,0:T(8,128)S(1)}, u32[]{:S(2)}, u32[]{:S(2)}) collective-permute-start(f32[32,768]{1,0:T(8,128)S(1)} %slice_bitcast_fusion), channel_id=1, source_target_pairs={{0,3},{1,8},{2,11},{3,0},{4,13},{5,6},{6,5},{7,14},{8,1},{9,10},{1... | collective-permute-start | bytes 294920 | tf_op jit(solution)/shard_map/ppermute | solution.py:300
  8.3 0.0 collective-permute-done.8
  8.3 0.2 collective-permute-start.9
  8.5 2.1 %collective-permute-done.1 = f32[32,768]{1,0:T(8,128)S(1)} collective-permute-done((f32[32,768]{1,0:T(8,128)S(1)}, f32[32,768]{1,0:T(8,128)S(1)}, u32[]{:S(2)}, u32[]{:S(2)}) %collective-permute-start.1) | collective-permute-done | bytes 98336 | tf_op jit(solution)/shard_map/ppermute | solution.py:300
  10.6 2.2 %collective-permute-start.2 = (f32[32,768]{1,0:T(8,128)S(1)}, f32[32,768]{1,0:T(8,128)S(1)}, u32[]{:S(2)}, u32[]{:S(2)}) collective-permute-start(f32[32,768]{1,0:T(8,128)S(1)} %fusion), channel_id=1, source_target_pairs={{0,9},{1,4},{2,7},{3,10},{4,1},{5,12},{6,15},{7,2},{8,13},{9,0},{1... | collective-permute-start | bytes 294920 | tf_op jit(solution)/shard_map/ppermute | solution.py:300
  12.8 0.0 collective-permute-done.9
  12.8 1.2 %collective-permute-start.10 = (f32[32,768]{1,0:T(8,128)S(1)}, f32[32,768]{1,0:T(8,128)S(1)}, u32[]{:S(2)}, u32[]{:S(2)}) collective-permute-start(f32[32,768]{1,0:T(8,128)S(1)} %add.42), channel_id=1, source_target_pairs={{0,9},{1,4},{2,7},{3,10},{4,1},{5,12},{6,15},{7,2},{8,13},{9,0},{1... | collective-permute-start | bytes 294920 | tf_op jit(solution)/shard_map/ppermute | solution.py:300
  14.1 1.0 %collective-permute-done.2 = f32[32,768]{1,0:T(8,128)S(1)} collective-permute-done((f32[32,768]{1,0:T(8,128)S(1)}, f32[32,768]{1,0:T(8,128)S(1)}, u32[]{:S(2)}, u32[]{:S(2)}) %collective-permute-start.2) | collective-permute-done | bytes 98336 | tf_op jit(solution)/shard_map/ppermute | solution.py:300
  15.1 1.5 %collective-permute-start.3 = (f32[32,768]{1,0:T(8,128)S(1)}, f32[32,768]{1,0:T(8,128)S(1)}, u32[]{:S(2)}, u32[]{:S(2)}) collective-permute-start(f32[32,768]{1,0:T(8,128)S(1)} %add.38), channel_id=1, source_target_pairs={{0,5},{1,16},{2,19},{3,6},{4,21},{5,0},{6,3},{7,22},{8,25},{9,12},... | collective-permute-start | bytes 294920 | tf_op jit(solution)/shard_map/ppermute | solution.py:300
  16.6 0.4 collective-permute-done.10
  17.0 1.3 %collective-permute-start.11 = (f32[32,768]{1,0:T(8,128)S(1)}, f32[32,768]{1,0:T(8,128)S(1)}, u32[]{:S(2)}, u32[]{:S(2)}) collective-permute-start(f32[32,768]{1,0:T(8,128)S(1)} %add.43), channel_id=1, source_target_pairs={{0,5},{1,16},{2,19},{3,6},{4,21},{5,0},{6,3},{7,22},{8,25},{9,12},... | collective-permute-start | bytes 294920 | tf_op jit(solution)/shard_map/ppermute | solution.py:300
  18.2 1.0 %collective-permute-done.3 = f32[32,768]{1,0:T(8,128)S(1)} collective-permute-done((f32[32,768]{1,0:T(8,128)S(1)}, f32[32,768]{1,0:T(8,128)S(1)}, u32[]{:S(2)}, u32[]{:S(2)}) %collective-permute-start.3) | collective-permute-done | bytes 98336 | tf_op jit(solution)/shard_map/ppermute | solution.py:300
  19.3 2.8 %collective-permute-start.4 = (f32[32,768]{1,0:T(8,128)S(1)}, f32[32,768]{1,0:T(8,128)S(1)}, u32[]{:S(2)}, u32[]{:S(2)}) collective-permute-start(f32[32,768]{1,0:T(8,128)S(1)} %add.39), channel_id=1, source_target_pairs={{0,17},{1,2},{2,1},{3,18},{4,7},{5,20},{6,23},{7,4},{8,11},{9,24},... | collective-permute-start | bytes 294920 | tf_op jit(solution)/shard_map/ppermute | solution.py:300
  22.1 0.0 collective-permute-done.11
  22.1 1.6 %collective-permute-start.12 = (f32[32,768]{1,0:T(8,128)S(1)}, f32[32,768]{1,0:T(8,128)S(1)}, u32[]{:S(2)}, u32[]{:S(2)}) collective-permute-start(f32[32,768]{1,0:T(8,128)S(1)} %add.44), channel_id=1, source_target_pairs={{0,17},{1,2},{2,1},{3,18},{4,7},{5,20},{6,23},{7,4},{8,11},{9,24},... | collective-permute-start | bytes 294920 | tf_op jit(solution)/shard_map/ppermute | solution.py:300
  23.7 1.6 %collective-permute-done.4 = f32[32,768]{1,0:T(8,128)S(1)} collective-permute-done((f32[32,768]{1,0:T(8,128)S(1)}, f32[32,768]{1,0:T(8,128)S(1)}, u32[]{:S(2)}, u32[]{:S(2)}) %collective-permute-start.4) | collective-permute-done | bytes 98336 | tf_op jit(solution)/shard_map/ppermute | solution.py:300
  25.4 2.0 %collective-permute-start.5 = (f32[32,768]{1,0:T(8,128)S(1)}, f32[32,768]{1,0:T(8,128)S(1)}, u32[]{:S(2)}, u32[]{:S(2)}) collective-permute-start(f32[32,768]{1,0:T(8,128)S(1)} %add.40.a3.refs_4_), channel_id=1, source_target_pairs={{0,3},{1,8},{2,11},{3,0},{4,13},{5,6},{6,5},{7,14},{8,1},{9,10},{1... | collective-permute-start | bytes 294920 | tf_op jit(solution)/shard_map/ppermute | solution.py:300
  27.4 1.3 %collective-permute-done.12 = f32[32,768]{1,0:T(8,128)S(1)} collective-permute-done((f32[32,768]{1,0:T(8,128)S(1)}, f32[32,768]{1,0:T(8,128)S(1)}, u32[]{:S(2)}, u32[]{:S(2)}) %collective-permute-start.12) | collective-permute-done | bytes 98336 | tf_op jit(solution)/shard_map/ppermute | solution.py:300
  28.7 0.1 collective-permute-start.13
  28.8 0.5 %collective-permute-start.7 = (f32[32,768]{1,0:T(8,128)S(1)}, f32[32,768]{1,0:T(8,128)S(1)}, u32[]{:S(2)}, u32[]{:S(2)}) collective-permute-start(f32[32,768]{1,0:T(8,128)S(1)} %add.40.a3.refs_4_), channel_id=1, source_target_pairs={{0,1},{1,0},{2,3},{3,2},{4,5},{5,4},{6,7},{7,6},{8,9},{9,8},{10,11... | collective-permute-start | bytes 294920 | tf_op jit(solution)/shard_map/ppermute | solution.py:297
  29.3 0.4 collective-permute-done.5.p_ref.a2.refs_3_
  29.7 0.1 collective-permute-start.6
  29.8 0.3 collective-permute-done.13.b0.refs_2_
  30.1 0.2 collective-permute-done.7.a1.refs_1_
  30.2 0.8 %right_products.1 = (f32[32,256]{1,0:T(8,128)S(1)}, f32[32,32]{1,0:T(8,128)S(1)}) custom-call(f32[32,768]{1,0:T(8,128)S(1)} %collective-permute-done.7.a1.refs_1_, f32[32,768]{1,0:T(8,128)S(1)} %collective-permute-done.13.b0.refs_2_, f32[32,768]{1,0:T(8,128)S(1)} %add.40.a3.refs_4_, f32[32,768]{1,0:T(8,128)S(1)} %add.45.b1.refs_5_, ...), custom_call_target="tpu_custom_call" | custom-call | flops 226492416 | tf_op jit(solution)/shard_map/right_products/pallas_call | solution.py:264
  31.0 0.3 right_products_own.1.before
  31.3 0.0 collective-permute-done.6.p_ref.a0.refs_0_
  31.3 0.3 right_products_other.1
  31.6 1.5 %collective-permute-start.15 = (f32[32,256]{1,0:T(8,128)S(1)}, f32[32,256]{1,0:T(8,128)S(1)}, u32[]{:S(2)}, u32[]{:S(2)}) collective-permute-start(f32[32,256]{1,0:T(8,128)S(1)} %right_products_other.1), channel_id=1, source_target_pairs={{0,5},{1,4},{2,7},{3,6},{4,1},{5,0},{6,3},{7,2},{8,13},{9,12},{10,... | collective-permute-start | bytes 98312 | tf_op jit(solution)/shard_map/ppermute | solution.py:297
  33.1 0.3 collective-permute-start.14
  33.4 1.6 %factor_first_half.1.state_ref = f32[32,128]{1,0:T(8,128)S(1)} custom-call(f32[32,32]{1,0:T(8,128)S(1)} %get-tuple-element.34.gram_ref, f32[32,768]{1,0:T(8,128)S(1)} %collective-permute-done.6.p_ref.a0.refs_0_, f32[32,768]{1,0:T(8,128)S(1)} %collective-permute-done.5.p_ref.a2.refs_3_), custom_call_target="tpu_custom_call" | custom-call | flops 226492416 | tf_op jit(solution)/shard_map/factor_first_half/pallas_call | solution.py:264
  35.0 0.0 collective-permute-done.15
  35.0 0.0 collective-permute-done.14
  35.1 1.4 %collective-permute-start.17 = (f32[32,256]{1,0:T(8,128)S(1)}, f32[32,256]{1,0:T(8,128)S(1)}, u32[]{:S(2)}, u32[]{:S(2)}) collective-permute-start(f32[32,256]{1,0:T(8,128)S(1)} %add.46), channel_id=1, source_target_pairs={{0,9},{1,8},{2,11},{3,10},{4,13},{5,12},{6,15},{7,14},{8,1},{9,0},... | collective-permute-start | bytes 98312 | tf_op jit(solution)/shard_map/ppermute | solution.py:297
  36.5 0.2 collective-permute-start.16
  36.7 1.3 %factor_second_half.1.inv_ref = f32[32,32]{1,0:T(8,128)S(1)} custom-call(f32[32,128]{1,0:T(8,128)S(1)} %factor_first_half.1.state_ref), custom_call_target="tpu_custom_call" | custom-call | flops 226492416 | tf_op jit(solution)/shard_map/factor_second_half/pallas_call | solution.py:264
  38.0 0.4 collective-permute-done.17
  38.5 0.0 collective-permute-done.16
  38.5 2.9 %collective-permute-start.18 = (f32[32,256]{1,0:T(8,128)S(1)}, f32[32,256]{1,0:T(8,128)S(1)}, u32[]{:S(2)}, u32[]{:S(2)}) collective-permute-start(f32[32,256]{1,0:T(8,128)S(1)} %add.47.t0_ref), channel_id=1, source_target_pairs={{0,16},{1,17},{2,18},{3,19},{4,20},{5,21},{6,22},{7,23},{8,24},{9,... | collective-permute-start | bytes 98312 | tf_op jit(solution)/shard_map/ppermute | solution.py:297
  41.4 1.2 %left_factor.1 = (f32[32,4608]{1,0:T(8,128)}, bf16[4608,128]{1,0:T(8,128)(2,1)S(1)}) custom-call(f32[32,32]{1,0:T(8,128)S(1)} %factor_second_half.1.inv_ref, f32[32,768]{1,0:T(8,128)S(1)} %collective-permute-done.6.p_ref.a0.refs_0_, f32[32,768]{1,0:T(8,128)S(1)} %collective-permute-done.7.a1.refs_1_, f32[32,768]{1,0:T(8,128)S(1)} %collective-permute-done.13.b0.refs_2_, ...), custom_call_target="tpu_custom_call" | custom-call | flops 226492416 | tf_op jit(solution)/shard_map/left_factor/pallas_call | solution.py:264
  42.6 0.7 %collective-permute-done.18.t1_ref = f32[32,256]{1,0:T(8,128)S(1)} collective-permute-done((f32[32,256]{1,0:T(8,128)S(1)}, f32[32,256]{1,0:T(8,128)S(1)}, u32[]{:S(2)}, u32[]{:S(2)}) %collective-permute-start.18) | collective-permute-done | bytes 32800 | tf_op jit(solution)/shard_map/ppermute | solution.py:297
  43.4 2.5 %new_error.1 = (f32[4608,256]{1,0:T(8,128)}, f32[32,256]{1,0:T(8,128)}) custom-call(f32[32,256]{1,0:T(8,128)S(1)} %add.47.t0_ref, f32[32,256]{1,0:T(8,128)S(1)} %collective-permute-done.18.t1_ref, f32[32,32]{1,0:T(8,128)S(1)} %factor_second_half.1.inv_ref, bf16[4608,128]{1,0:T(8,128)(2,1)S(1)} %get-tuple-element.37.rows_ref, ...), custom_call_target="tpu_custom_call" | custom-call | flops 226492416 | tf_op jit(solution)/shard_map/new_error/pallas_call | solution.py:264
  (14 shorter events, 0.2 us)
Async XLA Ops:
  0.6 4.0 %copy-start = (f32[256,32]{0,1:T(8,128)S(1)}, f32[256,32]{0,1:T(8,128)}, u32[]{:S(2)}) copy-start(f32[256,32]{0,1:T(8,128)} %param.5) | copy-start | bytes 98308
  4.0 1.6 %collective-permute-start = (f32[2,32,768]{2,1,0:T(8,128)S(1)}, f32[2,32,768]{2,1,0:T(8,128)S(1)}, u32[]{:S(2)}, u32[]{:S(2)}) collective-permute-start(f32[2,32,768]{2,1,0:T(8,128)S(1)} %get-tuple-element.26), channel_id=1, source_target_pairs={{0,1},{1,0},{2,3},{3,2},{4,5},{5,4},{6,7},{7,6},{8,9},{9,8},{10,11... | collective-permute-start | bytes 589832 | tf_op jit(solution)/shard_map/ppermute | solution.py:297
  4.5 3.8 %collective-permute-start.8 = (f32[32,768]{1,0:T(8,128)S(1)}, f32[32,768]{1,0:T(8,128)S(1)}, u32[]{:S(2)}, u32[]{:S(2)}) collective-permute-start(f32[32,768]{1,0:T(8,128)S(1)} %get-tuple-element.32), channel_id=1, source_target_pairs={{0,1},{1,0},{2,3},{3,2},{4,5},{5,4},{6,7},{7,6},{8,9},{9,8},{10,11... | collective-permute-start | bytes 294920 | tf_op jit(solution)/shard_map/ppermute | solution.py:297
  5.6 5.0 %collective-permute-start.1 = (f32[32,768]{1,0:T(8,128)S(1)}, f32[32,768]{1,0:T(8,128)S(1)}, u32[]{:S(2)}, u32[]{:S(2)}) collective-permute-start(f32[32,768]{1,0:T(8,128)S(1)} %slice_bitcast_fusion), channel_id=1, source_target_pairs={{0,3},{1,8},{2,11},{3,0},{4,13},{5,6},{6,5},{7,14},{8,1},{9,10},{1... | collective-permute-start | bytes 294920 | tf_op jit(solution)/shard_map/ppermute | solution.py:300
  8.3 4.5 %collective-permute-start.9 = (f32[32,768]{1,0:T(8,128)S(1)}, f32[32,768]{1,0:T(8,128)S(1)}, u32[]{:S(2)}, u32[]{:S(2)}) collective-permute-start(f32[32,768]{1,0:T(8,128)S(1)} %add.41), channel_id=1, source_target_pairs={{0,3},{1,8},{2,11},{3,0},{4,13},{5,6},{6,5},{7,14},{8,1},{9,10},{1... | collective-permute-start | bytes 294920 | tf_op jit(solution)/shard_map/ppermute | solution.py:300
  10.6 4.5 %collective-permute-start.2 = (f32[32,768]{1,0:T(8,128)S(1)}, f32[32,768]{1,0:T(8,128)S(1)}, u32[]{:S(2)}, u32[]{:S(2)}) collective-permute-start(f32[32,768]{1,0:T(8,128)S(1)} %fusion), channel_id=1, source_target_pairs={{0,9},{1,4},{2,7},{3,10},{4,1},{5,12},{6,15},{7,2},{8,13},{9,0},{1... | collective-permute-start | bytes 294920 | tf_op jit(solution)/shard_map/ppermute | solution.py:300
  12.8 4.1 %collective-permute-start.10 = (f32[32,768]{1,0:T(8,128)S(1)}, f32[32,768]{1,0:T(8,128)S(1)}, u32[]{:S(2)}, u32[]{:S(2)}) collective-permute-start(f32[32,768]{1,0:T(8,128)S(1)} %add.42), channel_id=1, source_target_pairs={{0,9},{1,4},{2,7},{3,10},{4,1},{5,12},{6,15},{7,2},{8,13},{9,0},{1... | collective-permute-start | bytes 294920 | tf_op jit(solution)/shard_map/ppermute | solution.py:300
  15.1 4.1 %collective-permute-start.3 = (f32[32,768]{1,0:T(8,128)S(1)}, f32[32,768]{1,0:T(8,128)S(1)}, u32[]{:S(2)}, u32[]{:S(2)}) collective-permute-start(f32[32,768]{1,0:T(8,128)S(1)} %add.38), channel_id=1, source_target_pairs={{0,5},{1,16},{2,19},{3,6},{4,21},{5,0},{6,3},{7,22},{8,25},{9,12},... | collective-permute-start | bytes 294920 | tf_op jit(solution)/shard_map/ppermute | solution.py:300
  17.0 5.1 %collective-permute-start.11 = (f32[32,768]{1,0:T(8,128)S(1)}, f32[32,768]{1,0:T(8,128)S(1)}, u32[]{:S(2)}, u32[]{:S(2)}) collective-permute-start(f32[32,768]{1,0:T(8,128)S(1)} %add.43), channel_id=1, source_target_pairs={{0,5},{1,16},{2,19},{3,6},{4,21},{5,0},{6,3},{7,22},{8,25},{9,12},... | collective-permute-start | bytes 294920 | tf_op jit(solution)/shard_map/ppermute | solution.py:300
  19.3 6.1 %collective-permute-start.4 = (f32[32,768]{1,0:T(8,128)S(1)}, f32[32,768]{1,0:T(8,128)S(1)}, u32[]{:S(2)}, u32[]{:S(2)}) collective-permute-start(f32[32,768]{1,0:T(8,128)S(1)} %add.39), channel_id=1, source_target_pairs={{0,17},{1,2},{2,1},{3,18},{4,7},{5,20},{6,23},{7,4},{8,11},{9,24},... | collective-permute-start | bytes 294920 | tf_op jit(solution)/shard_map/ppermute | solution.py:300
  22.1 6.6 %collective-permute-start.12 = (f32[32,768]{1,0:T(8,128)S(1)}, f32[32,768]{1,0:T(8,128)S(1)}, u32[]{:S(2)}, u32[]{:S(2)}) collective-permute-start(f32[32,768]{1,0:T(8,128)S(1)} %add.44), channel_id=1, source_target_pairs={{0,17},{1,2},{2,1},{3,18},{4,7},{5,20},{6,23},{7,4},{8,11},{9,24},... | collective-permute-start | bytes 294920 | tf_op jit(solution)/shard_map/ppermute | solution.py:300
  25.4 4.3 %collective-permute-start.5 = (f32[32,768]{1,0:T(8,128)S(1)}, f32[32,768]{1,0:T(8,128)S(1)}, u32[]{:S(2)}, u32[]{:S(2)}) collective-permute-start(f32[32,768]{1,0:T(8,128)S(1)} %add.40.a3.refs_4_), channel_id=1, source_target_pairs={{0,3},{1,8},{2,11},{3,0},{4,13},{5,6},{6,5},{7,14},{8,1},{9,10},{1... | collective-permute-start | bytes 294920 | tf_op jit(solution)/shard_map/ppermute | solution.py:300
  28.7 1.4 %collective-permute-start.13 = (f32[32,768]{1,0:T(8,128)S(1)}, f32[32,768]{1,0:T(8,128)S(1)}, u32[]{:S(2)}, u32[]{:S(2)}) collective-permute-start(f32[32,768]{1,0:T(8,128)S(1)} %add.45.b1.refs_5_), channel_id=1, source_target_pairs={{0,1},{1,0},{2,3},{3,2},{4,5},{5,4},{6,7},{7,6},{8,9},{9,8},{10,11... | collective-permute-start | bytes 294920 | tf_op jit(solution)/shard_map/ppermute | solution.py:297
  28.8 1.4 %collective-permute-start.7 = (f32[32,768]{1,0:T(8,128)S(1)}, f32[32,768]{1,0:T(8,128)S(1)}, u32[]{:S(2)}, u32[]{:S(2)}) collective-permute-start(f32[32,768]{1,0:T(8,128)S(1)} %add.40.a3.refs_4_), channel_id=1, source_target_pairs={{0,1},{1,0},{2,3},{3,2},{4,5},{5,4},{6,7},{7,6},{8,9},{9,8},{10,11... | collective-permute-start | bytes 294920 | tf_op jit(solution)/shard_map/ppermute | solution.py:297
  29.7 1.6 %collective-permute-start.6 = (f32[32,768]{1,0:T(8,128)S(1)}, f32[32,768]{1,0:T(8,128)S(1)}, u32[]{:S(2)}, u32[]{:S(2)}) collective-permute-start(f32[32,768]{1,0:T(8,128)S(1)} %collective-permute-done.5.p_ref.a2.refs_3_), channel_id=1, source_target_pairs={{0,1},{1,0},{2,3},{3,2},{4,5},{5,4},{6,7},{7,6},{8,9},{9,8},{10,11... | collective-permute-start | bytes 294920 | tf_op jit(solution)/shard_map/ppermute | solution.py:297
  31.6 3.4 %collective-permute-start.15 = (f32[32,256]{1,0:T(8,128)S(1)}, f32[32,256]{1,0:T(8,128)S(1)}, u32[]{:S(2)}, u32[]{:S(2)}) collective-permute-start(f32[32,256]{1,0:T(8,128)S(1)} %right_products_other.1), channel_id=1, source_target_pairs={{0,5},{1,4},{2,7},{3,6},{4,1},{5,0},{6,3},{7,2},{8,13},{9,12},{10,... | collective-permute-start | bytes 98312 | tf_op jit(solution)/shard_map/ppermute | solution.py:297
  33.1 1.9 %collective-permute-start.14 = (f32[32,256]{1,0:T(8,128)S(1)}, f32[32,256]{1,0:T(8,128)S(1)}, u32[]{:S(2)}, u32[]{:S(2)}) collective-permute-start(f32[32,256]{1,0:T(8,128)S(1)} %right_products_other.1), channel_id=1, source_target_pairs={{0,1},{1,0},{2,3},{3,2},{4,5},{5,4},{6,7},{7,6},{8,9},{9,8},{10,11... | collective-permute-start | bytes 98312 | tf_op jit(solution)/shard_map/ppermute | solution.py:297
  35.1 3.4 %collective-permute-start.17 = (f32[32,256]{1,0:T(8,128)S(1)}, f32[32,256]{1,0:T(8,128)S(1)}, u32[]{:S(2)}, u32[]{:S(2)}) collective-permute-start(f32[32,256]{1,0:T(8,128)S(1)} %add.46), channel_id=1, source_target_pairs={{0,9},{1,8},{2,11},{3,10},{4,13},{5,12},{6,15},{7,14},{8,1},{9,0},... | collective-permute-start | bytes 98312 | tf_op jit(solution)/shard_map/ppermute | solution.py:297
  36.5 2.0 %collective-permute-start.16 = (f32[32,256]{1,0:T(8,128)S(1)}, f32[32,256]{1,0:T(8,128)S(1)}, u32[]{:S(2)}, u32[]{:S(2)}) collective-permute-start(f32[32,256]{1,0:T(8,128)S(1)} %add.46), channel_id=1, source_target_pairs={{0,1},{1,0},{2,3},{3,2},{4,5},{5,4},{6,7},{7,6},{8,9},{9,8},{10,11... | collective-permute-start | bytes 98312 | tf_op jit(solution)/shard_map/ppermute | solution.py:297
  38.5 4.9 %collective-permute-start.18 = (f32[32,256]{1,0:T(8,128)S(1)}, f32[32,256]{1,0:T(8,128)S(1)}, u32[]{:S(2)}, u32[]{:S(2)}) collective-permute-start(f32[32,256]{1,0:T(8,128)S(1)} %add.47.t0_ref), channel_id=1, source_target_pairs={{0,16},{1,17},{2,18},{3,19},{4,20},{5,21},{6,22},{7,23},{8,24},{9,... | collective-permute-start | bytes 98312 | tf_op jit(solution)/shard_map/ppermute | solution.py:297

commit v7 on v6

--- a/solution.py
+++ b/solution.py
@@ -13,6 +13,7 @@
 AXES = ("dp", "tensor")
 LIMIT = 12 * 2**20
 UNITS = 6
+FIRST = 13
 
 
 def split(x, terms):
@@ -157,23 +158,30 @@
     return pl.ds(n * rows if isinstance(n, int) else pl.multiple_of(n * rows, rows), rows)
 
 
-def right_early_kernel(a1, b0, a3, b1, mh_ref, ml_ref, mh2_ref, ml2_ref, t_ref, gram_ref, *, devices):
+def right_early_kernel(a1, b0, a3, b1, a2, mh_ref, ml_ref, mh2_ref, ml2_ref, t_ref, gram_ref, *, devices):
     rank, rows = a1.shape
     (_, their_bit), (_, bit) = sides(devices)
     t = gram = 0.0
-    for ref, unit, hs, ls in ((a3, bit, mh2_ref, ml2_ref), (b1, 2, mh2_ref, ml2_ref), (a1, their_bit, mh_ref, ml_ref), (b0, 2, mh_ref, ml_ref)):
+    for ref, unit, hs, ls in (
+        (a3, bit, mh2_ref, ml2_ref),
+        (b1, 2, mh2_ref, ml2_ref),
+        (a1, their_bit, mh_ref, ml_ref),
+        (b0, 2, mh_ref, ml_ref),
+        (a2, 1 - bit, mh2_ref, ml2_ref),
+    ):
         at = unit_at(unit, rows)
         p = terms_of((ref,))
         t = t + dot(p, hs[at], (1, 0)) + dot(p, ls[at], (1, 0))
-        gram = gram + square(p, rank)
+        if ref is not a2:
+            gram = gram + square(p, rank)
     t_ref[...] = fold(t, rank)
     gram_ref[...] = gram
 
 
-def right_kernel(p_ref, mh_ref, ml_ref, before, t_ref, *, side, devices):
+def right_kernel(p_ref, mh_ref, ml_ref, before, t_ref, *, devices):
     rank, rows = p_ref.shape
     p = terms_of((p_ref,))
-    at = unit_at(1 - sides(devices)[side][1], rows)
+    at = unit_at(1 - sides(devices)[0][1], rows)
     t_ref[...] = before[...] + fold(dot(p, mh_ref[at], (1, 0)) + dot(p, ml_ref[at], (1, 0)), rank)
 
 
@@ -192,12 +200,12 @@
     row = lax.broadcasted_iota(jnp.int32, (rank, 128), 0)
     lane = lax.broadcasted_iota(jnp.int32, (rank, 128), 1)
     eye = (lane == row + rank).astype(F32)
-    state_ref[...] = eliminate(jnp.concatenate([gram, eye[:, rank:]], axis=1), range(rank // 2))
+    state_ref[...] = eliminate(jnp.concatenate([gram, eye[:, rank:]], axis=1), range(FIRST))
 
 
 def inverse_kernel(state_ref, inv_ref):
     rank = state_ref.shape[0]
-    a = eliminate(state_ref[...], range(rank // 2, rank - 1))
+    a = eliminate(state_ref[...], range(FIRST, rank - 1))
     row = lax.broadcasted_iota(jnp.int32, a.shape, 0)
     lane = lax.broadcasted_iota(jnp.int32, a.shape, 1)
     pivots = jnp.sum(jnp.where(row == lane, a, 0.0), axis=1, keepdims=True)
@@ -225,18 +233,18 @@
         copy.wait()
 
 
-def error_kernel(t0_ref, t1_ref, inv_ref, rows_ref, m_ref, m2_ref, out_hbm, q_hbm, buf, q_buf, sems, q_sem, *, replicas, block, devices):
+def error_kernel(t0_ref, t1_ref, inv_ref, rows_ref, m_ref, m2_ref, out_hbm, q_hbm, buf, q_buf, sems, q_sem, *, replicas, cuts, devices):
     t = (t0_ref[...] + t1_ref[...]) / replicas
     u, v = split(t, 2)
     terms = stack([u, u, v, v])
     half = m_ref.shape[0]
     copies = []
     for source, side, shift in ((m_ref, 0, 0), (m2_ref, 1, half)):
-        for at in range(0, half, block):
-            here = slice(shift + at, shift + at + block)
-            buf[here] = source[at : at + block] - dot(rows_ref[here], terms, (1, 0))
-            to = pl.ds(pl.multiple_of(sides(devices)[side][0] * half + at, block), block)
-            copies.append(pltpu.make_async_copy(buf.at[pl.ds(shift + at, block)], out_hbm.at[to], sems.at[len(copies)]))
+        for at, end in zip(cuts[:-1], cuts[1:], strict=True):
+            here = slice(shift + at, shift + end)
+            buf[here] = source[at:end] - dot(rows_ref[here], terms, (1, 0))
+            to = pl.ds(pl.multiple_of(sides(devices)[side][0] * half + at, 16), end - at)
+            copies.append(pltpu.make_async_copy(buf.at[pl.ds(shift + at, end - at)], out_hbm.at[to], sems.at[len(copies)]))
             copies[-1].start()
     q_buf[...] = dot(six_left(inv_ref[...]), six_right(t), (1, 0))
     copies.append(pltpu.make_async_copy(q_buf, q_hbm, q_sem))
@@ -314,18 +322,17 @@
         "right_products",
         work,
         out_shape=(wide, small),
-        in_specs=[VMEM] * 8,
+        in_specs=[VMEM] * 9,
         out_specs=(VMEM, VMEM),
-    )(a1, b0, a3, b1, mh, ml, mh2, ml2)
-    for side, name, x, hs, ls in ((1, "own", a2, mh2, ml2), (0, "other", a0, mh, ml)):
-        t = call(
-            functools.partial(right_kernel, side=side, devices=devices),
-            "right_products_" + name,
-            work,
-            out_shape=wide,
-            in_specs=[VMEM] * 4,
-            out_specs=VMEM,
-        )(x, hs, ls, t)
+    )(a1, b0, a3, b1, a2, mh, ml, mh2, ml2)
+    t = call(
+        functools.partial(right_kernel, devices=devices),
+        "right_products_last",
+        work,
+        out_shape=wide,
+        in_specs=[VMEM] * 4,
+        out_specs=VMEM,
+    )(a0, mh, ml, t)
 
     state = call(
         factor_kernel,
@@ -357,9 +364,10 @@
                 t, _ = lax.optimization_barrier((t, beside[n - 1]))
         parts = (swap(t, 1), swap(t, 1 ^ bit)) if n < turns else (t, swap(t, bit))
 
-    block = rows // 2
+    half = depth // 2
+    cuts = [half * n // 18 // 16 * 16 for n in (0, 1, 3, 6, 10, 14, 18)]
     error, q_new = call(
-        functools.partial(error_kernel, replicas=replicas, block=block, devices=devices),
+        functools.partial(error_kernel, replicas=replicas, cuts=cuts, devices=devices),
         "new_error",
         work,
         out_shape=(pltpu.HBM((depth, columns), F32), pltpu.HBM((rank, columns), F32)),
@@ -368,7 +376,7 @@
         scratch_shapes=[
             pltpu.VMEM((depth, columns), F32),
             pltpu.VMEM((rank, columns), F32),
-            pltpu.SemaphoreType.DMA((depth // block,)),
+            pltpu.SemaphoreType.DMA((2 * len(cuts) - 2,)),
             pltpu.SemaphoreType.DMA(()),
         ],
     )(*parts, inverse, hat_rows, m, m2)

time: 46 us -> 46 us (level)
    pallas_call x9 -> x8, Pallas kernels: 12.3 us -> 12.1 us  [call(): made(*(pltpu.with_memory_space_constraint(x, space) for x, space in zip(a...]
  transfers between devices with their start and end apart: 19 -> 19, of which waited for: 12 -> 13; matrix products, arithmetic and copies ran while one was open for 0% -> 0% of each run, Pallas kernels for 13% -> 13%
where the time goes in v7:
time: 46 us; the launch traced here: 45.8 us
  starting transfers between devices  23.3 us (51%)
  Pallas kernels  12.1 us (26%)
  waiting for transfers between devices  9.5 us (21%)
  between operations  0.77 us (2%)
    ppermute x9, starting transfers between devices, cross(): lax.ppermute(x, AXES, [(i, i ^ 1 ^ bits[role(i)]) for i in range(devices)])  15.5 us
    pallas_call x8, Pallas kernels, call(): made(*(pltpu.with_memory_space_constraint(x, space) for x, space in zip(a...  12.1 us
    ppermute x10, starting transfers between devices, swap(): return lax.ppermute(x, AXES, [(i, i ^ bit) for i in range(devices)])  7.86 us
    ppermute x9, waiting for transfers between devices, cross(): lax.ppermute(x, AXES, [(i, i ^ 1 ^ bits[role(i)]) for i in range(devices)])  7.85 us
    ppermute x10, waiting for transfers between devices, swap(): return lax.ppermute(x, AXES, [(i, i ^ bit) for i in range(devices)])  1.65 us
  transfers between devices with their start and end apart: 19, of which 13 were waited for; matrix products, arithmetic and copies ran while one was open for 0% of the time, Pallas kernels for 13%

profile of v7, /device:TPU:0, one launch (start us, length us, event | category | flops | bytes accessed | tf_op | source)
XLA Modules:
  0.0 45.8 jit_solution(2594712565982142613)
XLA Ops:
  0.6 0.0 copy-start
  0.6 3.4 %left_products.1 = (f32[2304,256]{1,0:T(8,128)S(1)}, bf16[2304,256]{1,0:T(8,128)(2,1)S(1)}, bf16[2304,256]{1,0:T(8,128)(2,1)S(1)}, f32[2304,256]{1,0:T(8,128)S(1...) custom-call(f32[32,256]{1,0:T(8,128)} %bitcast.12, ...), custom_call_target="tpu_custom_call" | custom-call | flops 226492416 | tf_op jit(solution)/shard_map/left_products/pallas_call | solution.py:272
  4.0 0.5 %collective-permute-start = (f32[2,32,768]{2,1,0:T(8,128)S(1)}, f32[2,32,768]{2,1,0:T(8,128)S(1)}, u32[]{:S(2)}, u32[]{:S(2)}) collective-permute-start(f32[2,32,768]{2,1,0:T(8,128)S(1)} %get-tuple-element.26), channel_id=1, source_target_pairs={{0,1},{1,0},{2,3},{3,2},{4,5},{5,4},{6,7},{7,6},{8,9},{9,8},{10,11... | collective-permute-start | bytes 589832 | tf_op jit(solution)/shard_map/ppermute | solution.py:305
  4.5 0.1 collective-permute-start.8
  4.6 0.0 copy-done
  4.6 0.9 %left_products_rest.1 = (f32[2304,256]{1,0:T(8,128)S(1)}, bf16[2304,256]{1,0:T(8,128)(2,1)S(1)}, bf16[2304,256]{1,0:T(8,128)(2,1)S(1)}, f32[2,32,768]{2,1,0:T(8,128)S(1)}, f32[32,768]{1,0:T(8,128)S(1)}) custom-call(f32[32,256]{1,0:T(8,128)S(1)} %bitcast.13, f32[2304,256]{1,0:T(8,128)S(1)} %get-tuple-element.23.e_ref, ...), custom_call_target="tpu_custom_call" | custom-call | flops 226492416 | tf_op jit(solution)/shard_map/left_products_rest/pallas_call | solution.py:272
  5.5 0.1 collective-permute-done
  5.6 2.7 %collective-permute-start.1 = (f32[32,768]{1,0:T(8,128)S(1)}, f32[32,768]{1,0:T(8,128)S(1)}, u32[]{:S(2)}, u32[]{:S(2)}) collective-permute-start(f32[32,768]{1,0:T(8,128)S(1)} %slice_bitcast_fusion), channel_id=1, source_target_pairs={{0,3},{1,8},{2,11},{3,0},{4,13},{5,6},{6,5},{7,14},{8,1},{9,10},{1... | collective-permute-start | bytes 294920 | tf_op jit(solution)/shard_map/ppermute | solution.py:308
  8.3 0.0 collective-permute-done.8
  8.3 0.2 collective-permute-start.9
  8.5 2.1 %collective-permute-done.1 = f32[32,768]{1,0:T(8,128)S(1)} collective-permute-done((f32[32,768]{1,0:T(8,128)S(1)}, f32[32,768]{1,0:T(8,128)S(1)}, u32[]{:S(2)}, u32[]{:S(2)}) %collective-permute-start.1) | collective-permute-done | bytes 98336 | tf_op jit(solution)/shard_map/ppermute | solution.py:308
  10.6 2.2 %collective-permute-start.2 = (f32[32,768]{1,0:T(8,128)S(1)}, f32[32,768]{1,0:T(8,128)S(1)}, u32[]{:S(2)}, u32[]{:S(2)}) collective-permute-start(f32[32,768]{1,0:T(8,128)S(1)} %fusion), channel_id=1, source_target_pairs={{0,9},{1,4},{2,7},{3,10},{4,1},{5,12},{6,15},{7,2},{8,13},{9,0},{1... | collective-permute-start | bytes 294920 | tf_op jit(solution)/shard_map/ppermute | solution.py:308
  12.8 0.0 collective-permute-done.9
  12.8 1.2 %collective-permute-start.10 = (f32[32,768]{1,0:T(8,128)S(1)}, f32[32,768]{1,0:T(8,128)S(1)}, u32[]{:S(2)}, u32[]{:S(2)}) collective-permute-start(f32[32,768]{1,0:T(8,128)S(1)} %add.42), channel_id=1, source_target_pairs={{0,9},{1,4},{2,7},{3,10},{4,1},{5,12},{6,15},{7,2},{8,13},{9,0},{1... | collective-permute-start | bytes 294920 | tf_op jit(solution)/shard_map/ppermute | solution.py:308
  14.1 1.0 %collective-permute-done.2 = f32[32,768]{1,0:T(8,128)S(1)} collective-permute-done((f32[32,768]{1,0:T(8,128)S(1)}, f32[32,768]{1,0:T(8,128)S(1)}, u32[]{:S(2)}, u32[]{:S(2)}) %collective-permute-start.2) | collective-permute-done | bytes 98336 | tf_op jit(solution)/shard_map/ppermute | solution.py:308
  15.1 1.5 %collective-permute-start.3 = (f32[32,768]{1,0:T(8,128)S(1)}, f32[32,768]{1,0:T(8,128)S(1)}, u32[]{:S(2)}, u32[]{:S(2)}) collective-permute-start(f32[32,768]{1,0:T(8,128)S(1)} %add.38), channel_id=1, source_target_pairs={{0,5},{1,16},{2,19},{3,6},{4,21},{5,0},{6,3},{7,22},{8,25},{9,12},... | collective-permute-start | bytes 294920 | tf_op jit(solution)/shard_map/ppermute | solution.py:308
  16.6 0.4 collective-permute-done.10
  17.0 1.3 %collective-permute-start.11 = (f32[32,768]{1,0:T(8,128)S(1)}, f32[32,768]{1,0:T(8,128)S(1)}, u32[]{:S(2)}, u32[]{:S(2)}) collective-permute-start(f32[32,768]{1,0:T(8,128)S(1)} %add.43), channel_id=1, source_target_pairs={{0,5},{1,16},{2,19},{3,6},{4,21},{5,0},{6,3},{7,22},{8,25},{9,12},... | collective-permute-start | bytes 294920 | tf_op jit(solution)/shard_map/ppermute | solution.py:308
  18.2 1.0 %collective-permute-done.3 = f32[32,768]{1,0:T(8,128)S(1)} collective-permute-done((f32[32,768]{1,0:T(8,128)S(1)}, f32[32,768]{1,0:T(8,128)S(1)}, u32[]{:S(2)}, u32[]{:S(2)}) %collective-permute-start.3) | collective-permute-done | bytes 98336 | tf_op jit(solution)/shard_map/ppermute | solution.py:308
  19.3 2.8 %collective-permute-start.4 = (f32[32,768]{1,0:T(8,128)S(1)}, f32[32,768]{1,0:T(8,128)S(1)}, u32[]{:S(2)}, u32[]{:S(2)}) collective-permute-start(f32[32,768]{1,0:T(8,128)S(1)} %add.39), channel_id=1, source_target_pairs={{0,17},{1,2},{2,1},{3,18},{4,7},{5,20},{6,23},{7,4},{8,11},{9,24},... | collective-permute-start | bytes 294920 | tf_op jit(solution)/shard_map/ppermute | solution.py:308
  22.1 0.0 collective-permute-done.11
  22.1 1.6 %collective-permute-start.12 = (f32[32,768]{1,0:T(8,128)S(1)}, f32[32,768]{1,0:T(8,128)S(1)}, u32[]{:S(2)}, u32[]{:S(2)}) collective-permute-start(f32[32,768]{1,0:T(8,128)S(1)} %add.44), channel_id=1, source_target_pairs={{0,17},{1,2},{2,1},{3,18},{4,7},{5,20},{6,23},{7,4},{8,11},{9,24},... | collective-permute-start | bytes 294920 | tf_op jit(solution)/shard_map/ppermute | solution.py:308
  23.7 1.6 %collective-permute-done.4 = f32[32,768]{1,0:T(8,128)S(1)} collective-permute-done((f32[32,768]{1,0:T(8,128)S(1)}, f32[32,768]{1,0:T(8,128)S(1)}, u32[]{:S(2)}, u32[]{:S(2)}) %collective-permute-start.4) | collective-permute-done | bytes 98336 | tf_op jit(solution)/shard_map/ppermute | solution.py:308
  25.4 2.0 %collective-permute-start.5 = (f32[32,768]{1,0:T(8,128)S(1)}, f32[32,768]{1,0:T(8,128)S(1)}, u32[]{:S(2)}, u32[]{:S(2)}) collective-permute-start(f32[32,768]{1,0:T(8,128)S(1)} %add.40.a3.refs_4_), channel_id=1, source_target_pairs={{0,3},{1,8},{2,11},{3,0},{4,13},{5,6},{6,5},{7,14},{8,1},{9,10},{1... | collective-permute-start | bytes 294920 | tf_op jit(solution)/shard_map/ppermute | solution.py:308
  27.4 1.3 %collective-permute-done.12 = f32[32,768]{1,0:T(8,128)S(1)} collective-permute-done((f32[32,768]{1,0:T(8,128)S(1)}, f32[32,768]{1,0:T(8,128)S(1)}, u32[]{:S(2)}, u32[]{:S(2)}) %collective-permute-start.12) | collective-permute-done | bytes 98336 | tf_op jit(solution)/shard_map/ppermute | solution.py:308
  28.7 0.1 collective-permute-start.13
  28.8 0.5 %collective-permute-start.7 = (f32[32,768]{1,0:T(8,128)S(1)}, f32[32,768]{1,0:T(8,128)S(1)}, u32[]{:S(2)}, u32[]{:S(2)}) collective-permute-start(f32[32,768]{1,0:T(8,128)S(1)} %add.40.a3.refs_4_), channel_id=1, source_target_pairs={{0,1},{1,0},{2,3},{3,2},{4,5},{5,4},{6,7},{7,6},{8,9},{9,8},{10,11... | collective-permute-start | bytes 294920 | tf_op jit(solution)/shard_map/ppermute | solution.py:305
  29.3 0.4 collective-permute-done.5.a2.refs_3_
  29.7 0.1 collective-permute-start.6
  29.8 0.3 collective-permute-done.13.b0.refs_2_
  30.1 0.2 collective-permute-done.7.a1.refs_1_
  30.2 0.9 %right_products.1 = (f32[32,256]{1,0:T(8,128)S(1)}, f32[32,32]{1,0:T(8,128)S(1)}) custom-call(f32[32,768]{1,0:T(8,128)S(1)} %collective-permute-done.7.a1.refs_1_, f32[32,768]{1,0:T(8,128)S(1)} %collective-permute-done.13.b0.refs_2_, f32[32,768]{1,0:T(8,128)S(1)} %add.40.a3.refs_4_, f32[32,768]{1,0:T(8,128)S(1)} %add.45.b1.refs_5_, ...), custom_call_target="tpu_custom_call" | custom-call | flops 226492416 | tf_op jit(solution)/shard_map/right_products/pallas_call | solution.py:272
  31.2 0.0 collective-permute-done.6.p_ref.a0.refs_0_
  31.2 0.3 right_products_last.1
  31.5 1.7 %collective-permute-start.15 = (f32[32,256]{1,0:T(8,128)S(1)}, f32[32,256]{1,0:T(8,128)S(1)}, u32[]{:S(2)}, u32[]{:S(2)}) collective-permute-start(f32[32,256]{1,0:T(8,128)S(1)} %right_products_last.1), channel_id=1, source_target_pairs={{0,5},{1,4},{2,7},{3,6},{4,1},{5,0},{6,3},{7,2},{8,13},{9,12},{10,... | collective-permute-start | bytes 98312 | tf_op jit(solution)/shard_map/ppermute | solution.py:305
  33.1 0.2 collective-permute-start.14
  33.3 1.4 %factor_first_half.1.state_ref = f32[32,128]{1,0:T(8,128)S(1)} custom-call(f32[32,32]{1,0:T(8,128)S(1)} %get-tuple-element.34.gram_ref, f32[32,768]{1,0:T(8,128)S(1)} %collective-permute-done.6.p_ref.a0.refs_0_, f32[32,768]{1,0:T(8,128)S(1)} %collective-permute-done.5.a2.refs_3_), custom_call_target="tpu_custom_call" | custom-call | flops 226492416 | tf_op jit(solution)/shard_map/factor_first_half/pallas_call | solution.py:272
  34.6 0.2 collective-permute-done.15
  34.9 0.0 collective-permute-done.14
  34.9 1.3 %collective-permute-start.17 = (f32[32,256]{1,0:T(8,128)S(1)}, f32[32,256]{1,0:T(8,128)S(1)}, u32[]{:S(2)}, u32[]{:S(2)}) collective-permute-start(f32[32,256]{1,0:T(8,128)S(1)} %add.46), channel_id=1, source_target_pairs={{0,9},{1,8},{2,11},{3,10},{4,13},{5,12},{6,15},{7,14},{8,1},{9,0},... | collective-permute-start | bytes 98312 | tf_op jit(solution)/shard_map/ppermute | solution.py:305
  36.2 0.3 collective-permute-start.16
  36.5 1.6 %factor_second_half.1.inv_ref = f32[32,32]{1,0:T(8,128)S(1)} custom-call(f32[32,128]{1,0:T(8,128)S(1)} %factor_first_half.1.state_ref), custom_call_target="tpu_custom_call" | custom-call | flops 226492416 | tf_op jit(solution)/shard_map/factor_second_half/pallas_call | solution.py:272
  38.1 0.2 collective-permute-done.17
  38.3 0.0 collective-permute-done.16
  38.3 3.1 %collective-permute-start.18 = (f32[32,256]{1,0:T(8,128)S(1)}, f32[32,256]{1,0:T(8,128)S(1)}, u32[]{:S(2)}, u32[]{:S(2)}) collective-permute-start(f32[32,256]{1,0:T(8,128)S(1)} %add.47.t0_ref), channel_id=1, source_target_pairs={{0,16},{1,17},{2,18},{3,19},{4,20},{5,21},{6,22},{7,23},{8,24},{9,... | collective-permute-start | bytes 98312 | tf_op jit(solution)/shard_map/ppermute | solution.py:305
  41.4 1.2 %left_factor.1 = (f32[32,4608]{1,0:T(8,128)}, bf16[4608,128]{1,0:T(8,128)(2,1)S(1)}) custom-call(f32[32,32]{1,0:T(8,128)S(1)} %factor_second_half.1.inv_ref, f32[32,768]{1,0:T(8,128)S(1)} %collective-permute-done.6.p_ref.a0.refs_0_, f32[32,768]{1,0:T(8,128)S(1)} %collective-permute-done.7.a1.refs_1_, f32[32,768]{1,0:T(8,128)S(1)} %collective-permute-done.13.b0.refs_2_, ...), custom_call_target="tpu_custom_call" | custom-call | flops 226492416 | tf_op jit(solution)/shard_map/left_factor/pallas_call | solution.py:272
  42.7 0.7 %collective-permute-done.18.t1_ref = f32[32,256]{1,0:T(8,128)S(1)} collective-permute-done((f32[32,256]{1,0:T(8,128)S(1)}, f32[32,256]{1,0:T(8,128)S(1)}, u32[]{:S(2)}, u32[]{:S(2)}) %collective-permute-start.18) | collective-permute-done | bytes 32800 | tf_op jit(solution)/shard_map/ppermute | solution.py:305
  43.3 2.5 %new_error.1 = (f32[4608,256]{1,0:T(8,128)}, f32[32,256]{1,0:T(8,128)}) custom-call(f32[32,256]{1,0:T(8,128)S(1)} %add.47.t0_ref, f32[32,256]{1,0:T(8,128)S(1)} %collective-permute-done.18.t1_ref, f32[32,32]{1,0:T(8,128)S(1)} %factor_second_half.1.inv_ref, bf16[4608,128]{1,0:T(8,128)(2,1)S(1)} %get-tuple-element.37.rows_ref, ...), custom_call_target="tpu_custom_call" | custom-call | flops 226492416 | tf_op jit(solution)/shard_map/new_error/pallas_call | solution.py:272
  (13 shorter events, 0.2 us)
Async XLA Ops:
  0.6 4.0 %copy-start = (f32[256,32]{0,1:T(8,128)S(1)}, f32[256,32]{0,1:T(8,128)}, u32[]{:S(2)}) copy-start(f32[256,32]{0,1:T(8,128)} %param.5) | copy-start | bytes 98308
  4.0 1.6 %collective-permute-start = (f32[2,32,768]{2,1,0:T(8,128)S(1)}, f32[2,32,768]{2,1,0:T(8,128)S(1)}, u32[]{:S(2)}, u32[]{:S(2)}) collective-permute-start(f32[2,32,768]{2,1,0:T(8,128)S(1)} %get-tuple-element.26), channel_id=1, source_target_pairs={{0,1},{1,0},{2,3},{3,2},{4,5},{5,4},{6,7},{7,6},{8,9},{9,8},{10,11... | collective-permute-start | bytes 589832 | tf_op jit(solution)/shard_map/ppermute | solution.py:305
  4.5 3.8 %collective-permute-start.8 = (f32[32,768]{1,0:T(8,128)S(1)}, f32[32,768]{1,0:T(8,128)S(1)}, u32[]{:S(2)}, u32[]{:S(2)}) collective-permute-start(f32[32,768]{1,0:T(8,128)S(1)} %get-tuple-element.30), channel_id=1, source_target_pairs={{0,1},{1,0},{2,3},{3,2},{4,5},{5,4},{6,7},{7,6},{8,9},{9,8},{10,11... | collective-permute-start | bytes 294920 | tf_op jit(solution)/shard_map/ppermute | solution.py:305
  5.6 5.0 %collective-permute-start.1 = (f32[32,768]{1,0:T(8,128)S(1)}, f32[32,768]{1,0:T(8,128)S(1)}, u32[]{:S(2)}, u32[]{:S(2)}) collective-permute-start(f32[32,768]{1,0:T(8,128)S(1)} %slice_bitcast_fusion), channel_id=1, source_target_pairs={{0,3},{1,8},{2,11},{3,0},{4,13},{5,6},{6,5},{7,14},{8,1},{9,10},{1... | collective-permute-start | bytes 294920 | tf_op jit(solution)/shard_map/ppermute | solution.py:308
  8.3 4.5 %collective-permute-start.9 = (f32[32,768]{1,0:T(8,128)S(1)}, f32[32,768]{1,0:T(8,128)S(1)}, u32[]{:S(2)}, u32[]{:S(2)}) collective-permute-start(f32[32,768]{1,0:T(8,128)S(1)} %add.41), channel_id=1, source_target_pairs={{0,3},{1,8},{2,11},{3,0},{4,13},{5,6},{6,5},{7,14},{8,1},{9,10},{1... | collective-permute-start | bytes 294920 | tf_op jit(solution)/shard_map/ppermute | solution.py:308
  10.6 4.5 %collective-permute-start.2 = (f32[32,768]{1,0:T(8,128)S(1)}, f32[32,768]{1,0:T(8,128)S(1)}, u32[]{:S(2)}, u32[]{:S(2)}) collective-permute-start(f32[32,768]{1,0:T(8,128)S(1)} %fusion), channel_id=1, source_target_pairs={{0,9},{1,4},{2,7},{3,10},{4,1},{5,12},{6,15},{7,2},{8,13},{9,0},{1... | collective-permute-start | bytes 294920 | tf_op jit(solution)/shard_map/ppermute | solution.py:308
  12.8 4.1 %collective-permute-start.10 = (f32[32,768]{1,0:T(8,128)S(1)}, f32[32,768]{1,0:T(8,128)S(1)}, u32[]{:S(2)}, u32[]{:S(2)}) collective-permute-start(f32[32,768]{1,0:T(8,128)S(1)} %add.42), channel_id=1, source_target_pairs={{0,9},{1,4},{2,7},{3,10},{4,1},{5,12},{6,15},{7,2},{8,13},{9,0},{1... | collective-permute-start | bytes 294920 | tf_op jit(solution)/shard_map/ppermute | solution.py:308
  15.1 4.1 %collective-permute-start.3 = (f32[32,768]{1,0:T(8,128)S(1)}, f32[32,768]{1,0:T(8,128)S(1)}, u32[]{:S(2)}, u32[]{:S(2)}) collective-permute-start(f32[32,768]{1,0:T(8,128)S(1)} %add.38), channel_id=1, source_target_pairs={{0,5},{1,16},{2,19},{3,6},{4,21},{5,0},{6,3},{7,22},{8,25},{9,12},... | collective-permute-start | bytes 294920 | tf_op jit(solution)/shard_map/ppermute | solution.py:308
  17.0 5.1 %collective-permute-start.11 = (f32[32,768]{1,0:T(8,128)S(1)}, f32[32,768]{1,0:T(8,128)S(1)}, u32[]{:S(2)}, u32[]{:S(2)}) collective-permute-start(f32[32,768]{1,0:T(8,128)S(1)} %add.43), channel_id=1, source_target_pairs={{0,5},{1,16},{2,19},{3,6},{4,21},{5,0},{6,3},{7,22},{8,25},{9,12},... | collective-permute-start | bytes 294920 | tf_op jit(solution)/shard_map/ppermute | solution.py:308
  19.3 6.1 %collective-permute-start.4 = (f32[32,768]{1,0:T(8,128)S(1)}, f32[32,768]{1,0:T(8,128)S(1)}, u32[]{:S(2)}, u32[]{:S(2)}) collective-permute-start(f32[32,768]{1,0:T(8,128)S(1)} %add.39), channel_id=1, source_target_pairs={{0,17},{1,2},{2,1},{3,18},{4,7},{5,20},{6,23},{7,4},{8,11},{9,24},... | collective-permute-start | bytes 294920 | tf_op jit(solution)/shard_map/ppermute | solution.py:308
  22.1 6.6 %collective-permute-start.12 = (f32[32,768]{1,0:T(8,128)S(1)}, f32[32,768]{1,0:T(8,128)S(1)}, u32[]{:S(2)}, u32[]{:S(2)}) collective-permute-start(f32[32,768]{1,0:T(8,128)S(1)} %add.44), channel_id=1, source_target_pairs={{0,17},{1,2},{2,1},{3,18},{4,7},{5,20},{6,23},{7,4},{8,11},{9,24},... | collective-permute-start | bytes 294920 | tf_op jit(solution)/shard_map/ppermute | solution.py:308
  25.4 4.3 %collective-permute-start.5 = (f32[32,768]{1,0:T(8,128)S(1)}, f32[32,768]{1,0:T(8,128)S(1)}, u32[]{:S(2)}, u32[]{:S(2)}) collective-permute-start(f32[32,768]{1,0:T(8,128)S(1)} %add.40.a3.refs_4_), channel_id=1, source_target_pairs={{0,3},{1,8},{2,11},{3,0},{4,13},{5,6},{6,5},{7,14},{8,1},{9,10},{1... | collective-permute-start | bytes 294920 | tf_op jit(solution)/shard_map/ppermute | solution.py:308
  28.7 1.4 %collective-permute-start.13 = (f32[32,768]{1,0:T(8,128)S(1)}, f32[32,768]{1,0:T(8,128)S(1)}, u32[]{:S(2)}, u32[]{:S(2)}) collective-permute-start(f32[32,768]{1,0:T(8,128)S(1)} %add.45.b1.refs_5_), channel_id=1, source_target_pairs={{0,1},{1,0},{2,3},{3,2},{4,5},{5,4},{6,7},{7,6},{8,9},{9,8},{10,11... | collective-permute-start | bytes 294920 | tf_op jit(solution)/shard_map/ppermute | solution.py:305
  28.8 1.4 %collective-permute-start.7 = (f32[32,768]{1,0:T(8,128)S(1)}, f32[32,768]{1,0:T(8,128)S(1)}, u32[]{:S(2)}, u32[]{:S(2)}) collective-permute-start(f32[32,768]{1,0:T(8,128)S(1)} %add.40.a3.refs_4_), channel_id=1, source_target_pairs={{0,1},{1,0},{2,3},{3,2},{4,5},{5,4},{6,7},{7,6},{8,9},{9,8},{10,11... | collective-permute-start | bytes 294920 | tf_op jit(solution)/shard_map/ppermute | solution.py:305
  29.7 1.5 %collective-permute-start.6 = (f32[32,768]{1,0:T(8,128)S(1)}, f32[32,768]{1,0:T(8,128)S(1)}, u32[]{:S(2)}, u32[]{:S(2)}) collective-permute-start(f32[32,768]{1,0:T(8,128)S(1)} %collective-permute-done.5.a2.refs_3_), channel_id=1, source_target_pairs={{0,1},{1,0},{2,3},{3,2},{4,5},{5,4},{6,7},{7,6},{8,9},{9,8},{10,11... | collective-permute-start | bytes 294920 | tf_op jit(solution)/shard_map/ppermute | solution.py:305
  31.5 3.4 %collective-permute-start.15 = (f32[32,256]{1,0:T(8,128)S(1)}, f32[32,256]{1,0:T(8,128)S(1)}, u32[]{:S(2)}, u32[]{:S(2)}) collective-permute-start(f32[32,256]{1,0:T(8,128)S(1)} %right_products_last.1), channel_id=1, source_target_pairs={{0,5},{1,4},{2,7},{3,6},{4,1},{5,0},{6,3},{7,2},{8,13},{9,12},{10,... | collective-permute-start | bytes 98312 | tf_op jit(solution)/shard_map/ppermute | solution.py:305
  33.1 1.8 %collective-permute-start.14 = (f32[32,256]{1,0:T(8,128)S(1)}, f32[32,256]{1,0:T(8,128)S(1)}, u32[]{:S(2)}, u32[]{:S(2)}) collective-permute-start(f32[32,256]{1,0:T(8,128)S(1)} %right_products_last.1), channel_id=1, source_target_pairs={{0,1},{1,0},{2,3},{3,2},{4,5},{5,4},{6,7},{7,6},{8,9},{9,8},{10,11... | collective-permute-start | bytes 98312 | tf_op jit(solution)/shard_map/ppermute | solution.py:305
  34.9 3.4 %collective-permute-start.17 = (f32[32,256]{1,0:T(8,128)S(1)}, f32[32,256]{1,0:T(8,128)S(1)}, u32[]{:S(2)}, u32[]{:S(2)}) collective-permute-start(f32[32,256]{1,0:T(8,128)S(1)} %add.46), channel_id=1, source_target_pairs={{0,9},{1,8},{2,11},{3,10},{4,13},{5,12},{6,15},{7,14},{8,1},{9,0},... | collective-permute-start | bytes 98312 | tf_op jit(solution)/shard_map/ppermute | solution.py:305
  36.2 2.1 %collective-permute-start.16 = (f32[32,256]{1,0:T(8,128)S(1)}, f32[32,256]{1,0:T(8,128)S(1)}, u32[]{:S(2)}, u32[]{:S(2)}) collective-permute-start(f32[32,256]{1,0:T(8,128)S(1)} %add.46), channel_id=1, source_target_pairs={{0,1},{1,0},{2,3},{3,2},{4,5},{5,4},{6,7},{7,6},{8,9},{9,8},{10,11... | collective-permute-start | bytes 98312 | tf_op jit(solution)/shard_map/ppermute | solution.py:305
  38.3 5.0 %collective-permute-start.18 = (f32[32,256]{1,0:T(8,128)S(1)}, f32[32,256]{1,0:T(8,128)S(1)}, u32[]{:S(2)}, u32[]{:S(2)}) collective-permute-start(f32[32,256]{1,0:T(8,128)S(1)} %add.47.t0_ref), channel_id=1, source_target_pairs={{0,16},{1,17},{2,18},{3,19},{4,20},{5,21},{6,22},{7,23},{8,24},{9,... | collective-permute-start | bytes 98312 | tf_op jit(solution)/shard_map/ppermute | solution.py:305

commit v8 on v7

--- a/solution.py
+++ b/solution.py
@@ -158,10 +158,10 @@
     return pl.ds(n * rows if isinstance(n, int) else pl.multiple_of(n * rows, rows), rows)
 
 
-def right_early_kernel(a1, b0, a3, b1, a2, mh_ref, ml_ref, mh2_ref, ml2_ref, t_ref, gram_ref, *, devices):
+def right_early_kernel(a1, b0, a3, b1, a2, mh_ref, ml_ref, mh2_ref, ml2_ref, t_ref, *, devices):
     rank, rows = a1.shape
     (_, their_bit), (_, bit) = sides(devices)
-    t = gram = 0.0
+    t = 0.0
     for ref, unit, hs, ls in (
         (a3, bit, mh2_ref, ml2_ref),
         (b1, 2, mh2_ref, ml2_ref),
@@ -172,10 +172,7 @@
         at = unit_at(unit, rows)
         p = terms_of((ref,))
         t = t + dot(p, hs[at], (1, 0)) + dot(p, ls[at], (1, 0))
-        if ref is not a2:
-            gram = gram + square(p, rank)
     t_ref[...] = fold(t, rank)
-    gram_ref[...] = gram
 
 
 def right_kernel(p_ref, mh_ref, ml_ref, before, t_ref, *, devices):
@@ -194,9 +191,10 @@
     return a
 
 
-def factor_kernel(gram_ref, a0, a2, state_ref):
-    rank = gram_ref.shape[0]
-    gram = gram_ref[...] + square(terms_of((a0, a2)), rank)
+def factor_kernel(*refs):
+    pieces, state_ref = refs[:UNITS], refs[UNITS]
+    rank = pieces[0].shape[0]
+    gram = square(terms_of(pieces), rank)
     row = lax.broadcasted_iota(jnp.int32, (rank, 128), 0)
     lane = lax.broadcasted_iota(jnp.int32, (rank, 128), 1)
     eye = (lane == row + rank).astype(F32)
@@ -317,13 +315,13 @@
     a2 = cross(a3, *walk[0])
     a1, b0, a0 = swap(a3, 1), swap(b1, 1), swap(a2, 1)
 
-    t, gram = call(
+    t = call(
         functools.partial(right_early_kernel, devices=devices),
         "right_products",
         work,
-        out_shape=(wide, small),
+        out_shape=wide,
         in_specs=[VMEM] * 9,
-        out_specs=(VMEM, VMEM),
+        out_specs=VMEM,
     )(a1, b0, a3, b1, a2, mh, ml, mh2, ml2)
     t = call(
         functools.partial(right_kernel, devices=devices),
@@ -339,9 +337,9 @@
         "factor_first_half",
         work,
         out_shape=pltpu.VMEM((rank, 128), F32),
-        in_specs=[VMEM] * 3,
+        in_specs=[VMEM] * UNITS,
         out_specs=VMEM,
-    )(gram, a0, a2)
+    )(a0, a1, b0, a2, a3, b1)
     inverse = call(inverse_kernel, "factor_second_half", work, out_shape=small, in_specs=[VMEM], out_specs=VMEM)(state)
     hat, hat_rows = call(
         functools.partial(hat_kernel, devices=devices),

time: 46 us -> 46 us (level)
  transfers between devices with their start and end apart: 19 -> 19, of which waited for: 13 -> 12; matrix products, arithmetic and copies ran while one was open for 0% -> 0% of each run, Pallas kernels for 13% -> 13%
where the time goes in v8:
time: 46 us; the launch traced here: 45.8 us
  starting transfers between devices  23.7 us (52%)
  Pallas kernels  12.1 us (26%)
  waiting for transfers between devices  9.16 us (20%)
  between operations  0.78 us (2%)
    ppermute x9, starting transfers between devices, cross(): lax.ppermute(x, AXES, [(i, i ^ 1 ^ bits[role(i)]) for i in range(devices)])  15.5 us
    pallas_call x8, Pallas kernels, call(): made(*(pltpu.with_memory_space_constraint(x, space) for x, space in zip(a...  12.1 us
    ppermute x10, starting transfers between devices, swap(): return lax.ppermute(x, AXES, [(i, i ^ bit) for i in range(devices)])  8.21 us
    ppermute x9, waiting for transfers between devices, cross(): lax.ppermute(x, AXES, [(i, i ^ 1 ^ bits[role(i)]) for i in range(devices)])  7.85 us
    ppermute x10, waiting for transfers between devices, swap(): return lax.ppermute(x, AXES, [(i, i ^ bit) for i in range(devices)])  1.31 us
  transfers between devices with their start and end apart: 19, of which 12 were waited for; matrix products, arithmetic and copies ran while one was open for 0% of the time, Pallas kernels for 13%

profile of v8, /device:TPU:0, one launch (start us, length us, event | category | flops | bytes accessed | tf_op | source)
XLA Modules:
  0.0 45.8 jit_solution(7166530350295150263)
XLA Ops:
  0.6 0.0 copy-start
  0.6 3.4 %left_products.1 = (f32[2304,256]{1,0:T(8,128)S(1)}, bf16[2304,256]{1,0:T(8,128)(2,1)S(1)}, bf16[2304,256]{1,0:T(8,128)(2,1)S(1)}, f32[2304,256]{1,0:T(8,128)S(1...) custom-call(f32[32,256]{1,0:T(8,128)} %bitcast.12, ...), custom_call_target="tpu_custom_call" | custom-call | flops 226492416 | tf_op jit(solution)/shard_map/left_products/pallas_call | solution.py:270
  4.0 0.5 %collective-permute-start = (f32[2,32,768]{2,1,0:T(8,128)S(1)}, f32[2,32,768]{2,1,0:T(8,128)S(1)}, u32[]{:S(2)}, u32[]{:S(2)}) collective-permute-start(f32[2,32,768]{2,1,0:T(8,128)S(1)} %get-tuple-element.24), channel_id=1, source_target_pairs={{0,1},{1,0},{2,3},{3,2},{4,5},{5,4},{6,7},{7,6},{8,9},{9,8},{10,11... | collective-permute-start | bytes 589832 | tf_op jit(solution)/shard_map/ppermute | solution.py:303
  4.5 0.1 collective-permute-start.8
  4.6 0.0 copy-done
  4.6 0.9 %left_products_rest.1 = (f32[2304,256]{1,0:T(8,128)S(1)}, bf16[2304,256]{1,0:T(8,128)(2,1)S(1)}, bf16[2304,256]{1,0:T(8,128)(2,1)S(1)}, f32[2,32,768]{2,1,0:T(8,128)S(1)}, f32[32,768]{1,0:T(8,128)S(1)}) custom-call(f32[32,256]{1,0:T(8,128)S(1)} %bitcast.13, f32[2304,256]{1,0:T(8,128)S(1)} %get-tuple-element.21.e_ref, ...), custom_call_target="tpu_custom_call" | custom-call | flops 226492416 | tf_op jit(solution)/shard_map/left_products_rest/pallas_call | solution.py:270
  5.5 0.1 collective-permute-done
  5.6 2.7 %collective-permute-start.1 = (f32[32,768]{1,0:T(8,128)S(1)}, f32[32,768]{1,0:T(8,128)S(1)}, u32[]{:S(2)}, u32[]{:S(2)}) collective-permute-start(f32[32,768]{1,0:T(8,128)S(1)} %slice_bitcast_fusion), channel_id=1, source_target_pairs={{0,3},{1,8},{2,11},{3,0},{4,13},{5,6},{6,5},{7,14},{8,1},{9,10},{1... | collective-permute-start | bytes 294920 | tf_op jit(solution)/shard_map/ppermute | solution.py:306
  8.3 0.0 collective-permute-done.8
  8.3 0.2 collective-permute-start.9
  8.5 2.1 %collective-permute-done.1 = f32[32,768]{1,0:T(8,128)S(1)} collective-permute-done((f32[32,768]{1,0:T(8,128)S(1)}, f32[32,768]{1,0:T(8,128)S(1)}, u32[]{:S(2)}, u32[]{:S(2)}) %collective-permute-start.1) | collective-permute-done | bytes 98336 | tf_op jit(solution)/shard_map/ppermute | solution.py:306
  10.6 2.2 %collective-permute-start.2 = (f32[32,768]{1,0:T(8,128)S(1)}, f32[32,768]{1,0:T(8,128)S(1)}, u32[]{:S(2)}, u32[]{:S(2)}) collective-permute-start(f32[32,768]{1,0:T(8,128)S(1)} %fusion), channel_id=1, source_target_pairs={{0,9},{1,4},{2,7},{3,10},{4,1},{5,12},{6,15},{7,2},{8,13},{9,0},{1... | collective-permute-start | bytes 294920 | tf_op jit(solution)/shard_map/ppermute | solution.py:306
  12.8 0.0 collective-permute-done.9
  12.8 1.2 %collective-permute-start.10 = (f32[32,768]{1,0:T(8,128)S(1)}, f32[32,768]{1,0:T(8,128)S(1)}, u32[]{:S(2)}, u32[]{:S(2)}) collective-permute-start(f32[32,768]{1,0:T(8,128)S(1)} %add.42), channel_id=1, source_target_pairs={{0,9},{1,4},{2,7},{3,10},{4,1},{5,12},{6,15},{7,2},{8,13},{9,0},{1... | collective-permute-start | bytes 294920 | tf_op jit(solution)/shard_map/ppermute | solution.py:306
  14.1 1.0 %collective-permute-done.2 = f32[32,768]{1,0:T(8,128)S(1)} collective-permute-done((f32[32,768]{1,0:T(8,128)S(1)}, f32[32,768]{1,0:T(8,128)S(1)}, u32[]{:S(2)}, u32[]{:S(2)}) %collective-permute-start.2) | collective-permute-done | bytes 98336 | tf_op jit(solution)/shard_map/ppermute | solution.py:306
  15.1 1.5 %collective-permute-start.3 = (f32[32,768]{1,0:T(8,128)S(1)}, f32[32,768]{1,0:T(8,128)S(1)}, u32[]{:S(2)}, u32[]{:S(2)}) collective-permute-start(f32[32,768]{1,0:T(8,128)S(1)} %add.38), channel_id=1, source_target_pairs={{0,5},{1,16},{2,19},{3,6},{4,21},{5,0},{6,3},{7,22},{8,25},{9,12},... | collective-permute-start | bytes 294920 | tf_op jit(solution)/shard_map/ppermute | solution.py:306
  16.6 0.4 collective-permute-done.10
  17.0 1.3 %collective-permute-start.11 = (f32[32,768]{1,0:T(8,128)S(1)}, f32[32,768]{1,0:T(8,128)S(1)}, u32[]{:S(2)}, u32[]{:S(2)}) collective-permute-start(f32[32,768]{1,0:T(8,128)S(1)} %add.43), channel_id=1, source_target_pairs={{0,5},{1,16},{2,19},{3,6},{4,21},{5,0},{6,3},{7,22},{8,25},{9,12},... | collective-permute-start | bytes 294920 | tf_op jit(solution)/shard_map/ppermute | solution.py:306
  18.2 1.0 %collective-permute-done.3 = f32[32,768]{1,0:T(8,128)S(1)} collective-permute-done((f32[32,768]{1,0:T(8,128)S(1)}, f32[32,768]{1,0:T(8,128)S(1)}, u32[]{:S(2)}, u32[]{:S(2)}) %collective-permute-start.3) | collective-permute-done | bytes 98336 | tf_op jit(solution)/shard_map/ppermute | solution.py:306
  19.3 2.8 %collective-permute-start.4 = (f32[32,768]{1,0:T(8,128)S(1)}, f32[32,768]{1,0:T(8,128)S(1)}, u32[]{:S(2)}, u32[]{:S(2)}) collective-permute-start(f32[32,768]{1,0:T(8,128)S(1)} %add.39), channel_id=1, source_target_pairs={{0,17},{1,2},{2,1},{3,18},{4,7},{5,20},{6,23},{7,4},{8,11},{9,24},... | collective-permute-start | bytes 294920 | tf_op jit(solution)/shard_map/ppermute | solution.py:306
  22.1 0.0 collective-permute-done.11
  22.1 1.6 %collective-permute-start.12 = (f32[32,768]{1,0:T(8,128)S(1)}, f32[32,768]{1,0:T(8,128)S(1)}, u32[]{:S(2)}, u32[]{:S(2)}) collective-permute-start(f32[32,768]{1,0:T(8,128)S(1)} %add.44), channel_id=1, source_target_pairs={{0,17},{1,2},{2,1},{3,18},{4,7},{5,20},{6,23},{7,4},{8,11},{9,24},... | collective-permute-start | bytes 294920 | tf_op jit(solution)/shard_map/ppermute | solution.py:306
  23.7 1.6 %collective-permute-done.4 = f32[32,768]{1,0:T(8,128)S(1)} collective-permute-done((f32[32,768]{1,0:T(8,128)S(1)}, f32[32,768]{1,0:T(8,128)S(1)}, u32[]{:S(2)}, u32[]{:S(2)}) %collective-permute-start.4) | collective-permute-done | bytes 98336 | tf_op jit(solution)/shard_map/ppermute | solution.py:306
  25.4 2.0 %collective-permute-start.5 = (f32[32,768]{1,0:T(8,128)S(1)}, f32[32,768]{1,0:T(8,128)S(1)}, u32[]{:S(2)}, u32[]{:S(2)}) collective-permute-start(f32[32,768]{1,0:T(8,128)S(1)} %add.40.a3.refs_4_), channel_id=1, source_target_pairs={{0,3},{1,8},{2,11},{3,0},{4,13},{5,6},{6,5},{7,14},{8,1},{9,10},{1... | collective-permute-start | bytes 294920 | tf_op jit(solution)/shard_map/ppermute | solution.py:306
  27.4 1.3 %collective-permute-done.12 = f32[32,768]{1,0:T(8,128)S(1)} collective-permute-done((f32[32,768]{1,0:T(8,128)S(1)}, f32[32,768]{1,0:T(8,128)S(1)}, u32[]{:S(2)}, u32[]{:S(2)}) %collective-permute-start.12) | collective-permute-done | bytes 98336 | tf_op jit(solution)/shard_map/ppermute | solution.py:306
  28.7 0.1 collective-permute-start.13
  28.8 0.5 %collective-permute-start.7 = (f32[32,768]{1,0:T(8,128)S(1)}, f32[32,768]{1,0:T(8,128)S(1)}, u32[]{:S(2)}, u32[]{:S(2)}) collective-permute-start(f32[32,768]{1,0:T(8,128)S(1)} %add.40.a3.refs_4_), channel_id=1, source_target_pairs={{0,1},{1,0},{2,3},{3,2},{4,5},{5,4},{6,7},{7,6},{8,9},{9,8},{10,11... | collective-permute-start | bytes 294920 | tf_op jit(solution)/shard_map/ppermute | solution.py:303
  29.3 0.4 collective-permute-done.5.a2.refs_3_
  29.7 0.1 collective-permute-start.6
  29.8 0.3 collective-permute-done.13.b0.refs_2_
  30.1 0.2 collective-permute-done.7.a1.refs_1_
  30.2 0.8 %right_products.1.before = f32[32,256]{1,0:T(8,128)S(1)} custom-call(f32[32,768]{1,0:T(8,128)S(1)} %collective-permute-done.7.a1.refs_1_, f32[32,768]{1,0:T(8,128)S(1)} %collective-permute-done.13.b0.refs_2_, f32[32,768]{1,0:T(8,128)S(1)} %add.40.a3.refs_4_, f32[32,768]{1,0:T(8,128)S(1)} %add.45.b1.refs_5_, f32[32,768]{1,0:T(8,128)S(1)} %collective-permute-done.5.a2.refs_3_, ...), custom_call_target="tpu_custom_call" | custom-call | flops 226492416 | tf_op jit(solution)/shard_map/right_products/pallas_call | solution.py:270
  31.0 0.0 collective-permute-done.6.p_ref.refs_0_
  31.0 0.3 right_products_last.1
  31.3 1.8 %collective-permute-start.15 = (f32[32,256]{1,0:T(8,128)S(1)}, f32[32,256]{1,0:T(8,128)S(1)}, u32[]{:S(2)}, u32[]{:S(2)}) collective-permute-start(f32[32,256]{1,0:T(8,128)S(1)} %right_products_last.1), channel_id=1, source_target_pairs={{0,5},{1,4},{2,7},{3,6},{4,1},{5,0},{6,3},{7,2},{8,13},{9,12},{10,... | collective-permute-start | bytes 98312 | tf_op jit(solution)/shard_map/ppermute | solution.py:303
  33.1 0.2 collective-permute-start.14
  33.3 1.5 %factor_first_half.1.state_ref = f32[32,128]{1,0:T(8,128)S(1)} custom-call(f32[32,768]{1,0:T(8,128)S(1)} %collective-permute-done.6.p_ref.refs_0_, f32[32,768]{1,0:T(8,128)S(1)} %collective-permute-done.7.a1.refs_1_, f32[32,768]{1,0:T(8,128)S(1)} %collective-permute-done.13.b0.refs_2_, f32[32,768]{1,0:T(8,128)S(1)} %collective-permute-done.5.a2.refs_3_, ...), custom_call_target="tpu_custom_call" | custom-call | flops 226492416 | tf_op jit(solution)/shard_map/factor_first_half/pallas_call | solution.py:270
  34.8 0.0 collective-permute-done.15
  34.8 0.0 collective-permute-done.14
  34.8 1.4 %collective-permute-start.17 = (f32[32,256]{1,0:T(8,128)S(1)}, f32[32,256]{1,0:T(8,128)S(1)}, u32[]{:S(2)}, u32[]{:S(2)}) collective-permute-start(f32[32,256]{1,0:T(8,128)S(1)} %add.46), channel_id=1, source_target_pairs={{0,9},{1,8},{2,11},{3,10},{4,13},{5,12},{6,15},{7,14},{8,1},{9,0},... | collective-permute-start | bytes 98312 | tf_op jit(solution)/shard_map/ppermute | solution.py:303
  36.2 0.4 collective-permute-start.16
  36.6 1.6 %factor_second_half.1.inv_ref = f32[32,32]{1,0:T(8,128)S(1)} custom-call(f32[32,128]{1,0:T(8,128)S(1)} %factor_first_half.1.state_ref), custom_call_target="tpu_custom_call" | custom-call | flops 226492416 | tf_op jit(solution)/shard_map/factor_second_half/pallas_call | solution.py:270
  38.2 0.1 collective-permute-done.17
  38.2 0.0 collective-permute-done.16
  38.3 3.2 %collective-permute-start.18 = (f32[32,256]{1,0:T(8,128)S(1)}, f32[32,256]{1,0:T(8,128)S(1)}, u32[]{:S(2)}, u32[]{:S(2)}) collective-permute-start(f32[32,256]{1,0:T(8,128)S(1)} %add.47.t0_ref), channel_id=1, source_target_pairs={{0,16},{1,17},{2,18},{3,19},{4,20},{5,21},{6,22},{7,23},{8,24},{9,... | collective-permute-start | bytes 98312 | tf_op jit(solution)/shard_map/ppermute | solution.py:303
  41.5 1.2 %left_factor.1 = (f32[32,4608]{1,0:T(8,128)}, bf16[4608,128]{1,0:T(8,128)(2,1)S(1)}) custom-call(f32[32,32]{1,0:T(8,128)S(1)} %factor_second_half.1.inv_ref, f32[32,768]{1,0:T(8,128)S(1)} %collective-permute-done.6.p_ref.refs_0_, f32[32,768]{1,0:T(8,128)S(1)} %collective-permute-done.7.a1.refs_1_, f32[32,768]{1,0:T(8,128)S(1)} %collective-permute-done.13.b0.refs_2_, ...), custom_call_target="tpu_custom_call" | custom-call | flops 226492416 | tf_op jit(solution)/shard_map/left_factor/pallas_call | solution.py:270
  42.7 0.6 %collective-permute-done.18.t1_ref = f32[32,256]{1,0:T(8,128)S(1)} collective-permute-done((f32[32,256]{1,0:T(8,128)S(1)}, f32[32,256]{1,0:T(8,128)S(1)}, u32[]{:S(2)}, u32[]{:S(2)}) %collective-permute-start.18) | collective-permute-done | bytes 32800 | tf_op jit(solution)/shard_map/ppermute | solution.py:303
  43.4 2.5 %new_error.1 = (f32[4608,256]{1,0:T(8,128)}, f32[32,256]{1,0:T(8,128)}) custom-call(f32[32,256]{1,0:T(8,128)S(1)} %add.47.t0_ref, f32[32,256]{1,0:T(8,128)S(1)} %collective-permute-done.18.t1_ref, f32[32,32]{1,0:T(8,128)S(1)} %factor_second_half.1.inv_ref, bf16[4608,128]{1,0:T(8,128)(2,1)S(1)} %get-tuple-element.33.rows_ref, ...), custom_call_target="tpu_custom_call" | custom-call | flops 226492416 | tf_op jit(solution)/shard_map/new_error/pallas_call | solution.py:270
  (13 shorter events, 0.2 us)
Async XLA Ops:
  0.6 4.0 %copy-start = (f32[256,32]{0,1:T(8,128)S(1)}, f32[256,32]{0,1:T(8,128)}, u32[]{:S(2)}) copy-start(f32[256,32]{0,1:T(8,128)} %param.5) | copy-start | bytes 98308
  4.0 1.6 %collective-permute-start = (f32[2,32,768]{2,1,0:T(8,128)S(1)}, f32[2,32,768]{2,1,0:T(8,128)S(1)}, u32[]{:S(2)}, u32[]{:S(2)}) collective-permute-start(f32[2,32,768]{2,1,0:T(8,128)S(1)} %get-tuple-element.24), channel_id=1, source_target_pairs={{0,1},{1,0},{2,3},{3,2},{4,5},{5,4},{6,7},{7,6},{8,9},{9,8},{10,11... | collective-permute-start | bytes 589832 | tf_op jit(solution)/shard_map/ppermute | solution.py:303
  4.5 3.8 %collective-permute-start.8 = (f32[32,768]{1,0:T(8,128)S(1)}, f32[32,768]{1,0:T(8,128)S(1)}, u32[]{:S(2)}, u32[]{:S(2)}) collective-permute-start(f32[32,768]{1,0:T(8,128)S(1)} %get-tuple-element.28), channel_id=1, source_target_pairs={{0,1},{1,0},{2,3},{3,2},{4,5},{5,4},{6,7},{7,6},{8,9},{9,8},{10,11... | collective-permute-start | bytes 294920 | tf_op jit(solution)/shard_map/ppermute | solution.py:303
  5.6 5.0 %collective-permute-start.1 = (f32[32,768]{1,0:T(8,128)S(1)}, f32[32,768]{1,0:T(8,128)S(1)}, u32[]{:S(2)}, u32[]{:S(2)}) collective-permute-start(f32[32,768]{1,0:T(8,128)S(1)} %slice_bitcast_fusion), channel_id=1, source_target_pairs={{0,3},{1,8},{2,11},{3,0},{4,13},{5,6},{6,5},{7,14},{8,1},{9,10},{1... | collective-permute-start | bytes 294920 | tf_op jit(solution)/shard_map/ppermute | solution.py:306
  8.3 4.5 %collective-permute-start.9 = (f32[32,768]{1,0:T(8,128)S(1)}, f32[32,768]{1,0:T(8,128)S(1)}, u32[]{:S(2)}, u32[]{:S(2)}) collective-permute-start(f32[32,768]{1,0:T(8,128)S(1)} %add.41), channel_id=1, source_target_pairs={{0,3},{1,8},{2,11},{3,0},{4,13},{5,6},{6,5},{7,14},{8,1},{9,10},{1... | collective-permute-start | bytes 294920 | tf_op jit(solution)/shard_map/ppermute | solution.py:306
  10.6 4.5 %collective-permute-start.2 = (f32[32,768]{1,0:T(8,128)S(1)}, f32[32,768]{1,0:T(8,128)S(1)}, u32[]{:S(2)}, u32[]{:S(2)}) collective-permute-start(f32[32,768]{1,0:T(8,128)S(1)} %fusion), channel_id=1, source_target_pairs={{0,9},{1,4},{2,7},{3,10},{4,1},{5,12},{6,15},{7,2},{8,13},{9,0},{1... | collective-permute-start | bytes 294920 | tf_op jit(solution)/shard_map/ppermute | solution.py:306
  12.8 4.1 %collective-permute-start.10 = (f32[32,768]{1,0:T(8,128)S(1)}, f32[32,768]{1,0:T(8,128)S(1)}, u32[]{:S(2)}, u32[]{:S(2)}) collective-permute-start(f32[32,768]{1,0:T(8,128)S(1)} %add.42), channel_id=1, source_target_pairs={{0,9},{1,4},{2,7},{3,10},{4,1},{5,12},{6,15},{7,2},{8,13},{9,0},{1... | collective-permute-start | bytes 294920 | tf_op jit(solution)/shard_map/ppermute | solution.py:306
  15.1 4.1 %collective-permute-start.3 = (f32[32,768]{1,0:T(8,128)S(1)}, f32[32,768]{1,0:T(8,128)S(1)}, u32[]{:S(2)}, u32[]{:S(2)}) collective-permute-start(f32[32,768]{1,0:T(8,128)S(1)} %add.38), channel_id=1, source_target_pairs={{0,5},{1,16},{2,19},{3,6},{4,21},{5,0},{6,3},{7,22},{8,25},{9,12},... | collective-permute-start | bytes 294920 | tf_op jit(solution)/shard_map/ppermute | solution.py:306
  17.0 5.1 %collective-permute-start.11 = (f32[32,768]{1,0:T(8,128)S(1)}, f32[32,768]{1,0:T(8,128)S(1)}, u32[]{:S(2)}, u32[]{:S(2)}) collective-permute-start(f32[32,768]{1,0:T(8,128)S(1)} %add.43), channel_id=1, source_target_pairs={{0,5},{1,16},{2,19},{3,6},{4,21},{5,0},{6,3},{7,22},{8,25},{9,12},... | collective-permute-start | bytes 294920 | tf_op jit(solution)/shard_map/ppermute | solution.py:306
  19.3 6.1 %collective-permute-start.4 = (f32[32,768]{1,0:T(8,128)S(1)}, f32[32,768]{1,0:T(8,128)S(1)}, u32[]{:S(2)}, u32[]{:S(2)}) collective-permute-start(f32[32,768]{1,0:T(8,128)S(1)} %add.39), channel_id=1, source_target_pairs={{0,17},{1,2},{2,1},{3,18},{4,7},{5,20},{6,23},{7,4},{8,11},{9,24},... | collective-permute-start | bytes 294920 | tf_op jit(solution)/shard_map/ppermute | solution.py:306
  22.1 6.6 %collective-permute-start.12 = (f32[32,768]{1,0:T(8,128)S(1)}, f32[32,768]{1,0:T(8,128)S(1)}, u32[]{:S(2)}, u32[]{:S(2)}) collective-permute-start(f32[32,768]{1,0:T(8,128)S(1)} %add.44), channel_id=1, source_target_pairs={{0,17},{1,2},{2,1},{3,18},{4,7},{5,20},{6,23},{7,4},{8,11},{9,24},... | collective-permute-start | bytes 294920 | tf_op jit(solution)/shard_map/ppermute | solution.py:306
  25.4 4.3 %collective-permute-start.5 = (f32[32,768]{1,0:T(8,128)S(1)}, f32[32,768]{1,0:T(8,128)S(1)}, u32[]{:S(2)}, u32[]{:S(2)}) collective-permute-start(f32[32,768]{1,0:T(8,128)S(1)} %add.40.a3.refs_4_), channel_id=1, source_target_pairs={{0,3},{1,8},{2,11},{3,0},{4,13},{5,6},{6,5},{7,14},{8,1},{9,10},{1... | collective-permute-start | bytes 294920 | tf_op jit(solution)/shard_map/ppermute | solution.py:306
  28.7 1.4 %collective-permute-start.13 = (f32[32,768]{1,0:T(8,128)S(1)}, f32[32,768]{1,0:T(8,128)S(1)}, u32[]{:S(2)}, u32[]{:S(2)}) collective-permute-start(f32[32,768]{1,0:T(8,128)S(1)} %add.45.b1.refs_5_), channel_id=1, source_target_pairs={{0,1},{1,0},{2,3},{3,2},{4,5},{5,4},{6,7},{7,6},{8,9},{9,8},{10,11... | collective-permute-start | bytes 294920 | tf_op jit(solution)/shard_map/ppermute | solution.py:303
  28.8 1.4 %collective-permute-start.7 = (f32[32,768]{1,0:T(8,128)S(1)}, f32[32,768]{1,0:T(8,128)S(1)}, u32[]{:S(2)}, u32[]{:S(2)}) collective-permute-start(f32[32,768]{1,0:T(8,128)S(1)} %add.40.a3.refs_4_), channel_id=1, source_target_pairs={{0,1},{1,0},{2,3},{3,2},{4,5},{5,4},{6,7},{7,6},{8,9},{9,8},{10,11... | collective-permute-start | bytes 294920 | tf_op jit(solution)/shard_map/ppermute | solution.py:303
  29.7 1.3 %collective-permute-start.6 = (f32[32,768]{1,0:T(8,128)S(1)}, f32[32,768]{1,0:T(8,128)S(1)}, u32[]{:S(2)}, u32[]{:S(2)}) collective-permute-start(f32[32,768]{1,0:T(8,128)S(1)} %collective-permute-done.5.a2.refs_3_), channel_id=1, source_target_pairs={{0,1},{1,0},{2,3},{3,2},{4,5},{5,4},{6,7},{7,6},{8,9},{9,8},{10,11... | collective-permute-start | bytes 294920 | tf_op jit(solution)/shard_map/ppermute | solution.py:303
  31.3 3.5 %collective-permute-start.15 = (f32[32,256]{1,0:T(8,128)S(1)}, f32[32,256]{1,0:T(8,128)S(1)}, u32[]{:S(2)}, u32[]{:S(2)}) collective-permute-start(f32[32,256]{1,0:T(8,128)S(1)} %right_products_last.1), channel_id=1, source_target_pairs={{0,5},{1,4},{2,7},{3,6},{4,1},{5,0},{6,3},{7,2},{8,13},{9,12},{10,... | collective-permute-start | bytes 98312 | tf_op jit(solution)/shard_map/ppermute | solution.py:303
  33.1 1.7 %collective-permute-start.14 = (f32[32,256]{1,0:T(8,128)S(1)}, f32[32,256]{1,0:T(8,128)S(1)}, u32[]{:S(2)}, u32[]{:S(2)}) collective-permute-start(f32[32,256]{1,0:T(8,128)S(1)} %right_products_last.1), channel_id=1, source_target_pairs={{0,1},{1,0},{2,3},{3,2},{4,5},{5,4},{6,7},{7,6},{8,9},{9,8},{10,11... | collective-permute-start | bytes 98312 | tf_op jit(solution)/shard_map/ppermute | solution.py:303
  34.8 3.4 %collective-permute-start.17 = (f32[32,256]{1,0:T(8,128)S(1)}, f32[32,256]{1,0:T(8,128)S(1)}, u32[]{:S(2)}, u32[]{:S(2)}) collective-permute-start(f32[32,256]{1,0:T(8,128)S(1)} %add.46), channel_id=1, source_target_pairs={{0,9},{1,8},{2,11},{3,10},{4,13},{5,12},{6,15},{7,14},{8,1},{9,0},... | collective-permute-start | bytes 98312 | tf_op jit(solution)/shard_map/ppermute | solution.py:303
  36.2 2.0 %collective-permute-start.16 = (f32[32,256]{1,0:T(8,128)S(1)}, f32[32,256]{1,0:T(8,128)S(1)}, u32[]{:S(2)}, u32[]{:S(2)}) collective-permute-start(f32[32,256]{1,0:T(8,128)S(1)} %add.46), channel_id=1, source_target_pairs={{0,1},{1,0},{2,3},{3,2},{4,5},{5,4},{6,7},{7,6},{8,9},{9,8},{10,11... | collective-permute-start | bytes 98312 | tf_op jit(solution)/shard_map/ppermute | solution.py:303
  38.3 5.1 %collective-permute-start.18 = (f32[32,256]{1,0:T(8,128)S(1)}, f32[32,256]{1,0:T(8,128)S(1)}, u32[]{:S(2)}, u32[]{:S(2)}) collective-permute-start(f32[32,256]{1,0:T(8,128)S(1)} %add.47.t0_ref), channel_id=1, source_target_pairs={{0,16},{1,17},{2,18},{3,19},{4,20},{5,21},{6,22},{7,23},{8,24},{9,... | collective-permute-start | bytes 98312 | tf_op jit(solution)/shard_map/ppermute | solution.py:303

commit v9 on v8

--- a/solution.py
+++ b/solution.py
@@ -94,8 +94,8 @@
         to = pl.ds(n % 2 * block, block)
         copies.append(
             (
+                pltpu.make_async_copy(e_hbm.at[source], (e_ref if n > 1 else m_ref).at[to], sems.at[n, 1]),
                 pltpu.make_async_copy(g_hbm.at[source], (g_ref if n > 1 else g_buf).at[to], sems.at[n, 0]),
-                pltpu.make_async_copy(e_hbm.at[source], (e_ref if n > 1 else m_ref).at[to], sems.at[n, 1]),
             )
         )
     start(copies[:3])

time: 46 us -> 46 us (level)
  no operation moved by 1% of the time
where the time goes in v9:
time: 46 us; the launch traced here: 45.8 us
  starting transfers between devices  23.7 us (52%)
  Pallas kernels  12 us (26%)
  waiting for transfers between devices  9.14 us (20%)
  between operations  0.78 us (2%)
    ppermute x9, starting transfers between devices, cross(): lax.ppermute(x, AXES, [(i, i ^ 1 ^ bits[role(i)]) for i in range(devices)])  15.5 us
    pallas_call x8, Pallas kernels, call(): made(*(pltpu.with_memory_space_constraint(x, space) for x, space in zip(a...  12 us
    ppermute x10, starting transfers between devices, swap(): return lax.ppermute(x, AXES, [(i, i ^ bit) for i in range(devices)])  8.23 us
    ppermute x9, waiting for transfers between devices, cross(): lax.ppermute(x, AXES, [(i, i ^ 1 ^ bits[role(i)]) for i in range(devices)])  7.85 us
    ppermute x10, waiting for transfers between devices, swap(): return lax.ppermute(x, AXES, [(i, i ^ bit) for i in range(devices)])  1.29 us
  transfers between devices with their start and end apart: 19, of which 12 were waited for; matrix products, arithmetic and copies ran while one was open for 0% of the time, Pallas kernels for 13%

profile of v9, /device:TPU:0, one launch (start us, length us, event | category | flops | bytes accessed | tf_op | source)
XLA Modules:
  0.0 45.8 jit_solution(16297424543108256340)
XLA Ops:
  0.6 0.0 copy-start
  0.6 3.3 %left_products.1 = (f32[2304,256]{1,0:T(8,128)S(1)}, bf16[2304,256]{1,0:T(8,128)(2,1)S(1)}, bf16[2304,256]{1,0:T(8,128)(2,1)S(1)}, f32[2304,256]{1,0:T(8,128)S(1...) custom-call(f32[32,256]{1,0:T(8,128)} %bitcast.12, ...), custom_call_target="tpu_custom_call" | custom-call | flops 226492416 | tf_op jit(solution)/shard_map/left_products/pallas_call | solution.py:270
  4.0 0.5 %collective-permute-start = (f32[2,32,768]{2,1,0:T(8,128)S(1)}, f32[2,32,768]{2,1,0:T(8,128)S(1)}, u32[]{:S(2)}, u32[]{:S(2)}) collective-permute-start(f32[2,32,768]{2,1,0:T(8,128)S(1)} %get-tuple-element.24), channel_id=1, source_target_pairs={{0,1},{1,0},{2,3},{3,2},{4,5},{5,4},{6,7},{7,6},{8,9},{9,8},{10,11... | collective-permute-start | bytes 589832 | tf_op jit(solution)/shard_map/ppermute | solution.py:303
  4.5 0.1 collective-permute-start.8
  4.6 0.0 copy-done
  4.6 0.9 %left_products_rest.1 = (f32[2304,256]{1,0:T(8,128)S(1)}, bf16[2304,256]{1,0:T(8,128)(2,1)S(1)}, bf16[2304,256]{1,0:T(8,128)(2,1)S(1)}, f32[2,32,768]{2,1,0:T(8,128)S(1)}, f32[32,768]{1,0:T(8,128)S(1)}) custom-call(f32[32,256]{1,0:T(8,128)S(1)} %bitcast.13, f32[2304,256]{1,0:T(8,128)S(1)} %get-tuple-element.21.e_ref, ...), custom_call_target="tpu_custom_call" | custom-call | flops 226492416 | tf_op jit(solution)/shard_map/left_products_rest/pallas_call | solution.py:270
  5.5 0.1 collective-permute-done
  5.6 2.7 %collective-permute-start.1 = (f32[32,768]{1,0:T(8,128)S(1)}, f32[32,768]{1,0:T(8,128)S(1)}, u32[]{:S(2)}, u32[]{:S(2)}) collective-permute-start(f32[32,768]{1,0:T(8,128)S(1)} %slice_bitcast_fusion), channel_id=1, source_target_pairs={{0,3},{1,8},{2,11},{3,0},{4,13},{5,6},{6,5},{7,14},{8,1},{9,10},{1... | collective-permute-start | bytes 294920 | tf_op jit(solution)/shard_map/ppermute | solution.py:306
  8.3 0.0 collective-permute-done.8
  8.3 0.2 collective-permute-start.9
  8.5 2.1 %collective-permute-done.1 = f32[32,768]{1,0:T(8,128)S(1)} collective-permute-done((f32[32,768]{1,0:T(8,128)S(1)}, f32[32,768]{1,0:T(8,128)S(1)}, u32[]{:S(2)}, u32[]{:S(2)}) %collective-permute-start.1) | collective-permute-done | bytes 98336 | tf_op jit(solution)/shard_map/ppermute | solution.py:306
  10.6 2.2 %collective-permute-start.2 = (f32[32,768]{1,0:T(8,128)S(1)}, f32[32,768]{1,0:T(8,128)S(1)}, u32[]{:S(2)}, u32[]{:S(2)}) collective-permute-start(f32[32,768]{1,0:T(8,128)S(1)} %fusion), channel_id=1, source_target_pairs={{0,9},{1,4},{2,7},{3,10},{4,1},{5,12},{6,15},{7,2},{8,13},{9,0},{1... | collective-permute-start | bytes 294920 | tf_op jit(solution)/shard_map/ppermute | solution.py:306
  12.8 0.0 collective-permute-done.9
  12.8 1.2 %collective-permute-start.10 = (f32[32,768]{1,0:T(8,128)S(1)}, f32[32,768]{1,0:T(8,128)S(1)}, u32[]{:S(2)}, u32[]{:S(2)}) collective-permute-start(f32[32,768]{1,0:T(8,128)S(1)} %add.42), channel_id=1, source_target_pairs={{0,9},{1,4},{2,7},{3,10},{4,1},{5,12},{6,15},{7,2},{8,13},{9,0},{1... | collective-permute-start | bytes 294920 | tf_op jit(solution)/shard_map/ppermute | solution.py:306
  14.0 1.0 %collective-permute-done.2 = f32[32,768]{1,0:T(8,128)S(1)} collective-permute-done((f32[32,768]{1,0:T(8,128)S(1)}, f32[32,768]{1,0:T(8,128)S(1)}, u32[]{:S(2)}, u32[]{:S(2)}) %collective-permute-start.2) | collective-permute-done | bytes 98336 | tf_op jit(solution)/shard_map/ppermute | solution.py:306
  15.1 1.5 %collective-permute-start.3 = (f32[32,768]{1,0:T(8,128)S(1)}, f32[32,768]{1,0:T(8,128)S(1)}, u32[]{:S(2)}, u32[]{:S(2)}) collective-permute-start(f32[32,768]{1,0:T(8,128)S(1)} %add.38), channel_id=1, source_target_pairs={{0,5},{1,16},{2,19},{3,6},{4,21},{5,0},{6,3},{7,22},{8,25},{9,12},... | collective-permute-start | bytes 294920 | tf_op jit(solution)/shard_map/ppermute | solution.py:306
  16.6 0.4 collective-permute-done.10
  16.9 1.3 %collective-permute-start.11 = (f32[32,768]{1,0:T(8,128)S(1)}, f32[32,768]{1,0:T(8,128)S(1)}, u32[]{:S(2)}, u32[]{:S(2)}) collective-permute-start(f32[32,768]{1,0:T(8,128)S(1)} %add.43), channel_id=1, source_target_pairs={{0,5},{1,16},{2,19},{3,6},{4,21},{5,0},{6,3},{7,22},{8,25},{9,12},... | collective-permute-start | bytes 294920 | tf_op jit(solution)/shard_map/ppermute | solution.py:306
  18.2 1.0 %collective-permute-done.3 = f32[32,768]{1,0:T(8,128)S(1)} collective-permute-done((f32[32,768]{1,0:T(8,128)S(1)}, f32[32,768]{1,0:T(8,128)S(1)}, u32[]{:S(2)}, u32[]{:S(2)}) %collective-permute-start.3) | collective-permute-done | bytes 98336 | tf_op jit(solution)/shard_map/ppermute | solution.py:306
  19.2 2.8 %collective-permute-start.4 = (f32[32,768]{1,0:T(8,128)S(1)}, f32[32,768]{1,0:T(8,128)S(1)}, u32[]{:S(2)}, u32[]{:S(2)}) collective-permute-start(f32[32,768]{1,0:T(8,128)S(1)} %add.39), channel_id=1, source_target_pairs={{0,17},{1,2},{2,1},{3,18},{4,7},{5,20},{6,23},{7,4},{8,11},{9,24},... | collective-permute-start | bytes 294920 | tf_op jit(solution)/shard_map/ppermute | solution.py:306
  22.0 0.0 collective-permute-done.11
  22.1 1.6 %collective-permute-start.12 = (f32[32,768]{1,0:T(8,128)S(1)}, f32[32,768]{1,0:T(8,128)S(1)}, u32[]{:S(2)}, u32[]{:S(2)}) collective-permute-start(f32[32,768]{1,0:T(8,128)S(1)} %add.44), channel_id=1, source_target_pairs={{0,17},{1,2},{2,1},{3,18},{4,7},{5,20},{6,23},{7,4},{8,11},{9,24},... | collective-permute-start | bytes 294920 | tf_op jit(solution)/shard_map/ppermute | solution.py:306
  23.7 1.6 %collective-permute-done.4 = f32[32,768]{1,0:T(8,128)S(1)} collective-permute-done((f32[32,768]{1,0:T(8,128)S(1)}, f32[32,768]{1,0:T(8,128)S(1)}, u32[]{:S(2)}, u32[]{:S(2)}) %collective-permute-start.4) | collective-permute-done | bytes 98336 | tf_op jit(solution)/shard_map/ppermute | solution.py:306
  25.3 2.0 %collective-permute-start.5 = (f32[32,768]{1,0:T(8,128)S(1)}, f32[32,768]{1,0:T(8,128)S(1)}, u32[]{:S(2)}, u32[]{:S(2)}) collective-permute-start(f32[32,768]{1,0:T(8,128)S(1)} %add.40.a3.refs_4_), channel_id=1, source_target_pairs={{0,3},{1,8},{2,11},{3,0},{4,13},{5,6},{6,5},{7,14},{8,1},{9,10},{1... | collective-permute-start | bytes 294920 | tf_op jit(solution)/shard_map/ppermute | solution.py:306
  27.4 1.3 %collective-permute-done.12 = f32[32,768]{1,0:T(8,128)S(1)} collective-permute-done((f32[32,768]{1,0:T(8,128)S(1)}, f32[32,768]{1,0:T(8,128)S(1)}, u32[]{:S(2)}, u32[]{:S(2)}) %collective-permute-start.12) | collective-permute-done | bytes 98336 | tf_op jit(solution)/shard_map/ppermute | solution.py:306
  28.7 0.1 collective-permute-start.13
  28.8 0.5 %collective-permute-start.7 = (f32[32,768]{1,0:T(8,128)S(1)}, f32[32,768]{1,0:T(8,128)S(1)}, u32[]{:S(2)}, u32[]{:S(2)}) collective-permute-start(f32[32,768]{1,0:T(8,128)S(1)} %add.40.a3.refs_4_), channel_id=1, source_target_pairs={{0,1},{1,0},{2,3},{3,2},{4,5},{5,4},{6,7},{7,6},{8,9},{9,8},{10,11... | collective-permute-start | bytes 294920 | tf_op jit(solution)/shard_map/ppermute | solution.py:303
  29.3 0.4 collective-permute-done.5.a2.refs_3_
  29.7 0.1 collective-permute-start.6
  29.8 0.3 collective-permute-done.13.b0.refs_2_
  30.1 0.2 collective-permute-done.7.a1.refs_1_
  30.2 0.8 %right_products.1.before = f32[32,256]{1,0:T(8,128)S(1)} custom-call(f32[32,768]{1,0:T(8,128)S(1)} %collective-permute-done.7.a1.refs_1_, f32[32,768]{1,0:T(8,128)S(1)} %collective-permute-done.13.b0.refs_2_, f32[32,768]{1,0:T(8,128)S(1)} %add.40.a3.refs_4_, f32[32,768]{1,0:T(8,128)S(1)} %add.45.b1.refs_5_, f32[32,768]{1,0:T(8,128)S(1)} %collective-permute-done.5.a2.refs_3_, ...), custom_call_target="tpu_custom_call" | custom-call | flops 226492416 | tf_op jit(solution)/shard_map/right_products/pallas_call | solution.py:270
  31.0 0.0 collective-permute-done.6.p_ref.refs_0_
  31.0 0.3 right_products_last.1
  31.3 1.8 %collective-permute-start.15 = (f32[32,256]{1,0:T(8,128)S(1)}, f32[32,256]{1,0:T(8,128)S(1)}, u32[]{:S(2)}, u32[]{:S(2)}) collective-permute-start(f32[32,256]{1,0:T(8,128)S(1)} %right_products_last.1), channel_id=1, source_target_pairs={{0,5},{1,4},{2,7},{3,6},{4,1},{5,0},{6,3},{7,2},{8,13},{9,12},{10,... | collective-permute-start | bytes 98312 | tf_op jit(solution)/shard_map/ppermute | solution.py:303
  33.1 0.2 collective-permute-start.14
  33.2 1.5 %factor_first_half.1.state_ref = f32[32,128]{1,0:T(8,128)S(1)} custom-call(f32[32,768]{1,0:T(8,128)S(1)} %collective-permute-done.6.p_ref.refs_0_, f32[32,768]{1,0:T(8,128)S(1)} %collective-permute-done.7.a1.refs_1_, f32[32,768]{1,0:T(8,128)S(1)} %collective-permute-done.13.b0.refs_2_, f32[32,768]{1,0:T(8,128)S(1)} %collective-permute-done.5.a2.refs_3_, ...), custom_call_target="tpu_custom_call" | custom-call | flops 226492416 | tf_op jit(solution)/shard_map/factor_first_half/pallas_call | solution.py:270
  34.8 0.0 collective-permute-done.15
  34.8 0.0 collective-permute-done.14
  34.8 1.4 %collective-permute-start.17 = (f32[32,256]{1,0:T(8,128)S(1)}, f32[32,256]{1,0:T(8,128)S(1)}, u32[]{:S(2)}, u32[]{:S(2)}) collective-permute-start(f32[32,256]{1,0:T(8,128)S(1)} %add.46), channel_id=1, source_target_pairs={{0,9},{1,8},{2,11},{3,10},{4,13},{5,12},{6,15},{7,14},{8,1},{9,0},... | collective-permute-start | bytes 98312 | tf_op jit(solution)/shard_map/ppermute | solution.py:303
  36.2 0.4 collective-permute-start.16
  36.6 1.6 %factor_second_half.1.inv_ref = f32[32,32]{1,0:T(8,128)S(1)} custom-call(f32[32,128]{1,0:T(8,128)S(1)} %factor_first_half.1.state_ref), custom_call_target="tpu_custom_call" | custom-call | flops 226492416 | tf_op jit(solution)/shard_map/factor_second_half/pallas_call | solution.py:270
  38.1 0.1 collective-permute-done.17
  38.2 0.0 collective-permute-done.16
  38.2 3.2 %collective-permute-start.18 = (f32[32,256]{1,0:T(8,128)S(1)}, f32[32,256]{1,0:T(8,128)S(1)}, u32[]{:S(2)}, u32[]{:S(2)}) collective-permute-start(f32[32,256]{1,0:T(8,128)S(1)} %add.47.t0_ref), channel_id=1, source_target_pairs={{0,16},{1,17},{2,18},{3,19},{4,20},{5,21},{6,22},{7,23},{8,24},{9,... | collective-permute-start | bytes 98312 | tf_op jit(solution)/shard_map/ppermute | solution.py:303
  41.4 1.2 %left_factor.1 = (f32[32,4608]{1,0:T(8,128)}, bf16[4608,128]{1,0:T(8,128)(2,1)S(1)}) custom-call(f32[32,32]{1,0:T(8,128)S(1)} %factor_second_half.1.inv_ref, f32[32,768]{1,0:T(8,128)S(1)} %collective-permute-done.6.p_ref.refs_0_, f32[32,768]{1,0:T(8,128)S(1)} %collective-permute-done.7.a1.refs_1_, f32[32,768]{1,0:T(8,128)S(1)} %collective-permute-done.13.b0.refs_2_, ...), custom_call_target="tpu_custom_call" | custom-call | flops 226492416 | tf_op jit(solution)/shard_map/left_factor/pallas_call | solution.py:270
  42.7 0.6 %collective-permute-done.18.t1_ref = f32[32,256]{1,0:T(8,128)S(1)} collective-permute-done((f32[32,256]{1,0:T(8,128)S(1)}, f32[32,256]{1,0:T(8,128)S(1)}, u32[]{:S(2)}, u32[]{:S(2)}) %collective-permute-start.18) | collective-permute-done | bytes 32800 | tf_op jit(solution)/shard_map/ppermute | solution.py:303
  43.3 2.5 %new_error.1 = (f32[4608,256]{1,0:T(8,128)}, f32[32,256]{1,0:T(8,128)}) custom-call(f32[32,256]{1,0:T(8,128)S(1)} %add.47.t0_ref, f32[32,256]{1,0:T(8,128)S(1)} %collective-permute-done.18.t1_ref, f32[32,32]{1,0:T(8,128)S(1)} %factor_second_half.1.inv_ref, bf16[4608,128]{1,0:T(8,128)(2,1)S(1)} %get-tuple-element.33.rows_ref, ...), custom_call_target="tpu_custom_call" | custom-call | flops 226492416 | tf_op jit(solution)/shard_map/new_error/pallas_call | solution.py:270
  (13 shorter events, 0.2 us)
Async XLA Ops:
  0.6 4.0 %copy-start = (f32[256,32]{0,1:T(8,128)S(1)}, f32[256,32]{0,1:T(8,128)}, u32[]{:S(2)}) copy-start(f32[256,32]{0,1:T(8,128)} %param.5) | copy-start | bytes 98308
  4.0 1.6 %collective-permute-start = (f32[2,32,768]{2,1,0:T(8,128)S(1)}, f32[2,32,768]{2,1,0:T(8,128)S(1)}, u32[]{:S(2)}, u32[]{:S(2)}) collective-permute-start(f32[2,32,768]{2,1,0:T(8,128)S(1)} %get-tuple-element.24), channel_id=1, source_target_pairs={{0,1},{1,0},{2,3},{3,2},{4,5},{5,4},{6,7},{7,6},{8,9},{9,8},{10,11... | collective-permute-start | bytes 589832 | tf_op jit(solution)/shard_map/ppermute | solution.py:303
  4.5 3.8 %collective-permute-start.8 = (f32[32,768]{1,0:T(8,128)S(1)}, f32[32,768]{1,0:T(8,128)S(1)}, u32[]{:S(2)}, u32[]{:S(2)}) collective-permute-start(f32[32,768]{1,0:T(8,128)S(1)} %get-tuple-element.28), channel_id=1, source_target_pairs={{0,1},{1,0},{2,3},{3,2},{4,5},{5,4},{6,7},{7,6},{8,9},{9,8},{10,11... | collective-permute-start | bytes 294920 | tf_op jit(solution)/shard_map/ppermute | solution.py:303
  5.6 5.0 %collective-permute-start.1 = (f32[32,768]{1,0:T(8,128)S(1)}, f32[32,768]{1,0:T(8,128)S(1)}, u32[]{:S(2)}, u32[]{:S(2)}) collective-permute-start(f32[32,768]{1,0:T(8,128)S(1)} %slice_bitcast_fusion), channel_id=1, source_target_pairs={{0,3},{1,8},{2,11},{3,0},{4,13},{5,6},{6,5},{7,14},{8,1},{9,10},{1... | collective-permute-start | bytes 294920 | tf_op jit(solution)/shard_map/ppermute | solution.py:306
  8.3 4.5 %collective-permute-start.9 = (f32[32,768]{1,0:T(8,128)S(1)}, f32[32,768]{1,0:T(8,128)S(1)}, u32[]{:S(2)}, u32[]{:S(2)}) collective-permute-start(f32[32,768]{1,0:T(8,128)S(1)} %add.41), channel_id=1, source_target_pairs={{0,3},{1,8},{2,11},{3,0},{4,13},{5,6},{6,5},{7,14},{8,1},{9,10},{1... | collective-permute-start | bytes 294920 | tf_op jit(solution)/shard_map/ppermute | solution.py:306
  10.6 4.5 %collective-permute-start.2 = (f32[32,768]{1,0:T(8,128)S(1)}, f32[32,768]{1,0:T(8,128)S(1)}, u32[]{:S(2)}, u32[]{:S(2)}) collective-permute-start(f32[32,768]{1,0:T(8,128)S(1)} %fusion), channel_id=1, source_target_pairs={{0,9},{1,4},{2,7},{3,10},{4,1},{5,12},{6,15},{7,2},{8,13},{9,0},{1... | collective-permute-start | bytes 294920 | tf_op jit(solution)/shard_map/ppermute | solution.py:306
  12.8 4.1 %collective-permute-start.10 = (f32[32,768]{1,0:T(8,128)S(1)}, f32[32,768]{1,0:T(8,128)S(1)}, u32[]{:S(2)}, u32[]{:S(2)}) collective-permute-start(f32[32,768]{1,0:T(8,128)S(1)} %add.42), channel_id=1, source_target_pairs={{0,9},{1,4},{2,7},{3,10},{4,1},{5,12},{6,15},{7,2},{8,13},{9,0},{1... | collective-permute-start | bytes 294920 | tf_op jit(solution)/shard_map/ppermute | solution.py:306
  15.1 4.1 %collective-permute-start.3 = (f32[32,768]{1,0:T(8,128)S(1)}, f32[32,768]{1,0:T(8,128)S(1)}, u32[]{:S(2)}, u32[]{:S(2)}) collective-permute-start(f32[32,768]{1,0:T(8,128)S(1)} %add.38), channel_id=1, source_target_pairs={{0,5},{1,16},{2,19},{3,6},{4,21},{5,0},{6,3},{7,22},{8,25},{9,12},... | collective-permute-start | bytes 294920 | tf_op jit(solution)/shard_map/ppermute | solution.py:306
  16.9 5.1 %collective-permute-start.11 = (f32[32,768]{1,0:T(8,128)S(1)}, f32[32,768]{1,0:T(8,128)S(1)}, u32[]{:S(2)}, u32[]{:S(2)}) collective-permute-start(f32[32,768]{1,0:T(8,128)S(1)} %add.43), channel_id=1, source_target_pairs={{0,5},{1,16},{2,19},{3,6},{4,21},{5,0},{6,3},{7,22},{8,25},{9,12},... | collective-permute-start | bytes 294920 | tf_op jit(solution)/shard_map/ppermute | solution.py:306
  19.2 6.1 %collective-permute-start.4 = (f32[32,768]{1,0:T(8,128)S(1)}, f32[32,768]{1,0:T(8,128)S(1)}, u32[]{:S(2)}, u32[]{:S(2)}) collective-permute-start(f32[32,768]{1,0:T(8,128)S(1)} %add.39), channel_id=1, source_target_pairs={{0,17},{1,2},{2,1},{3,18},{4,7},{5,20},{6,23},{7,4},{8,11},{9,24},... | collective-permute-start | bytes 294920 | tf_op jit(solution)/shard_map/ppermute | solution.py:306
  22.1 6.6 %collective-permute-start.12 = (f32[32,768]{1,0:T(8,128)S(1)}, f32[32,768]{1,0:T(8,128)S(1)}, u32[]{:S(2)}, u32[]{:S(2)}) collective-permute-start(f32[32,768]{1,0:T(8,128)S(1)} %add.44), channel_id=1, source_target_pairs={{0,17},{1,2},{2,1},{3,18},{4,7},{5,20},{6,23},{7,4},{8,11},{9,24},... | collective-permute-start | bytes 294920 | tf_op jit(solution)/shard_map/ppermute | solution.py:306
  25.3 4.3 %collective-permute-start.5 = (f32[32,768]{1,0:T(8,128)S(1)}, f32[32,768]{1,0:T(8,128)S(1)}, u32[]{:S(2)}, u32[]{:S(2)}) collective-permute-start(f32[32,768]{1,0:T(8,128)S(1)} %add.40.a3.refs_4_), channel_id=1, source_target_pairs={{0,3},{1,8},{2,11},{3,0},{4,13},{5,6},{6,5},{7,14},{8,1},{9,10},{1... | collective-permute-start | bytes 294920 | tf_op jit(solution)/shard_map/ppermute | solution.py:306
  28.7 1.4 %collective-permute-start.13 = (f32[32,768]{1,0:T(8,128)S(1)}, f32[32,768]{1,0:T(8,128)S(1)}, u32[]{:S(2)}, u32[]{:S(2)}) collective-permute-start(f32[32,768]{1,0:T(8,128)S(1)} %add.45.b1.refs_5_), channel_id=1, source_target_pairs={{0,1},{1,0},{2,3},{3,2},{4,5},{5,4},{6,7},{7,6},{8,9},{9,8},{10,11... | collective-permute-start | bytes 294920 | tf_op jit(solution)/shard_map/ppermute | solution.py:303
  28.8 1.4 %collective-permute-start.7 = (f32[32,768]{1,0:T(8,128)S(1)}, f32[32,768]{1,0:T(8,128)S(1)}, u32[]{:S(2)}, u32[]{:S(2)}) collective-permute-start(f32[32,768]{1,0:T(8,128)S(1)} %add.40.a3.refs_4_), channel_id=1, source_target_pairs={{0,1},{1,0},{2,3},{3,2},{4,5},{5,4},{6,7},{7,6},{8,9},{9,8},{10,11... | collective-permute-start | bytes 294920 | tf_op jit(solution)/shard_map/ppermute | solution.py:303
  29.7 1.3 %collective-permute-start.6 = (f32[32,768]{1,0:T(8,128)S(1)}, f32[32,768]{1,0:T(8,128)S(1)}, u32[]{:S(2)}, u32[]{:S(2)}) collective-permute-start(f32[32,768]{1,0:T(8,128)S(1)} %collective-permute-done.5.a2.refs_3_), channel_id=1, source_target_pairs={{0,1},{1,0},{2,3},{3,2},{4,5},{5,4},{6,7},{7,6},{8,9},{9,8},{10,11... | collective-permute-start | bytes 294920 | tf_op jit(solution)/shard_map/ppermute | solution.py:303
  31.3 3.5 %collective-permute-start.15 = (f32[32,256]{1,0:T(8,128)S(1)}, f32[32,256]{1,0:T(8,128)S(1)}, u32[]{:S(2)}, u32[]{:S(2)}) collective-permute-start(f32[32,256]{1,0:T(8,128)S(1)} %right_products_last.1), channel_id=1, source_target_pairs={{0,5},{1,4},{2,7},{3,6},{4,1},{5,0},{6,3},{7,2},{8,13},{9,12},{10,... | collective-permute-start | bytes 98312 | tf_op jit(solution)/shard_map/ppermute | solution.py:303
  33.1 1.7 %collective-permute-start.14 = (f32[32,256]{1,0:T(8,128)S(1)}, f32[32,256]{1,0:T(8,128)S(1)}, u32[]{:S(2)}, u32[]{:S(2)}) collective-permute-start(f32[32,256]{1,0:T(8,128)S(1)} %right_products_last.1), channel_id=1, source_target_pairs={{0,1},{1,0},{2,3},{3,2},{4,5},{5,4},{6,7},{7,6},{8,9},{9,8},{10,11... | collective-permute-start | bytes 98312 | tf_op jit(solution)/shard_map/ppermute | solution.py:303
  34.8 3.4 %collective-permute-start.17 = (f32[32,256]{1,0:T(8,128)S(1)}, f32[32,256]{1,0:T(8,128)S(1)}, u32[]{:S(2)}, u32[]{:S(2)}) collective-permute-start(f32[32,256]{1,0:T(8,128)S(1)} %add.46), channel_id=1, source_target_pairs={{0,9},{1,8},{2,11},{3,10},{4,13},{5,12},{6,15},{7,14},{8,1},{9,0},... | collective-permute-start | bytes 98312 | tf_op jit(solution)/shard_map/ppermute | solution.py:303
  36.2 2.0 %collective-permute-start.16 = (f32[32,256]{1,0:T(8,128)S(1)}, f32[32,256]{1,0:T(8,128)S(1)}, u32[]{:S(2)}, u32[]{:S(2)}) collective-permute-start(f32[32,256]{1,0:T(8,128)S(1)} %add.46), channel_id=1, source_target_pairs={{0,1},{1,0},{2,3},{3,2},{4,5},{5,4},{6,7},{7,6},{8,9},{9,8},{10,11... | collective-permute-start | bytes 98312 | tf_op jit(solution)/shard_map/ppermute | solution.py:303
  38.2 5.1 %collective-permute-start.18 = (f32[32,256]{1,0:T(8,128)S(1)}, f32[32,256]{1,0:T(8,128)S(1)}, u32[]{:S(2)}, u32[]{:S(2)}) collective-permute-start(f32[32,256]{1,0:T(8,128)S(1)} %add.47.t0_ref), channel_id=1, source_target_pairs={{0,16},{1,17},{2,18},{3,19},{4,20},{5,21},{6,22},{7,23},{8,24},{9,... | collective-permute-start | bytes 98312 | tf_op jit(solution)/shard_map/ppermute | solution.py:303

commit v10 on v9

--- a/solution.py
+++ b/solution.py
@@ -363,7 +363,7 @@
         parts = (swap(t, 1), swap(t, 1 ^ bit)) if n < turns else (t, swap(t, bit))
 
     half = depth // 2
-    cuts = [half * n // 18 // 16 * 16 for n in (0, 1, 3, 6, 10, 14, 18)]
+    cuts = [half * n // 18 // 16 * 16 for n in (0, 1, 5, 10, 18)]
     error, q_new = call(
         functools.partial(error_kernel, replicas=replicas, cuts=cuts, devices=devices),
         "new_error",

time: 46 us -> 46 us (level)
  no operation moved by 1% of the time
where the time goes in v10:
time: 46 us; the launch traced here: 45.8 us
  starting transfers between devices  23.7 us (52%)
  Pallas kernels  12 us (26%)
  waiting for transfers between devices  9.14 us (20%)
  between operations  0.78 us (2%)
    ppermute x9, starting transfers between devices, cross(): lax.ppermute(x, AXES, [(i, i ^ 1 ^ bits[role(i)]) for i in range(devices)])  15.5 us
    pallas_call x8, Pallas kernels, call(): made(*(pltpu.with_memory_space_constraint(x, space) for x, space in zip(a...  12 us
    ppermute x10, starting transfers between devices, swap(): return lax.ppermute(x, AXES, [(i, i ^ bit) for i in range(devices)])  8.23 us
    ppermute x9, waiting for transfers between devices, cross(): lax.ppermute(x, AXES, [(i, i ^ 1 ^ bits[role(i)]) for i in range(devices)])  7.85 us
    ppermute x10, waiting for transfers between devices, swap(): return lax.ppermute(x, AXES, [(i, i ^ bit) for i in range(devices)])  1.29 us
  transfers between devices with their start and end apart: 19, of which 12 were waited for; matrix products, arithmetic and copies ran while one was open for 0% of the time, Pallas kernels for 13%

profile of v10, /device:TPU:0, one launch (start us, length us, event | category | flops | bytes accessed | tf_op | source)
XLA Modules:
  0.0 45.8 jit_solution(9865338333095219261)
XLA Ops:
  0.6 0.0 copy-start
  0.6 3.3 %left_products.1 = (f32[2304,256]{1,0:T(8,128)S(1)}, bf16[2304,256]{1,0:T(8,128)(2,1)S(1)}, bf16[2304,256]{1,0:T(8,128)(2,1)S(1)}, f32[2304,256]{1,0:T(8,128)S(1...) custom-call(f32[32,256]{1,0:T(8,128)} %bitcast.12, ...), custom_call_target="tpu_custom_call" | custom-call | flops 226492416 | tf_op jit(solution)/shard_map/left_products/pallas_call | solution.py:270
  4.0 0.5 %collective-permute-start = (f32[2,32,768]{2,1,0:T(8,128)S(1)}, f32[2,32,768]{2,1,0:T(8,128)S(1)}, u32[]{:S(2)}, u32[]{:S(2)}) collective-permute-start(f32[2,32,768]{2,1,0:T(8,128)S(1)} %get-tuple-element.24), channel_id=1, source_target_pairs={{0,1},{1,0},{2,3},{3,2},{4,5},{5,4},{6,7},{7,6},{8,9},{9,8},{10,11... | collective-permute-start | bytes 589832 | tf_op jit(solution)/shard_map/ppermute | solution.py:303
  4.5 0.1 collective-permute-start.8
  4.6 0.0 copy-done
  4.6 0.9 %left_products_rest.1 = (f32[2304,256]{1,0:T(8,128)S(1)}, bf16[2304,256]{1,0:T(8,128)(2,1)S(1)}, bf16[2304,256]{1,0:T(8,128)(2,1)S(1)}, f32[2,32,768]{2,1,0:T(8,128)S(1)}, f32[32,768]{1,0:T(8,128)S(1)}) custom-call(f32[32,256]{1,0:T(8,128)S(1)} %bitcast.13, f32[2304,256]{1,0:T(8,128)S(1)} %get-tuple-element.21.e_ref, ...), custom_call_target="tpu_custom_call" | custom-call | flops 226492416 | tf_op jit(solution)/shard_map/left_products_rest/pallas_call | solution.py:270
  5.5 0.1 collective-permute-done
  5.6 2.7 %collective-permute-start.1 = (f32[32,768]{1,0:T(8,128)S(1)}, f32[32,768]{1,0:T(8,128)S(1)}, u32[]{:S(2)}, u32[]{:S(2)}) collective-permute-start(f32[32,768]{1,0:T(8,128)S(1)} %slice_bitcast_fusion), channel_id=1, source_target_pairs={{0,3},{1,8},{2,11},{3,0},{4,13},{5,6},{6,5},{7,14},{8,1},{9,10},{1... | collective-permute-start | bytes 294920 | tf_op jit(solution)/shard_map/ppermute | solution.py:306
  8.3 0.0 collective-permute-done.8
  8.3 0.2 collective-permute-start.9
  8.5 2.1 %collective-permute-done.1 = f32[32,768]{1,0:T(8,128)S(1)} collective-permute-done((f32[32,768]{1,0:T(8,128)S(1)}, f32[32,768]{1,0:T(8,128)S(1)}, u32[]{:S(2)}, u32[]{:S(2)}) %collective-permute-start.1) | collective-permute-done | bytes 98336 | tf_op jit(solution)/shard_map/ppermute | solution.py:306
  10.6 2.2 %collective-permute-start.2 = (f32[32,768]{1,0:T(8,128)S(1)}, f32[32,768]{1,0:T(8,128)S(1)}, u32[]{:S(2)}, u32[]{:S(2)}) collective-permute-start(f32[32,768]{1,0:T(8,128)S(1)} %fusion), channel_id=1, source_target_pairs={{0,9},{1,4},{2,7},{3,10},{4,1},{5,12},{6,15},{7,2},{8,13},{9,0},{1... | collective-permute-start | bytes 294920 | tf_op jit(solution)/shard_map/ppermute | solution.py:306
  12.8 0.0 collective-permute-done.9
  12.8 1.2 %collective-permute-start.10 = (f32[32,768]{1,0:T(8,128)S(1)}, f32[32,768]{1,0:T(8,128)S(1)}, u32[]{:S(2)}, u32[]{:S(2)}) collective-permute-start(f32[32,768]{1,0:T(8,128)S(1)} %add.42), channel_id=1, source_target_pairs={{0,9},{1,4},{2,7},{3,10},{4,1},{5,12},{6,15},{7,2},{8,13},{9,0},{1... | collective-permute-start | bytes 294920 | tf_op jit(solution)/shard_map/ppermute | solution.py:306
  14.0 1.0 %collective-permute-done.2 = f32[32,768]{1,0:T(8,128)S(1)} collective-permute-done((f32[32,768]{1,0:T(8,128)S(1)}, f32[32,768]{1,0:T(8,128)S(1)}, u32[]{:S(2)}, u32[]{:S(2)}) %collective-permute-start.2) | collective-permute-done | bytes 98336 | tf_op jit(solution)/shard_map/ppermute | solution.py:306
  15.1 1.5 %collective-permute-start.3 = (f32[32,768]{1,0:T(8,128)S(1)}, f32[32,768]{1,0:T(8,128)S(1)}, u32[]{:S(2)}, u32[]{:S(2)}) collective-permute-start(f32[32,768]{1,0:T(8,128)S(1)} %add.38), channel_id=1, source_target_pairs={{0,5},{1,16},{2,19},{3,6},{4,21},{5,0},{6,3},{7,22},{8,25},{9,12},... | collective-permute-start | bytes 294920 | tf_op jit(solution)/shard_map/ppermute | solution.py:306
  16.6 0.4 collective-permute-done.10
  16.9 1.3 %collective-permute-start.11 = (f32[32,768]{1,0:T(8,128)S(1)}, f32[32,768]{1,0:T(8,128)S(1)}, u32[]{:S(2)}, u32[]{:S(2)}) collective-permute-start(f32[32,768]{1,0:T(8,128)S(1)} %add.43), channel_id=1, source_target_pairs={{0,5},{1,16},{2,19},{3,6},{4,21},{5,0},{6,3},{7,22},{8,25},{9,12},... | collective-permute-start | bytes 294920 | tf_op jit(solution)/shard_map/ppermute | solution.py:306
  18.2 1.0 %collective-permute-done.3 = f32[32,768]{1,0:T(8,128)S(1)} collective-permute-done((f32[32,768]{1,0:T(8,128)S(1)}, f32[32,768]{1,0:T(8,128)S(1)}, u32[]{:S(2)}, u32[]{:S(2)}) %collective-permute-start.3) | collective-permute-done | bytes 98336 | tf_op jit(solution)/shard_map/ppermute | solution.py:306
  19.2 2.8 %collective-permute-start.4 = (f32[32,768]{1,0:T(8,128)S(1)}, f32[32,768]{1,0:T(8,128)S(1)}, u32[]{:S(2)}, u32[]{:S(2)}) collective-permute-start(f32[32,768]{1,0:T(8,128)S(1)} %add.39), channel_id=1, source_target_pairs={{0,17},{1,2},{2,1},{3,18},{4,7},{5,20},{6,23},{7,4},{8,11},{9,24},... | collective-permute-start | bytes 294920 | tf_op jit(solution)/shard_map/ppermute | solution.py:306
  22.0 0.0 collective-permute-done.11
  22.1 1.6 %collective-permute-start.12 = (f32[32,768]{1,0:T(8,128)S(1)}, f32[32,768]{1,0:T(8,128)S(1)}, u32[]{:S(2)}, u32[]{:S(2)}) collective-permute-start(f32[32,768]{1,0:T(8,128)S(1)} %add.44), channel_id=1, source_target_pairs={{0,17},{1,2},{2,1},{3,18},{4,7},{5,20},{6,23},{7,4},{8,11},{9,24},... | collective-permute-start | bytes 294920 | tf_op jit(solution)/shard_map/ppermute | solution.py:306
  23.7 1.6 %collective-permute-done.4 = f32[32,768]{1,0:T(8,128)S(1)} collective-permute-done((f32[32,768]{1,0:T(8,128)S(1)}, f32[32,768]{1,0:T(8,128)S(1)}, u32[]{:S(2)}, u32[]{:S(2)}) %collective-permute-start.4) | collective-permute-done | bytes 98336 | tf_op jit(solution)/shard_map/ppermute | solution.py:306
  25.3 2.0 %collective-permute-start.5 = (f32[32,768]{1,0:T(8,128)S(1)}, f32[32,768]{1,0:T(8,128)S(1)}, u32[]{:S(2)}, u32[]{:S(2)}) collective-permute-start(f32[32,768]{1,0:T(8,128)S(1)} %add.40.a3.refs_4_), channel_id=1, source_target_pairs={{0,3},{1,8},{2,11},{3,0},{4,13},{5,6},{6,5},{7,14},{8,1},{9,10},{1... | collective-permute-start | bytes 294920 | tf_op jit(solution)/shard_map/ppermute | solution.py:306
  27.4 1.3 %collective-permute-done.12 = f32[32,768]{1,0:T(8,128)S(1)} collective-permute-done((f32[32,768]{1,0:T(8,128)S(1)}, f32[32,768]{1,0:T(8,128)S(1)}, u32[]{:S(2)}, u32[]{:S(2)}) %collective-permute-start.12) | collective-permute-done | bytes 98336 | tf_op jit(solution)/shard_map/ppermute | solution.py:306
  28.7 0.1 collective-permute-start.13
  28.8 0.5 %collective-permute-start.7 = (f32[32,768]{1,0:T(8,128)S(1)}, f32[32,768]{1,0:T(8,128)S(1)}, u32[]{:S(2)}, u32[]{:S(2)}) collective-permute-start(f32[32,768]{1,0:T(8,128)S(1)} %add.40.a3.refs_4_), channel_id=1, source_target_pairs={{0,1},{1,0},{2,3},{3,2},{4,5},{5,4},{6,7},{7,6},{8,9},{9,8},{10,11... | collective-permute-start | bytes 294920 | tf_op jit(solution)/shard_map/ppermute | solution.py:303
  29.3 0.4 collective-permute-done.5.a2.refs_3_
  29.7 0.1 collective-permute-start.6
  29.8 0.3 collective-permute-done.13.b0.refs_2_
  30.1 0.2 collective-permute-done.7.a1.refs_1_
  30.2 0.8 %right_products.1.before = f32[32,256]{1,0:T(8,128)S(1)} custom-call(f32[32,768]{1,0:T(8,128)S(1)} %collective-permute-done.7.a1.refs_1_, f32[32,768]{1,0:T(8,128)S(1)} %collective-permute-done.13.b0.refs_2_, f32[32,768]{1,0:T(8,128)S(1)} %add.40.a3.refs_4_, f32[32,768]{1,0:T(8,128)S(1)} %add.45.b1.refs_5_, f32[32,768]{1,0:T(8,128)S(1)} %collective-permute-done.5.a2.refs_3_, ...), custom_call_target="tpu_custom_call" | custom-call | flops 226492416 | tf_op jit(solution)/shard_map/right_products/pallas_call | solution.py:270
  31.0 0.0 collective-permute-done.6.p_ref.refs_0_
  31.0 0.3 right_products_last.1
  31.3 1.8 %collective-permute-start.15 = (f32[32,256]{1,0:T(8,128)S(1)}, f32[32,256]{1,0:T(8,128)S(1)}, u32[]{:S(2)}, u32[]{:S(2)}) collective-permute-start(f32[32,256]{1,0:T(8,128)S(1)} %right_products_last.1), channel_id=1, source_target_pairs={{0,5},{1,4},{2,7},{3,6},{4,1},{5,0},{6,3},{7,2},{8,13},{9,12},{10,... | collective-permute-start | bytes 98312 | tf_op jit(solution)/shard_map/ppermute | solution.py:303
  33.1 0.2 collective-permute-start.14
  33.2 1.5 %factor_first_half.1.state_ref = f32[32,128]{1,0:T(8,128)S(1)} custom-call(f32[32,768]{1,0:T(8,128)S(1)} %collective-permute-done.6.p_ref.refs_0_, f32[32,768]{1,0:T(8,128)S(1)} %collective-permute-done.7.a1.refs_1_, f32[32,768]{1,0:T(8,128)S(1)} %collective-permute-done.13.b0.refs_2_, f32[32,768]{1,0:T(8,128)S(1)} %collective-permute-done.5.a2.refs_3_, ...), custom_call_target="tpu_custom_call" | custom-call | flops 226492416 | tf_op jit(solution)/shard_map/factor_first_half/pallas_call | solution.py:270
  34.8 0.0 collective-permute-done.15
  34.8 0.0 collective-permute-done.14
  34.8 1.4 %collective-permute-start.17 = (f32[32,256]{1,0:T(8,128)S(1)}, f32[32,256]{1,0:T(8,128)S(1)}, u32[]{:S(2)}, u32[]{:S(2)}) collective-permute-start(f32[32,256]{1,0:T(8,128)S(1)} %add.46), channel_id=1, source_target_pairs={{0,9},{1,8},{2,11},{3,10},{4,13},{5,12},{6,15},{7,14},{8,1},{9,0},... | collective-permute-start | bytes 98312 | tf_op jit(solution)/shard_map/ppermute | solution.py:303
  36.2 0.4 collective-permute-start.16
  36.6 1.6 %factor_second_half.1.inv_ref = f32[32,32]{1,0:T(8,128)S(1)} custom-call(f32[32,128]{1,0:T(8,128)S(1)} %factor_first_half.1.state_ref), custom_call_target="tpu_custom_call" | custom-call | flops 226492416 | tf_op jit(solution)/shard_map/factor_second_half/pallas_call | solution.py:270
  38.1 0.1 collective-permute-done.17
  38.2 0.0 collective-permute-done.16
  38.2 3.2 %collective-permute-start.18 = (f32[32,256]{1,0:T(8,128)S(1)}, f32[32,256]{1,0:T(8,128)S(1)}, u32[]{:S(2)}, u32[]{:S(2)}) collective-permute-start(f32[32,256]{1,0:T(8,128)S(1)} %add.47.t0_ref), channel_id=1, source_target_pairs={{0,16},{1,17},{2,18},{3,19},{4,20},{5,21},{6,22},{7,23},{8,24},{9,... | collective-permute-start | bytes 98312 | tf_op jit(solution)/shard_map/ppermute | solution.py:303
  41.4 1.2 %left_factor.1 = (f32[32,4608]{1,0:T(8,128)}, bf16[4608,128]{1,0:T(8,128)(2,1)S(1)}) custom-call(f32[32,32]{1,0:T(8,128)S(1)} %factor_second_half.1.inv_ref, f32[32,768]{1,0:T(8,128)S(1)} %collective-permute-done.6.p_ref.refs_0_, f32[32,768]{1,0:T(8,128)S(1)} %collective-permute-done.7.a1.refs_1_, f32[32,768]{1,0:T(8,128)S(1)} %collective-permute-done.13.b0.refs_2_, ...), custom_call_target="tpu_custom_call" | custom-call | flops 226492416 | tf_op jit(solution)/shard_map/left_factor/pallas_call | solution.py:270
  42.7 0.6 %collective-permute-done.18.t1_ref = f32[32,256]{1,0:T(8,128)S(1)} collective-permute-done((f32[32,256]{1,0:T(8,128)S(1)}, f32[32,256]{1,0:T(8,128)S(1)}, u32[]{:S(2)}, u32[]{:S(2)}) %collective-permute-start.18) | collective-permute-done | bytes 32800 | tf_op jit(solution)/shard_map/ppermute | solution.py:303
  43.3 2.5 %new_error.1 = (f32[4608,256]{1,0:T(8,128)}, f32[32,256]{1,0:T(8,128)}) custom-call(f32[32,256]{1,0:T(8,128)S(1)} %add.47.t0_ref, f32[32,256]{1,0:T(8,128)S(1)} %collective-permute-done.18.t1_ref, f32[32,32]{1,0:T(8,128)S(1)} %factor_second_half.1.inv_ref, bf16[4608,128]{1,0:T(8,128)(2,1)S(1)} %get-tuple-element.33.rows_ref, ...), custom_call_target="tpu_custom_call" | custom-call | flops 226492416 | tf_op jit(solution)/shard_map/new_error/pallas_call | solution.py:270
  (13 shorter events, 0.2 us)
Async XLA Ops:
  0.6 4.0 %copy-start = (f32[256,32]{0,1:T(8,128)S(1)}, f32[256,32]{0,1:T(8,128)}, u32[]{:S(2)}) copy-start(f32[256,32]{0,1:T(8,128)} %param.5) | copy-start | bytes 98308
  4.0 1.6 %collective-permute-start = (f32[2,32,768]{2,1,0:T(8,128)S(1)}, f32[2,32,768]{2,1,0:T(8,128)S(1)}, u32[]{:S(2)}, u32[]{:S(2)}) collective-permute-start(f32[2,32,768]{2,1,0:T(8,128)S(1)} %get-tuple-element.24), channel_id=1, source_target_pairs={{0,1},{1,0},{2,3},{3,2},{4,5},{5,4},{6,7},{7,6},{8,9},{9,8},{10,11... | collective-permute-start | bytes 589832 | tf_op jit(solution)/shard_map/ppermute | solution.py:303
  4.5 3.8 %collective-permute-start.8 = (f32[32,768]{1,0:T(8,128)S(1)}, f32[32,768]{1,0:T(8,128)S(1)}, u32[]{:S(2)}, u32[]{:S(2)}) collective-permute-start(f32[32,768]{1,0:T(8,128)S(1)} %get-tuple-element.28), channel_id=1, source_target_pairs={{0,1},{1,0},{2,3},{3,2},{4,5},{5,4},{6,7},{7,6},{8,9},{9,8},{10,11... | collective-permute-start | bytes 294920 | tf_op jit(solution)/shard_map/ppermute | solution.py:303
  5.6 5.0 %collective-permute-start.1 = (f32[32,768]{1,0:T(8,128)S(1)}, f32[32,768]{1,0:T(8,128)S(1)}, u32[]{:S(2)}, u32[]{:S(2)}) collective-permute-start(f32[32,768]{1,0:T(8,128)S(1)} %slice_bitcast_fusion), channel_id=1, source_target_pairs={{0,3},{1,8},{2,11},{3,0},{4,13},{5,6},{6,5},{7,14},{8,1},{9,10},{1... | collective-permute-start | bytes 294920 | tf_op jit(solution)/shard_map/ppermute | solution.py:306
  8.3 4.5 %collective-permute-start.9 = (f32[32,768]{1,0:T(8,128)S(1)}, f32[32,768]{1,0:T(8,128)S(1)}, u32[]{:S(2)}, u32[]{:S(2)}) collective-permute-start(f32[32,768]{1,0:T(8,128)S(1)} %add.41), channel_id=1, source_target_pairs={{0,3},{1,8},{2,11},{3,0},{4,13},{5,6},{6,5},{7,14},{8,1},{9,10},{1... | collective-permute-start | bytes 294920 | tf_op jit(solution)/shard_map/ppermute | solution.py:306
  10.6 4.5 %collective-permute-start.2 = (f32[32,768]{1,0:T(8,128)S(1)}, f32[32,768]{1,0:T(8,128)S(1)}, u32[]{:S(2)}, u32[]{:S(2)}) collective-permute-start(f32[32,768]{1,0:T(8,128)S(1)} %fusion), channel_id=1, source_target_pairs={{0,9},{1,4},{2,7},{3,10},{4,1},{5,12},{6,15},{7,2},{8,13},{9,0},{1... | collective-permute-start | bytes 294920 | tf_op jit(solution)/shard_map/ppermute | solution.py:306
  12.8 4.1 %collective-permute-start.10 = (f32[32,768]{1,0:T(8,128)S(1)}, f32[32,768]{1,0:T(8,128)S(1)}, u32[]{:S(2)}, u32[]{:S(2)}) collective-permute-start(f32[32,768]{1,0:T(8,128)S(1)} %add.42), channel_id=1, source_target_pairs={{0,9},{1,4},{2,7},{3,10},{4,1},{5,12},{6,15},{7,2},{8,13},{9,0},{1... | collective-permute-start | bytes 294920 | tf_op jit(solution)/shard_map/ppermute | solution.py:306
  15.1 4.1 %collective-permute-start.3 = (f32[32,768]{1,0:T(8,128)S(1)}, f32[32,768]{1,0:T(8,128)S(1)}, u32[]{:S(2)}, u32[]{:S(2)}) collective-permute-start(f32[32,768]{1,0:T(8,128)S(1)} %add.38), channel_id=1, source_target_pairs={{0,5},{1,16},{2,19},{3,6},{4,21},{5,0},{6,3},{7,22},{8,25},{9,12},... | collective-permute-start | bytes 294920 | tf_op jit(solution)/shard_map/ppermute | solution.py:306
  16.9 5.1 %collective-permute-start.11 = (f32[32,768]{1,0:T(8,128)S(1)}, f32[32,768]{1,0:T(8,128)S(1)}, u32[]{:S(2)}, u32[]{:S(2)}) collective-permute-start(f32[32,768]{1,0:T(8,128)S(1)} %add.43), channel_id=1, source_target_pairs={{0,5},{1,16},{2,19},{3,6},{4,21},{5,0},{6,3},{7,22},{8,25},{9,12},... | collective-permute-start | bytes 294920 | tf_op jit(solution)/shard_map/ppermute | solution.py:306
  19.2 6.1 %collective-permute-start.4 = (f32[32,768]{1,0:T(8,128)S(1)}, f32[32,768]{1,0:T(8,128)S(1)}, u32[]{:S(2)}, u32[]{:S(2)}) collective-permute-start(f32[32,768]{1,0:T(8,128)S(1)} %add.39), channel_id=1, source_target_pairs={{0,17},{1,2},{2,1},{3,18},{4,7},{5,20},{6,23},{7,4},{8,11},{9,24},... | collective-permute-start | bytes 294920 | tf_op jit(solution)/shard_map/ppermute | solution.py:306
  22.1 6.6 %collective-permute-start.12 = (f32[32,768]{1,0:T(8,128)S(1)}, f32[32,768]{1,0:T(8,128)S(1)}, u32[]{:S(2)}, u32[]{:S(2)}) collective-permute-start(f32[32,768]{1,0:T(8,128)S(1)} %add.44), channel_id=1, source_target_pairs={{0,17},{1,2},{2,1},{3,18},{4,7},{5,20},{6,23},{7,4},{8,11},{9,24},... | collective-permute-start | bytes 294920 | tf_op jit(solution)/shard_map/ppermute | solution.py:306
  25.3 4.3 %collective-permute-start.5 = (f32[32,768]{1,0:T(8,128)S(1)}, f32[32,768]{1,0:T(8,128)S(1)}, u32[]{:S(2)}, u32[]{:S(2)}) collective-permute-start(f32[32,768]{1,0:T(8,128)S(1)} %add.40.a3.refs_4_), channel_id=1, source_target_pairs={{0,3},{1,8},{2,11},{3,0},{4,13},{5,6},{6,5},{7,14},{8,1},{9,10},{1... | collective-permute-start | bytes 294920 | tf_op jit(solution)/shard_map/ppermute | solution.py:306
  28.7 1.4 %collective-permute-start.13 = (f32[32,768]{1,0:T(8,128)S(1)}, f32[32,768]{1,0:T(8,128)S(1)}, u32[]{:S(2)}, u32[]{:S(2)}) collective-permute-start(f32[32,768]{1,0:T(8,128)S(1)} %add.45.b1.refs_5_), channel_id=1, source_target_pairs={{0,1},{1,0},{2,3},{3,2},{4,5},{5,4},{6,7},{7,6},{8,9},{9,8},{10,11... | collective-permute-start | bytes 294920 | tf_op jit(solution)/shard_map/ppermute | solution.py:303
  28.8 1.4 %collective-permute-start.7 = (f32[32,768]{1,0:T(8,128)S(1)}, f32[32,768]{1,0:T(8,128)S(1)}, u32[]{:S(2)}, u32[]{:S(2)}) collective-permute-start(f32[32,768]{1,0:T(8,128)S(1)} %add.40.a3.refs_4_), channel_id=1, source_target_pairs={{0,1},{1,0},{2,3},{3,2},{4,5},{5,4},{6,7},{7,6},{8,9},{9,8},{10,11... | collective-permute-start | bytes 294920 | tf_op jit(solution)/shard_map/ppermute | solution.py:303
  29.7 1.3 %collective-permute-start.6 = (f32[32,768]{1,0:T(8,128)S(1)}, f32[32,768]{1,0:T(8,128)S(1)}, u32[]{:S(2)}, u32[]{:S(2)}) collective-permute-start(f32[32,768]{1,0:T(8,128)S(1)} %collective-permute-done.5.a2.refs_3_), channel_id=1, source_target_pairs={{0,1},{1,0},{2,3},{3,2},{4,5},{5,4},{6,7},{7,6},{8,9},{9,8},{10,11... | collective-permute-start | bytes 294920 | tf_op jit(solution)/shard_map/ppermute | solution.py:303
  31.3 3.5 %collective-permute-start.15 = (f32[32,256]{1,0:T(8,128)S(1)}, f32[32,256]{1,0:T(8,128)S(1)}, u32[]{:S(2)}, u32[]{:S(2)}) collective-permute-start(f32[32,256]{1,0:T(8,128)S(1)} %right_products_last.1), channel_id=1, source_target_pairs={{0,5},{1,4},{2,7},{3,6},{4,1},{5,0},{6,3},{7,2},{8,13},{9,12},{10,... | collective-permute-start | bytes 98312 | tf_op jit(solution)/shard_map/ppermute | solution.py:303
  33.1 1.7 %collective-permute-start.14 = (f32[32,256]{1,0:T(8,128)S(1)}, f32[32,256]{1,0:T(8,128)S(1)}, u32[]{:S(2)}, u32[]{:S(2)}) collective-permute-start(f32[32,256]{1,0:T(8,128)S(1)} %right_products_last.1), channel_id=1, source_target_pairs={{0,1},{1,0},{2,3},{3,2},{4,5},{5,4},{6,7},{7,6},{8,9},{9,8},{10,11... | collective-permute-start | bytes 98312 | tf_op jit(solution)/shard_map/ppermute | solution.py:303
  34.8 3.4 %collective-permute-start.17 = (f32[32,256]{1,0:T(8,128)S(1)}, f32[32,256]{1,0:T(8,128)S(1)}, u32[]{:S(2)}, u32[]{:S(2)}) collective-permute-start(f32[32,256]{1,0:T(8,128)S(1)} %add.46), channel_id=1, source_target_pairs={{0,9},{1,8},{2,11},{3,10},{4,13},{5,12},{6,15},{7,14},{8,1},{9,0},... | collective-permute-start | bytes 98312 | tf_op jit(solution)/shard_map/ppermute | solution.py:303
  36.2 2.0 %collective-permute-start.16 = (f32[32,256]{1,0:T(8,128)S(1)}, f32[32,256]{1,0:T(8,128)S(1)}, u32[]{:S(2)}, u32[]{:S(2)}) collective-permute-start(f32[32,256]{1,0:T(8,128)S(1)} %add.46), channel_id=1, source_target_pairs={{0,1},{1,0},{2,3},{3,2},{4,5},{5,4},{6,7},{7,6},{8,9},{9,8},{10,11... | collective-permute-start | bytes 98312 | tf_op jit(solution)/shard_map/ppermute | solution.py:303
  38.2 5.1 %collective-permute-start.18 = (f32[32,256]{1,0:T(8,128)S(1)}, f32[32,256]{1,0:T(8,128)S(1)}, u32[]{:S(2)}, u32[]{:S(2)}) collective-permute-start(f32[32,256]{1,0:T(8,128)S(1)} %add.47.t0_ref), channel_id=1, source_target_pairs={{0,16},{1,17},{2,18},{3,19},{4,20},{5,21},{6,22},{7,23},{8,24},{9,... | collective-permute-start | bytes 98312 | tf_op jit(solution)/shard_map/ppermute | solution.py:303
